TPU v7x, 32 devices: a whole 2x2x4 slice. The times are simulated.
32 devices in a mesh: frame: 4 (over x, core), rows: 8 (over z, y).
Axes of the slice: x: 2, y: 2, z: 4, core: 2. Of those that a mesh axis runs over, the one named last changes fastest.
Arguments:
- video: bfloat16 [2, 4, 8, 480, 256], P(None, 'frame', 'rows'), may hold values from -6 to 6
- stereo_qk: bfloat16 [256, 512], replicated, may hold values from -8 to 8
- stereo_v: bfloat16 [256, 256], replicated, may hold values from -0.375 to 0.375
- stereo_out: bfloat16 [256, 256], replicated, may hold values from -0.375 to 0.375
- temporal_qk: bfloat16 [256, 512], replicated, may hold values from -8 to 8
- temporal_v: bfloat16 [256, 256], replicated, may hold values from -0.375 to 0.375
- temporal_out: bfloat16 [256, 256], replicated, may hold values from -0.375 to 0.375
- mlp_up: bfloat16 [256, 1024], replicated, may hold values from -0.375 to 0.375
- mix_kernel: bfloat16 [3, 3, 1024], replicated, may hold values from -2 to 2
- mlp_down: bfloat16 [1024, 256], replicated, may hold values from -0.1875 to 0.1875
Outputs:
- block_output: bfloat16 [2, 4, 8, 480, 256], P(None, 'frame', 'rows')
All inputs are finite; a program needn't handle non-finite values.
Results may differ from a plain program's by a relative error of at most 0.013.
Values may be sent and summed in bfloat16 or wider, within the bound.
No kernel may reach another device: no remote copies, remote signals or barrier semaphores. Data moves between devices by JAX's collectives and lax.ppermute only.
A program may use at most 64 MiB of HBM per device.

v0:
```python
import jax
import jax.numpy as jnp
from jax import lax
from jax.sharding import PartitionSpec as P

HEADS = 8
HEAD_DIM = 32


def with_halo(array, sides, width):
    for axis, dim in sides:
        size, length = (lax.axis_size(axis), array.shape[dim])
        up = [(i, (i + 1) % size) for i in range(size - 1)]
        down = [(j, i) for i, j in up]
        last = lax.slice_in_dim(array, length - width, length, axis=dim)
        leading = lax.slice_in_dim(array, 0, width, axis=dim)
        before = lax.ppermute(last, axis, up)
        after = lax.ppermute(leading, axis, down)
        array = jnp.concatenate([before, array, after], axis=dim)
    return array


def layer_norm(values_in):
    widened = values_in.astype(jnp.float32)
    centred = widened - jnp.mean(widened, axis=-1, keepdims=True)
    variance = jnp.mean(centred * centred, axis=-1, keepdims=True)
    return (centred * lax.rsqrt(variance + 1e-05)).astype(jnp.bfloat16)


def stereo_row(image_row, stereo_qk, stereo_v, stereo_out):
    view_count, width_cols, channels = image_row.shape
    normed = layer_norm(image_row).reshape(view_count * width_cols, channels)
    paired = (
        jnp.dot(normed, stereo_qk, preferred_element_type=jnp.float32)
        .astype(jnp.bfloat16)
        .reshape(view_count, width_cols, 2 * channels)
    )
    value_rows = (
        jnp.dot(normed, stereo_v, preferred_element_type=jnp.float32)
        .astype(jnp.bfloat16)
        .reshape(view_count, width_cols, HEADS, HEAD_DIM)
    )
    query_rows = paired[:, :, :channels].reshape(view_count, width_cols, HEADS, HEAD_DIM)
    keys_other = paired[::-1, :, channels:].reshape(view_count, width_cols, HEADS, HEAD_DIM)
    values_other = value_rows[::-1]
    score_scale = HEAD_DIM ** (-0.5)
    group_size = max(HEADS // 2, 1)
    results = []
    for offset in range(0, HEADS, group_size):
        scores = (
            jnp.einsum(
                "vqhd,vkhd->vhqk",
                query_rows[:, :, offset : offset + group_size],
                keys_other[:, :, offset : offset + group_size],
                preferred_element_type=jnp.float32,
            )
            * score_scale
        )
        weights = jax.nn.softmax(scores, axis=-1).astype(jnp.bfloat16)
        results.append(
            jnp.einsum(
                "vhqk,vkhd->vqhd",
                weights,
                values_other[:, :, offset : offset + group_size],
                preferred_element_type=jnp.float32,
            ).astype(jnp.bfloat16)
        )
    attended = jnp.concatenate(results, axis=2).reshape(view_count * width_cols, channels)
    update = jnp.dot(attended, stereo_out, preferred_element_type=jnp.float32)
    return (image_row.astype(jnp.float32) + update.reshape(image_row.shape)).astype(jnp.bfloat16)


def temporal_attend(query_rows, key_rows, value_rows):
    shaped = query_rows.shape[:-1] + (HEADS, HEAD_DIM)
    scores = jnp.einsum(
        "vfphd,vgphd->vhfgp",
        query_rows.reshape(shaped),
        key_rows.reshape(shaped),
        preferred_element_type=jnp.float32,
    ) * HEAD_DIM ** (-0.5)
    weights = jax.nn.softmax(scores, axis=3).astype(jnp.bfloat16)
    mixed_out = jnp.einsum(
        "vhfgp,vgphd->vfphd",
        weights,
        value_rows.reshape(shaped),
        preferred_element_type=jnp.float32,
    ).astype(jnp.bfloat16)
    return mixed_out.reshape(query_rows.shape)


def flatten_items(pieces):
    view_count, frame_count, single, item_count, channels = pieces.shape
    return pieces.reshape(view_count, frame_count, single * item_count, channels)


def project_pairs(normed, pair_weight, value_weight):
    channels = normed.shape[-1]
    flat_rows = normed.reshape(-1, channels)
    paired = (
        jnp.dot(flat_rows, pair_weight, preferred_element_type=jnp.float32)
        .astype(jnp.bfloat16)
        .reshape(normed.shape[:-1] + (2 * channels,))
    )
    value_rows = (
        jnp.dot(flat_rows, value_weight, preferred_element_type=jnp.float32)
        .astype(jnp.bfloat16)
        .reshape(normed.shape)
    )
    return (paired, value_rows)


def expand_hidden(normed, mlp_up):
    pieces_out = []
    for view_index in range(normed.shape[0]):
        flat_rows = normed[view_index].reshape(-1, normed.shape[-1])
        product = jnp.dot(flat_rows, mlp_up, preferred_element_type=jnp.float32)
        pieces_out.append(
            jax.nn.gelu(product)
            .astype(jnp.bfloat16)
            .reshape(normed.shape[1:-1] + (mlp_up.shape[1],))
        )
    return jnp.stack(pieces_out)


def depthwise(padded, mix_kernel):
    rows_out = padded.shape[-3] - 2
    cols_out = padded.shape[-2]
    widened = jnp.pad(padded, [(0, 0)] * (padded.ndim - 2) + [(1, 1), (0, 0)])
    running = jnp.zeros(padded.shape[:-3] + (rows_out, cols_out, padded.shape[-1]), jnp.float32)
    for tap_row in range(3):
        for tap_col in range(3):
            window = widened[..., tap_row : tap_row + rows_out, tap_col : tap_col + cols_out, :]
            running = running + window.astype(jnp.float32) * mix_kernel[tap_row, tap_col].astype(
                jnp.float32
            )
    return running.astype(jnp.bfloat16)


def shards(
    video,
    stereo_qk,
    stereo_v,
    stereo_out,
    temporal_qk,
    temporal_v,
    temporal_out,
    mlp_up,
    mix_kernel,
    mlp_down,
):
    view_count, frames_here, rows_here, width_cols, channels = video.shape
    owners = lax.axis_size("frame")
    stereo_lines = jnp.transpose(video, (1, 2, 0, 3, 4)).reshape(
        frames_here * rows_here, view_count, width_cols, channels
    )
    after_lines = lax.map(
        lambda image_row: stereo_row(image_row, stereo_qk, stereo_v, stereo_out), stereo_lines
    )
    first_section = jnp.transpose(
        after_lines.reshape(frames_here, rows_here, view_count, width_cols, channels),
        (2, 0, 1, 3, 4),
    )
    token_rows = first_section.reshape(view_count, frames_here, rows_here * width_cols, channels)
    per_owner = rows_here * width_cols // owners
    normed = layer_norm(token_rows).reshape(view_count, frames_here, owners, per_owner, channels)
    paired, value_rows = project_pairs(normed, temporal_qk, temporal_v)
    pieces = (
        lax.all_to_all(paired, "frame", split_axis=2, concat_axis=1, tiled=True),
        lax.all_to_all(value_rows, "frame", split_axis=2, concat_axis=1, tiled=True),
    )
    pair_flat = flatten_items(pieces[0])
    value_flat = flatten_items(pieces[1])
    result = temporal_attend(pair_flat[..., :channels], pair_flat[..., channels:], value_flat)
    attended = result.reshape(pieces[1].shape)
    returned = lax.all_to_all(attended, "frame", split_axis=1, concat_axis=2, tiled=True)
    update = jnp.dot(
        returned.reshape(-1, channels), temporal_out, preferred_element_type=jnp.float32
    )
    second_section = (token_rows.astype(jnp.float32) + update.reshape(token_rows.shape)).astype(
        jnp.bfloat16
    )
    second_section = second_section.reshape(
        view_count, frames_here, rows_here, width_cols, channels
    )
    normed_mlp = layer_norm(second_section)
    hidden = expand_hidden(normed_mlp, mlp_up)
    padded = with_halo(hidden, (("rows", 2),), 1)
    mixed_out = depthwise(padded, mix_kernel)
    down_proj = jnp.dot(
        mixed_out.reshape(-1, mixed_out.shape[-1]), mlp_down, preferred_element_type=jnp.float32
    )
    return (second_section.astype(jnp.float32) + down_proj.reshape(second_section.shape)).astype(
        jnp.bfloat16
    )


def solution(mesh):
    in_specs = (P(None, "frame", "rows", None, None), P(), P(), P(), P(), P(), P(), P(), P(), P())
    out_specs = P(None, "frame", "rows", None, None)
    return jax.shard_map(shards, mesh=mesh, in_specs=in_specs, out_specs=out_specs, check_vma=False)
```

profile of v0, /device:TPU:0, one launch (start us, length us, event | category | flops | bytes accessed | tf_op | source)
XLA Modules:
  0.0 221.5 jit_solution(17831121942972189379)
XLA Ops:
  0.0 1.3 convert_reduce_fusion.2
  1.3 1.4 fusion.61
  2.9 1.4 fusion.59
  4.2 1.4 convolution_convert_fusion.1
  6.2 4.3 %fusion.63 = f32[2,4,480,480]{2,3,1,0:T(8,128)} fusion(bf16[2,480,8,32]{1,3,2,0:T(8,128)(2,1)S(1)} %bitcast.111, bf16[2,480,8,32]{1,3,2,0:T(8,128)(2,1)S(1)} %bitcast.118), kind=kOutput, calls=%fused_computation.83 | convolution fusion | flops 117964800 | bytes 8159232 | tf_op jit(solution)/shard_map/while/body/eval_jaxpr/vqhd,vkhd->vhqk/dot_general | solution.py:51
  10.5 4.4 %fusion.65 = f32[2,4,480,480]{2,3,1,0:T(8,128)} fusion(bf16[2,480,8,32]{1,3,2,0:T(8,128)(2,1)S(1)} %bitcast.112, bf16[2,480,8,32]{1,3,2,0:T(8,128)(2,1)S(1)} %bitcast.119), kind=kOutput, calls=%fused_computation.85 | convolution fusion | flops 117964800 | bytes 8159232 | tf_op jit(solution)/shard_map/while/body/eval_jaxpr/vqhd,vkhd->vhqk/dot_general | solution.py:51
  16.2 1.6 slice.104
  17.8 1.4 slice.110
  19.2 7.4 %fusion.92 = f32[2,4,480]{2,1,0:T(4,128)S(1)} fusion(f32[2,4,480,480]{2,3,1,0:T(8,128)} %fusion.63), kind=kOutput, calls=%fused_computation.122 | output fusion | flops 7373279 | bytes 7388160 | tf_op jit(solution)/shard_map/while/body/eval_jaxpr/sub | solution.py:59
  26.7 7.4 %fusion.93 = f32[2,4,480]{2,1,0:T(4,128)S(1)} fusion(f32[2,4,480,480]{2,3,1,0:T(8,128)} %fusion.65), kind=kOutput, calls=%fused_computation.123 | output fusion | flops 7373279 | bytes 7388160 | tf_op jit(solution)/shard_map/while/body/eval_jaxpr/sub | solution.py:59
  34.1 8.0 %fusion.49 = bf16[2,480,4,32]{1,3,2,0:T(8,128)(2,1)S(1)} fusion(f32[2,4,480]{2,1,0:T(4,128)S(1)} %fusion.92, bf16[2,480,4,32]{1,0,3,2:T(2,128)(2,1)S(1)} %slice.110, f32[2,4,480,480]{2,3,1,0:T(8,128)} %fusion.63), kind=kOutput, calls=%fused_computation.65 | convolution fusion | flops 127308000 | bytes 7879680 | tf_op jit(solution)/shard_map/while/body/eval_jaxpr/vhqk,vkhd->vqhd/dot_general | solution.py:61
  42.1 8.1 %fusion.48 = bf16[2,480,4,32]{1,3,2,0:T(8,128)(2,1)S(1)} fusion(f32[2,4,480]{2,1,0:T(4,128)S(1)} %fusion.93, bf16[2,480,4,32]{1,0,3,2:T(2,128)(2,1)S(1)} %slice.104, f32[2,4,480,480]{2,3,1,0:T(8,128)} %fusion.65), kind=kOutput, calls=%fused_computation.64 | convolution fusion | flops 127308000 | bytes 7879680 | tf_op jit(solution)/shard_map/while/body/eval_jaxpr/vhqk,vkhd->vqhd/dot_general | solution.py:61
  52.6 4.2 %all-to-all-start = ((bf16[2,1,4,120,256]{4,3,1,0,2:T(8,128)(2,1)}), bf16[2,1,4,120,256]{4,3,1,0,2:T(8,128)(2,1)S(1)}, u32[]{:S(2)}, u32[]{:S(2)}) async-start(bf16[2,1,4,120,256]{4,3,1,0,2:T(8,128)(2,1)} %copy.69), calls=%async_computation | async-start | bytes 983040 | tf_op jit(solution)/shard_map/all_to_all | solution.py:169
  58.3 7.0 %all-to-all-done = bf16[2,1,4,120,256]{4,3,1,0,2:T(8,128)(2,1)S(1)} async-done(((bf16[2,1,4,120,256]{4,3,1,0,2:T(8,128)(2,1)}), bf16[2,1,4,120,256]{4,3,1,0,2:T(8,128)(2,1)S(1)}, u32[]{:S(2)}, u32[]{:S(2)}) %all-to-all-start) | async-done | bytes 491552 | tf_op jit(solution)/shard_map/all_to_all | solution.py:169
  65.3 4.4 %all-to-all-start.1 = ((bf16[2,1,4,120,512]{4,3,1,0,2:T(8,128)(2,1)}), bf16[2,1,4,120,512]{4,3,1,0,2:T(8,128)(2,1)}, u32[]{:S(2)}, u32[]{:S(2)}) async-start(bf16[2,1,4,120,512]{4,3,1,0,2:T(8,128)(2,1)} %copy.71), calls=%async_computation.1 | async-start | bytes 1966080 | tf_op jit(solution)/shard_map/all_to_all | solution.py:168
  70.0 2.8 %copy.76 = bf16[2,4,120,8,32]{4,1,3,2,0:T(4,128)(2,1)} copy(bf16[2,4,120,8,32]{2,4,3,1,0:T(8,128)(2,1)S(1)} %bitcast.120) | data formatting | bytes 983040 | tf_op jit(solution)/shard_map/reshape;reshape | solution.py:85
  72.8 10.5 %all-to-all-done.1 = bf16[2,1,4,120,512]{4,3,1,0,2:T(8,128)(2,1)} async-done(((bf16[2,1,4,120,512]{4,3,1,0,2:T(8,128)(2,1)}), bf16[2,1,4,120,512]{4,3,1,0,2:T(8,128)(2,1)}, u32[]{:S(2)}, u32[]{:S(2)}) %all-to-all-start.1) | async-done | bytes 983072 | tf_op jit(solution)/shard_map/all_to_all | solution.py:168
  83.3 1.6 copy.72
  85.8 2.7 %copy.73 = bf16[2,4,120,8,32]{4,1,2,3,0:T(4,128)(2,1)S(1)} copy(bf16[2,4,120,8,32]{2,4,3,1,0:T(8,128)(2,1)} %bitcast.123) | data formatting | bytes 983040 | tf_op jit(solution)/shard_map/reshape | solution.py:78
  88.6 2.4 %copy.74 = bf16[2,4,120,8,32]{4,1,2,3,0:T(4,128)(2,1)} copy(bf16[2,4,120,8,32]{2,4,3,1,0:T(8,128)(2,1)S(1)} %bitcast.122) | data formatting | bytes 983040 | tf_op jit(solution)/shard_map/reshape | solution.py:77
  91.0 5.6 %fusion.94 = f32[2,8,120,4,4]{4,3,2,1,0:T(4,128)} fusion(bf16[2,4,120,8,32]{4,1,2,3,0:T(4,128)(2,1)S(1)} %copy.73, bf16[2,4,120,8,32]{4,1,2,3,0:T(4,128)(2,1)} %copy.74), kind=kOutput, calls=%fused_computation.124 | convolution fusion | flops 1966080 | bytes 1105920 | tf_op jit(solution)/shard_map/vfphd,vgphd->vhfgp/dot_general | solution.py:75
  96.6 2.7 %copy.75 = f32[2,8,120,4,4]{2,1,3,4,0:T(8,128)S(1)} copy(f32[2,8,120,4,4]{4,3,2,1,0:T(4,128)} %fusion.94) | data formatting | bytes 245760 | tf_op jit(solution)/shard_map/vfphd,vgphd->vhfgp/dot_general | solution.py:75
  99.5 3.3 %copy.77 = bf16[2,8,4,4,120]{3,2,1,4,0:T(4,128)(2,1)S(1)} copy(bf16[2,8,4,4,120]{4,1,3,2,0:T(8,128)(2,1)S(1)} %divide_convert_fusion.12) | data formatting | bytes 122880 | tf_op jit(solution)/shard_map/convert_element_type | solution.py:81
  102.7 5.0 %convert_bitcast_fusion = bf16[2,4,120,8,32]{4,1,3,2,0:T(4,128)(2,1)} fusion(bf16[2,4,120,8,32]{4,1,3,2,0:T(4,128)(2,1)} %copy.76, bf16[2,8,4,4,120]{3,2,1,4,0:T(4,128)(2,1)S(1)} %copy.77), kind=kOutput, calls=%fused_computation.44 | convolution fusion | flops 2211840 | bytes 1044480 | tf_op jit(solution)/shard_map/vhfgp,vgphd->vfphd/dot_general | solution.py:82
  107.7 3.3 %copy.78 = bf16[2,4,120,8,32]{2,4,3,1,0:T(8,128)(2,1)S(1)} copy(bf16[2,4,120,8,32]{4,1,3,2,0:T(4,128)(2,1)} %convert_bitcast_fusion) | data formatting | bytes 983040 | tf_op jit(solution)/shard_map/convert_element_type | solution.py:87
  111.3 10.9 %all_to_all.12 = bf16[2,4,1,120,256]{4,3,2,0,1:T(8,128)(2,1)S(1)} all-to-all(bf16[2,4,1,120,256]{4,3,2,0,1:T(8,128)(2,1)S(1)} %copy.79), channel_id=1, replica_groups=mesh['frame'=4,'rows'=8] {'frame'}, dimensions={1} | all-to-all | bytes 983040 | tf_op jit(solution)/shard_map/all_to_all | solution.py:175
  125.2 1.3 collective-permute-start.1
  126.5 4.9 %collective-permute-start = (bf16[2,1,1,480,1024]{4,3,2,1,0:T(8,128)(2,1)S(1)}, bf16[2,1,1,480,1024]{4,3,2,1,0:T(8,128)(2,1)S(1)}, u32[]{:S(2)}, u32[]{:S(2)}) collective-permute-start(bf16[2,1,1,480,1024]{4,3,2,1,0:T(8,128)(2,1)S(1)} %pad_maximum_fusion), channel_id=1, source_target_pairs={{0,1},{1,2},{2,3},{3,4},{4,5},{5,6},{6,7},{8,9},{9,10},{10,11},{11... | collective-permute-start | bytes 5898248 | tf_op jit(solution)/shard_map/ppermute | solution.py:17
  131.4 40.4 %collective-permute-done.1 = bf16[2,1,1,480,1024]{4,3,2,1,0:T(8,128)(2,1)S(1)} collective-permute-done((bf16[2,1,1,480,1024]{4,3,2,1,0:T(8,128)(2,1)S(1)}, bf16[2,1,1,480,1024]{4,3,2,1,0:T(8,128)(2,1)S(1)}, u32[]{:S(2)}, u32[]{:S(2)}) %collective-permute-start.1) | collective-permute-done | bytes 1966112 | tf_op jit(solution)/shard_map/ppermute | solution.py:18
  171.8 42.3 %collective-permute-done = bf16[2,1,1,480,1024]{4,3,2,1,0:T(8,128)(2,1)S(1)} collective-permute-done((bf16[2,1,1,480,1024]{4,3,2,1,0:T(8,128)(2,1)S(1)}, bf16[2,1,1,480,1024]{4,3,2,1,0:T(8,128)(2,1)S(1)}, u32[]{:S(2)}, u32[]{:S(2)}) %collective-permute-start) | collective-permute-done | bytes 1966112 | tf_op jit(solution)/shard_map/ppermute | solution.py:17
  214.1 2.1 select_maximum_fusion
  216.2 5.2 %fusion.43 = bf16[2,1,1,480,256]{4,3,2,1,0:T(8,128)(2,1)} fusion(f32[1024]{0:T(1024)S(1)} %bitcast.134, bf16[2,1,3,482,1024]{4,3,2,1,0:T(8,128)(2,1)S(1)} %select_maximum_fusion, f32[1024]{0:T(1024)S(1)} %bitcast.135, bf16[2,1,1,480,1024]{4,3,2,1,0:T(8,128)(2,1)S(1)} %collective-permute-done.1, f32[1024]{0:T(1024)S(1)} %bitcast.128, ...), kind=kOutput, calls=%fused_computation.61 | convolution fusion | flops 531578880 | bytes 19238912 | tf_op jit(solution)/shard_map/dot_general | solution.py:189
  (56 shorter events, 10.3 us)
Async XLA Ops:
  0.0 123.4 %copy-start = (bf16[256,1024]{1,0:T(8,128)(2,1)S(1)}, bf16[256,1024]{1,0:T(8,128)(2,1)}, u32[]{:S(2)}) copy-start(bf16[256,1024]{1,0:T(8,128)(2,1)} %param.17) | copy-start | bytes 1572868
  10.5 4.4 %copy-start.3 = (bf16[256,256]{1,0:T(8,128)(2,1)S(1)}, bf16[256,256]{1,0:T(8,128)(2,1)}, u32[]{:S(2)}) copy-start(bf16[256,256]{1,0:T(8,128)(2,1)} %param.12) | copy-start | bytes 393220
  42.1 8.2 %copy-start.1 = (bf16[2,1,1,480,256]{4,3,2,1,0:T(8,128)(2,1)S(1)}, bf16[2,1,1,480,256]{4,3,2,1,0:T(8,128)(2,1)}, u32[]{:S(2)}) copy-start(bf16[2,1,1,480,256]{4,3,2,1,0:T(8,128)(2,1)} %param.10) | copy-start | bytes 1474564
  42.1 8.2 %copy-start.8 = (bf16[256,256]{1,0:T(8,128)(2,1)S(1)}, bf16[256,256]{1,0:T(8,128)(2,1)}, u32[]{:S(2)}) copy-start(bf16[256,256]{1,0:T(8,128)(2,1)} %param.13) | copy-start | bytes 393220
  50.2 1.3 copy-start.4
  50.2 6.6 %copy-start.2 = (bf16[256,512]{1,0:T(8,128)(2,1)S(1)}, bf16[256,512]{1,0:T(8,128)(2,1)}, u32[]{:S(2)}) copy-start(bf16[256,512]{1,0:T(8,128)(2,1)} %param.14) | copy-start | bytes 786436
  52.6 12.7 %all-to-all-start = ((bf16[2,1,4,120,256]{4,3,1,0,2:T(8,128)(2,1)}), bf16[2,1,4,120,256]{4,3,1,0,2:T(8,128)(2,1)S(1)}, u32[]{:S(2)}, u32[]{:S(2)}) async-start(bf16[2,1,4,120,256]{4,3,1,0,2:T(8,128)(2,1)} %copy.69), calls=%async_computation | async-start | bytes 983040 | tf_op jit(solution)/shard_map/all_to_all | solution.py:169
  65.3 18.0 %all-to-all-start.1 = ((bf16[2,1,4,120,512]{4,3,1,0,2:T(8,128)(2,1)}), bf16[2,1,4,120,512]{4,3,1,0,2:T(8,128)(2,1)}, u32[]{:S(2)}, u32[]{:S(2)}) async-start(bf16[2,1,4,120,512]{4,3,1,0,2:T(8,128)(2,1)} %copy.71), calls=%async_computation.1 | async-start | bytes 1966080 | tf_op jit(solution)/shard_map/all_to_all | solution.py:168
  107.7 14.5 %copy-start.5 = (bf16[256,256]{1,0:T(8,128)(2,1)S(1)}, bf16[256,256]{1,0:T(8,128)(2,1)}, u32[]{:S(2)}) copy-start(bf16[256,256]{1,0:T(8,128)(2,1)} %param.16) | copy-start | bytes 393220
  124.2 7.2 %copy-start.6 = (bf16[3,3,1024]{2,1,0:T(4,128)(2,1)S(1)}, bf16[3,3,1024]{2,1,0:T(4,128)(2,1)}, u32[]{:S(2)}) copy-start(bf16[3,3,1024]{2,1,0:T(4,128)(2,1)} %param.18) | copy-start | bytes 55300
  125.2 46.7 %collective-permute-start.1 = (bf16[2,1,1,480,1024]{4,3,2,1,0:T(8,128)(2,1)S(1)}, bf16[2,1,1,480,1024]{4,3,2,1,0:T(8,128)(2,1)S(1)}, u32[]{:S(2)}, u32[]{:S(2)}) collective-permute-start(bf16[2,1,1,480,1024]{4,3,2,1,0:T(8,128)(2,1)S(1)} %pad_maximum_fusion), channel_id=1, source_target_pairs={{1,0},{2,1},{3,2},{4,3},{5,4},{6,5},{7,6},{9,8},{10,9},{11,10},{12... | collective-permute-start | bytes 5898248 | tf_op jit(solution)/shard_map/ppermute | solution.py:18
  126.5 87.7 %collective-permute-start = (bf16[2,1,1,480,1024]{4,3,2,1,0:T(8,128)(2,1)S(1)}, bf16[2,1,1,480,1024]{4,3,2,1,0:T(8,128)(2,1)S(1)}, u32[]{:S(2)}, u32[]{:S(2)}) collective-permute-start(bf16[2,1,1,480,1024]{4,3,2,1,0:T(8,128)(2,1)S(1)} %pad_maximum_fusion), channel_id=1, source_target_pairs={{0,1},{1,2},{2,3},{3,4},{4,5},{5,6},{6,7},{8,9},{9,10},{10,11},{11... | collective-permute-start | bytes 5898248 | tf_op jit(solution)/shard_map/ppermute | solution.py:17
  131.4 84.8 %copy-start.7 = (bf16[1024,256]{1,0:T(8,128)(2,1)S(1)}, bf16[1024,256]{1,0:T(8,128)(2,1)}, u32[]{:S(2)}) copy-start(bf16[1024,256]{1,0:T(8,128)(2,1)} %param.19) | copy-start | bytes 1572868
where the time goes:
time: 222 us; the launch traced here: 221 us
  waiting for transfers between devices  100 us (45%)
  matrix products  45.4 us (20%)
  local copies, waits for them, and re-layouts  27 us (12%)
  other arithmetic  22.8 us (10%)
  starting transfers between devices  14.8 us (7%)
  blocking collectives  10.9 us (5%)
    ppermute x1, waiting for transfers between devices, with_halo(): before = lax.ppermute(last, axis, up)  42.3 us
    ppermute x1, waiting for transfers between devices, with_halo(): after = lax.ppermute(leading, axis, down)  40.4 us
    dot_general x2, matrix products, stereo_row(): jnp.einsum('vhqk,vkhd->vqhd', weights, values_other[:, :, offset:offset +...  16.1 us
    sub x2, other arithmetic, stereo_row(): weights = jax.nn.softmax(scores, axis=-1).astype(jnp.bfloat16)  14.9 us
    all_to_all x1, blocking collectives, shards(): lax.all_to_all(attended, 'frame', split_axis=1, concat_axis=2, tiled=True)  10.9 us
    all_to_all x1, waiting for transfers between devices, shards(): lax.all_to_all(paired, 'frame', split_axis=2, concat_axis=1, tiled=True)  10.5 us
    dot_general x2, matrix products, stereo_row(): jnp.einsum('vqhd,vkhd->vhqk', query_rows[:, :, offset:offset + group_size...  8.69 us
    all_to_all x1, waiting for transfers between devices, shards(): lax.all_to_all(value_rows, 'frame', split_axis=2, concat_axis=1, tiled=True)  6.99 us
  transfers between devices with their start and end apart: 4, of which 4 were waited for; matrix products, arithmetic and copies ran while one was open for 2% of the time, Pallas kernels for 0%

commit v1 on v0

v1 whole, which is shorter than its diff:
```python
import functools

import jax
import jax.numpy as jnp
from jax import lax
from jax.experimental import pallas as pl
from jax.experimental.pallas import tpu as pltpu
from jax.sharding import PartitionSpec as P

HEADS = 8
HEAD_DIM = 32
SCALE_LOG2 = HEAD_DIM ** (-0.5) * 1.4426950408889634
VMEM_LIMIT = 40 * 1024 * 1024


def round_up(value, unit):
    return (value + unit - 1) // unit * unit


def layer_norm(widened):
    centred = widened - jnp.mean(widened, axis=-1, keepdims=True)
    variance = jnp.mean(centred * centred, axis=-1, keepdims=True)
    return (centred * lax.rsqrt(variance + 1e-05)).astype(jnp.bfloat16)


def dot_dims(lhs, rhs, lhs_dim, rhs_dim):
    return lax.dot_general(
        lhs, rhs, (((lhs_dim,), (rhs_dim,)), ((), ())), preferred_element_type=jnp.float32
    )


def stereo_kernel(left, cols, window, query_ref, other_ref, qk_ref, v_ref, out_ref, windows_ref):
    width, channels = query_ref.shape[-2:]
    rows = query_ref[...].reshape(width, channels).astype(jnp.float32)
    normed = layer_norm(rows)
    normed_other = layer_norm(other_ref[...].reshape(width, channels).astype(jnp.float32))
    queries = dot_dims(normed, qk_ref[:, :channels], 1, 0).astype(jnp.bfloat16)
    keys = dot_dims(normed_other, qk_ref[:, channels:], 1, 0).astype(jnp.bfloat16)
    values_t = dot_dims(v_ref[...], normed_other, 0, 1).astype(jnp.bfloat16)
    lane_head = lax.broadcasted_iota(jnp.int32, (width, 128), 1) // HEAD_DIM
    per_group = 128 // HEAD_DIM
    attended = []
    for head in range(HEADS):
        lanes = slice(head // per_group * 128, head // per_group * 128 + 128)
        keys_head = jnp.where(
            lane_head == head % per_group, keys[:, lanes], jnp.zeros((), jnp.bfloat16)
        )
        scores_t = dot_dims(keys_head, queries[:, lanes], 1, 1)
        top = jnp.max(scores_t, axis=0, keepdims=True)
        weights_t = jnp.exp2((scores_t - top) * SCALE_LOG2)
        total = jnp.sum(weights_t, axis=0, keepdims=True)
        mixed = dot_dims(
            values_t[head * HEAD_DIM : (head + 1) * HEAD_DIM], weights_t.astype(jnp.bfloat16), 1, 0
        )
        attended.append((mixed / total).astype(jnp.bfloat16))
    update = dot_dims(jnp.concatenate(attended, axis=0), out_ref[...], 0, 0)
    section = rows + update
    owners = width // cols
    tail = round_up((owners - 1) * cols + window, 8) - width
    padded = jnp.concatenate([section, jnp.zeros((tail, channels), jnp.float32)], axis=0)
    padded = pltpu.roll(padded, left, 0)
    for owner in range(owners):
        windows_ref[0, owner] = padded[owner * cols : owner * cols + window].astype(jnp.bfloat16)


def stereo(video, first, count, owners, left, window, stereo_qk, stereo_v, stereo_out):
    width, channels = video.shape[-2:]
    row_block = (1, 1, 1, width, channels)
    whole = lambda array: pl.BlockSpec(array.shape, lambda v: (0,) * array.ndim)
    return pl.pallas_call(
        functools.partial(stereo_kernel, left, width // owners, window),
        grid=(count,),
        in_specs=[
            pl.BlockSpec(row_block, lambda v: (first + v, 0, 0, 0, 0)),
            pl.BlockSpec(row_block, lambda v: (1 - first - v, 0, 0, 0, 0)),
            whole(stereo_qk),
            whole(stereo_v),
            whole(stereo_out),
        ],
        out_specs=pl.BlockSpec((1, owners, window, channels), lambda v: (v, 0, 0, 0)),
        out_shape=jax.ShapeDtypeStruct((count, owners, window, channels), jnp.bfloat16),
        compiler_params=pltpu.CompilerParams(vmem_limit_bytes=VMEM_LIMIT),
        cost_estimate=pl.CostEstimate(
            flops=count * 1_200_000_000, bytes_accessed=2_000_000, transcendentals=count * 2_000_000
        ),
        name="stereo",
    )(video, video, stereo_qk, stereo_v, stereo_out)


def head_sum(product):
    channels, width = product.shape
    return jnp.sum(product.reshape(HEADS, HEAD_DIM, width), axis=1, keepdims=True)


def temporal_kernel(side_ref, own_ref, other_ref, qk_ref, v_ref, out_ref, section_ref):
    _, _, frames, window, channels = own_ref.shape
    side = side_ref[0]
    for slot in range(2):
        rows = own_ref[0, slot].reshape(frames * window, channels).astype(jnp.float32)
        rows_other = other_ref[0, slot].reshape(frames * window, channels).astype(jnp.float32)
        normed = layer_norm(rows)
        normed_all = jnp.concatenate([normed, layer_norm(rows_other)], axis=0)
        queries = dot_dims(qk_ref[:, :channels], normed, 0, 1).astype(jnp.bfloat16)
        keys = dot_dims(qk_ref[:, channels:], normed_all, 0, 1).astype(jnp.bfloat16)
        values = dot_dims(v_ref[...], normed_all, 0, 1).astype(jnp.bfloat16)
        attended = []
        for frame in range(frames):
            query = queries[:, frame * window : (frame + 1) * window].astype(jnp.float32)
            scores = [
                head_sum(
                    query * keys[:, other * window : (other + 1) * window].astype(jnp.float32)
                )
                for other in range(2 * frames)
            ]
            top = functools.reduce(jnp.maximum, scores)
            weights = [jnp.exp2((score - top) * SCALE_LOG2) for score in scores]
            inverse = 1.0 / functools.reduce(jnp.add, weights)
            mixed = jnp.zeros((HEADS, HEAD_DIM, window), jnp.float32)
            for other in range(2 * frames):
                value = values[:, other * window : (other + 1) * window].astype(jnp.float32)
                mixed = mixed + value.reshape(HEADS, HEAD_DIM, window) * (
                    weights[other] * inverse
                )
            attended.append(mixed.reshape(channels, window).astype(jnp.bfloat16))
        update = dot_dims(jnp.concatenate(attended, axis=1), out_ref[...], 0, 0)
        section = (rows + update).astype(jnp.bfloat16)
        section_ref[0, side ^ slot] = section.reshape(frames, window, channels)


def temporal(side, own, other, temporal_qk, temporal_v, temporal_out):
    block = pl.BlockSpec((1,) + own.shape[1:], lambda v, s: (v, 0, 0, 0, 0))
    whole = lambda array: pl.BlockSpec(array.shape, lambda v, s: (0,) * array.ndim)
    return pl.pallas_call(
        temporal_kernel,
        grid_spec=pltpu.PrefetchScalarGridSpec(
            num_scalar_prefetch=1,
            grid=(own.shape[0],),
            in_specs=[block, block, whole(temporal_qk), whole(temporal_v), whole(temporal_out)],
            out_specs=block,
        ),
        out_shape=jax.ShapeDtypeStruct(own.shape, jnp.bfloat16),
        compiler_params=pltpu.CompilerParams(vmem_limit_bytes=VMEM_LIMIT),
        cost_estimate=pl.CostEstimate(
            flops=own.shape[0] * 700_000_000, bytes_accessed=2_000_000, transcendentals=0
        ),
        name="temporal",
    )(side, own, other, temporal_qk, temporal_v, temporal_out)


def gelu(values):
    inner = values * (0.7978845608028654 + 0.035677408136300125 * (values * values))
    half = 0.5 * values
    return half + half * jnp.tanh(inner)


def mlp_kernel(left, side_ref, rows_ref, top_ref, bottom_ref, up_ref, mix_ref, down_ref, out_ref):
    _, _, frames, window, channels = rows_ref.shape
    hidden_size = up_ref.shape[1]
    chunk = 256
    side = side_ref[0]
    for frame in range(frames):
        middle = rows_ref[0, :, frame].reshape(2 * window, channels)
        rows = jnp.concatenate([top_ref[0, frame], middle, bottom_ref[0, frame]], axis=0)
        normed = layer_norm(rows.astype(jnp.float32))
        update = jnp.zeros((2 * window, channels), jnp.float32)
        for start in range(0, hidden_size, chunk):
            lanes = slice(start, start + chunk)
            hidden = gelu(dot_dims(normed, up_ref[:, lanes], 1, 0))
            hidden = hidden.astype(jnp.bfloat16).astype(jnp.float32)
            lines = [hidden[line * window : (line + 1) * window] for line in range(4)]
            taps = mix_ref[:, :, lanes].astype(jnp.float32)
            mixed = []
            for line in range(2):
                columns = [
                    functools.reduce(
                        jnp.add, [lines[line + a] * taps[a, b][None] for a in range(3)]
                    )
                    for b in range(3)
                ]
                mixed.append(
                    (
                        pltpu.roll(columns[0], 1, 0)
                        + columns[1]
                        + pltpu.roll(columns[2], window - 1, 0)
                    ).astype(jnp.bfloat16)
                )
            update = update + dot_dims(jnp.concatenate(mixed, axis=0), down_ref[lanes], 1, 0)
        result = middle.astype(jnp.float32) + update
        for line in range(2):
            shifted = pltpu.roll(result[line * window : (line + 1) * window], window - left, 0)
            out_ref[0, side ^ line, frame] = shifted.astype(jnp.bfloat16)


def mlp(side, left, rows, top, bottom, mlp_up, mix_kernel, mlp_down):
    block = pl.BlockSpec((1,) + rows.shape[1:], lambda v, s: (v, 0, 0, 0, 0))
    line = pl.BlockSpec((1,) + top.shape[1:], lambda v, s: (v, 0, 0, 0))
    whole = lambda array: pl.BlockSpec(array.shape, lambda v, s: (0,) * array.ndim)
    return pl.pallas_call(
        functools.partial(mlp_kernel, left),
        grid_spec=pltpu.PrefetchScalarGridSpec(
            num_scalar_prefetch=1,
            grid=(rows.shape[0],),
            in_specs=[block, line, line, whole(mlp_up), whole(mix_kernel), whole(mlp_down)],
            out_specs=block,
        ),
        out_shape=jax.ShapeDtypeStruct(rows.shape, jnp.bfloat16),
        compiler_params=pltpu.CompilerParams(vmem_limit_bytes=VMEM_LIMIT),
        cost_estimate=pl.CostEstimate(
            flops=rows.shape[0] * 1_000_000_000, bytes_accessed=3_000_000, transcendentals=0
        ),
        name="mlp",
    )(side, rows, top, bottom, mlp_up, mix_kernel, mlp_down)


VIEW_GROUPS = ((0, 2),)


def shards(
    video,
    stereo_qk,
    stereo_v,
    stereo_out,
    temporal_qk,
    temporal_v,
    temporal_out,
    mlp_up,
    mix_kernel,
    mlp_down,
):
    width, channels = video.shape[-2:]
    frame_size, rows_size = lax.axis_size("frame"), lax.axis_size("rows")
    pairs = frame_size // 2
    owners = frame_size
    cols = width // owners
    window = round_up(cols + 2, 16)
    left = (window - cols) // 2
    frame, row = lax.axis_index("frame"), lax.axis_index("rows")
    pair, side = frame // 2, row % 2
    side_arg = side.astype(jnp.int32)[None]
    both = ("frame", "rows")
    slots = [(s, p) for s in range(2) for p in range(pairs)]

    def owner_at(s, p):
        return lax.rem(pair + p, pairs) * 2 + (side ^ s)

    def chip_moves(s, p):
        return [
            (
                f * rows_size + r,
                ((f // 2 + p) % pairs * 2 + f % 2) * rows_size + (r ^ s),
            )
            for f in range(frame_size)
            for r in range(rows_size)
        ]

    siblings = [(f, f ^ 1) for f in range(frame_size)]
    upward = [(r, r + 2) for r in range(rows_size - 2)]
    downward = [(r + 2, r) for r in range(rows_size - 2)]
    outputs = []
    for first, count in VIEW_GROUPS:
        windows = stereo(
            video, first, count, owners, left, window, stereo_qk, stereo_v, stereo_out
        )
        pieces = []
        for s, p in slots:
            piece = lax.dynamic_index_in_dim(windows, owner_at(s, p), 1, keepdims=False)
            if (s, p) != (0, 0):
                piece = lax.ppermute(piece, both, chip_moves(s, p))
            pieces.append(piece)
        own = jnp.stack(pieces, axis=1).reshape(count, 2, pairs, window, channels)
        other = lax.ppermute(own, "frame", siblings)
        section = temporal(side_arg, own, other, temporal_qk, temporal_v, temporal_out)
        top = lax.ppermute(section[:, 1], "rows", upward)
        bottom = lax.ppermute(section[:, 0], "rows", downward)
        result = mlp(side_arg, left, section, top, bottom, mlp_up, mix_kernel, mlp_down)
        output = jnp.zeros((count, width, channels), jnp.bfloat16)
        for s, p in slots:
            piece = result[:, s, p, :cols]
            if (s, p) != (0, 0):
                back = [(j, i) for i, j in chip_moves(s, p)]
                piece = lax.ppermute(piece, both, back)
            output = lax.dynamic_update_slice(output, piece, (0, owner_at(s, p) * cols, 0))
        outputs.append(output)
    return jnp.concatenate(outputs, axis=0).reshape(video.shape)


def solution(mesh):
    in_specs = (P(None, "frame", "rows", None, None), P(), P(), P(), P(), P(), P(), P(), P(), P())
    out_specs = P(None, "frame", "rows", None, None)
    return jax.shard_map(shards, mesh=mesh, in_specs=in_specs, out_specs=out_specs, check_vma=False)
```

time: 222 us -> 60.2 us (0.27)
  waiting for transfers between devices: 100 us -> 21.3 us
  matrix products: 45.4 us -> 0 us
  other arithmetic: 22.8 us -> 0.07 us
  local copies, waits for them, and re-layouts: 27 us -> 5.42 us
  Pallas kernels: 0 us -> 19.8 us
  blocking collectives: 10.9 us -> 0 us
    ppermute x2 -> x9, waiting for transfers between devices: 82.7 us -> 21.3 us  [the longest x3 6.24 us: shards(): piece = lax.ppermute(piece, both, chip_moves(s, p))]
    dot_general x15 -> x0, matrix products: 45.4 us -> none  [the longest x2 16.1 us: stereo_row(): jnp.einsum('vhqk,vkhd->vqhd', weights, values_other[:, :, offset:offset +...]
    pallas_call x0 -> x3, Pallas kernels: none -> 19.8 us  [the longest x1 9.02 us: stereo(): pl.pallas_call(functools.partial(stereo_kernel, left, width // owners, wi...]
    all_to_all x2 -> x0, waiting for transfers between devices: 17.5 us -> none  [the longest x1 10.5 us: shards(): lax.all_to_all(paired, 'frame', split_axis=2, concat_axis=1, tiled=True)]
    sub x2 -> x0, other arithmetic: 14.9 us -> none  [stereo_row(): weights = jax.nn.softmax(scores, axis=-1).astype(jnp.bfloat16)]
    all_to_all x1 -> x0, blocking collectives: 10.9 us -> none  [shards(): lax.all_to_all(attended, 'frame', split_axis=1, concat_axis=2, tiled=True)]
    all_to_all x2 -> x0, starting transfers between devices: 8.63 us -> none  [the longest x1 4.44 us: shards(): lax.all_to_all(paired, 'frame', split_axis=2, concat_axis=1, tiled=True)]
    reshape x5 -> x1, local copies, waits for them, and re-layouts: 7.53 us -> 0.04 us  [shards(): return jnp.concatenate(outputs, axis=0).reshape(video.shape)]
  transfers between devices with their start and end apart: 4 -> 9, of which waited for: 4 -> 7; matrix products, arithmetic and copies ran while one was open for 2% -> 0% of each run, Pallas kernels for 0% -> 0%
where the time goes in v1:
time: 60.2 us; the launch traced here: 59.9 us
  waiting for transfers between devices  21.3 us (35%)
  Pallas kernels  19.8 us (33%)
  starting transfers between devices  13.1 us (22%)
  local copies, waits for them, and re-layouts  5.42 us (9%)
    pallas_call x1, Pallas kernels, stereo(): pl.pallas_call(functools.partial(stereo_kernel, left, width // owners, wi...  9.02 us
    pallas_call x1, Pallas kernels, mlp(): pl.pallas_call(functools.partial(mlp_kernel, left), grid_spec=pltpu.Prefe...  7.45 us
    ppermute x3, waiting for transfers between devices, shards(): piece = lax.ppermute(piece, both, chip_moves(s, p))  6.24 us
    unnamed x22, local copies, waits for them, and re-layouts  4.58 us
    ppermute x3, waiting for transfers between devices, shards(): piece = lax.ppermute(piece, both, back)  4.57 us
    ppermute x3, starting transfers between devices, shards(): piece = lax.ppermute(piece, both, chip_moves(s, p))  4.55 us
    ppermute x1, waiting for transfers between devices, shards(): top = lax.ppermute(section[:, 1], 'rows', upward)  4.52 us
    ppermute x1, waiting for transfers between devices, shards(): bottom = lax.ppermute(section[:, 0], 'rows', downward)  4.13 us
  transfers between devices with their start and end apart: 9, of which 7 were waited for; matrix products, arithmetic and copies ran while one was open for 0% of the time, Pallas kernels for 0%

profile of v1, /device:TPU:0, one launch (start us, length us, event | category | flops | bytes accessed | tf_op | source)
XLA Modules:
  0.0 59.9 jit_solution(10440907944810328169)
XLA Ops:
  0.0 1.0 %copy-done.2 = bf16[2,1,1,480,256]{4,3,2,1,0:T(8,128)(2,1)S(1)} copy-done((bf16[2,1,1,480,256]{4,3,2,1,0:T(8,128)(2,1)S(1)}, bf16[2,1,1,480,256]{4,3,2,1,0:T(8,128)(2,1)}, u32[]{:S(2)}) %copy-start.2) | copy-done | bytes 491544
  1.0 0.9 %copy-done.3 = bf16[256,512]{1,0:T(8,128)(2,1)S(1)} copy-done((bf16[256,512]{1,0:T(8,128)(2,1)S(1)}, bf16[256,512]{1,0:T(8,128)(2,1)}, u32[]{:S(2)}) %copy-start.3) | copy-done | bytes 262168
  2.0 0.9 %copy-done.5 = bf16[256,256]{1,0:T(8,128)(2,1)S(1)} copy-done((bf16[256,256]{1,0:T(8,128)(2,1)S(1)}, bf16[256,256]{1,0:T(8,128)(2,1)}, u32[]{:S(2)}) %copy-start.5) | copy-done | bytes 131096
  2.9 0.9 %copy-done.6 = bf16[256,256]{1,0:T(8,128)(2,1)S(1)} copy-done((bf16[256,256]{1,0:T(8,128)(2,1)S(1)}, bf16[256,256]{1,0:T(8,128)(2,1)}, u32[]{:S(2)}) %copy-start.6) | copy-done | bytes 131096
  3.8 9.0 %stereo.1 = bf16[2,4,128,256]{3,2,1,0:T(8,128)(2,1)S(1)} custom-call(bf16[2,1,1,480,256]{4,3,2,1,0:T(8,128)(2,1)S(1)} %copy-done.2, bf16[2,1,1,480,256]{4,3,2,1,0:T(8,128)(2,1)S(1)} %copy-done.2, bf16[256,512]{1,0:T(8,128)(2,1)S(1)} %copy-done.3, bf16[256,256]{1,0:T(8,128)(2,1)S(1)} %copy-done.5, bf16[256,256]{1,0:T(8,128)(2,1)S(1)} %copy-done.6), custom_call_target="tpu_custom_call" | custom-call | flops 2400000000 | bytes 2000000 | tf_op jit(solution)/shard_map/stereo/pallas_call | solution.py:70
  12.9 3.0 %collective-permute-start = (bf16[2,128,256]{2,1,0:T(8,128)(2,1)S(1)}, bf16[2,128,256]{2,1,0:T(8,128)(2,1)S(1)}, u32[]{:S(2)}, u32[]{:S(2)}) collective-permute-start(bf16[2,128,256]{2,1,0:T(8,128)(2,1)S(1)} %get-tuple-element.14), channel_id=1, source_target_pairs={{0,16},{1,17},{2,18},{3,19},{4,20},{5,21},{6,22},{7,23},{8,24},{9,... | collective-permute-start | bytes 393224 | tf_op jit(solution)/shard_map/ppermute | solution.py:268
  15.9 1.5 %collective-permute-start.1 = (bf16[2,128,256]{2,1,0:T(8,128)(2,1)S(1)}, bf16[2,128,256]{2,1,0:T(8,128)(2,1)S(1)}, u32[]{:S(2)}, u32[]{:S(2)}) collective-permute-start(bf16[2,128,256]{2,1,0:T(8,128)(2,1)S(1)} %get-tuple-element.13), channel_id=1, source_target_pairs={{0,1},{1,0},{2,3},{3,2},{4,5},{5,4},{6,7},{7,6},{8,9},{9,8},{10,11... | collective-permute-start | bytes 393224 | tf_op jit(solution)/shard_map/ppermute | solution.py:268
  17.4 0.0 collective-permute-start.2
  17.4 2.4 %collective-permute-done = bf16[2,128,256]{2,1,0:T(8,128)(2,1)S(1)} collective-permute-done((bf16[2,128,256]{2,1,0:T(8,128)(2,1)S(1)}, bf16[2,128,256]{2,1,0:T(8,128)(2,1)S(1)}, u32[]{:S(2)}, u32[]{:S(2)}) %collective-permute-start) | collective-permute-done | bytes 131104 | tf_op jit(solution)/shard_map/ppermute | solution.py:268
  19.8 3.9 %collective-permute-done.1 = bf16[2,128,256]{2,1,0:T(8,128)(2,1)S(1)} collective-permute-done((bf16[2,128,256]{2,1,0:T(8,128)(2,1)S(1)}, bf16[2,128,256]{2,1,0:T(8,128)(2,1)S(1)}, u32[]{:S(2)}, u32[]{:S(2)}) %collective-permute-start.1) | collective-permute-done | bytes 131104 | tf_op jit(solution)/shard_map/ppermute | solution.py:268
  23.7 0.0 collective-permute-done.2
  23.7 0.1 pad_maximum_fusion
  23.8 0.1 collective-permute-start.3
  23.8 1.9 %collective-permute-done.3.other_ref = bf16[2,2,2,128,256]{4,3,2,1,0:T(8,128)(2,1)S(1)} collective-permute-done((bf16[2,2,2,128,256]{4,3,2,1,0:T(8,128)(2,1)S(1)}, bf16[2,2,2,128,256]{4,3,2,1,0:T(8,128)(2,1)S(1)}, u32[]{:S(2)}, u32[]{:S(2)}) %collective-permute-start.3) | collective-permute-done | bytes 524320 | tf_op jit(solution)/shard_map/ppermute | solution.py:271
  25.7 0.0 copy-start.9
  25.8 3.4 %temporal.1.rows_ref = bf16[2,2,2,128,256]{4,3,2,1,0:T(8,128)(2,1)S(1)} custom-call(s32[1]{0:T(128)} %bitcast.side_ref, bf16[2,2,2,128,256]{4,3,2,1,0:T(8,128)(2,1)S(1)} %bitcast.38, bf16[2,2,2,128,256]{4,3,2,1,0:T(8,128)(2,1)S(1)} %collective-permute-done.3.other_ref, bf16[256,512]{1,0:T(8,128)(2,1)S(1)} %copy-done.4, bf16[256,256]{1,0:T(8,128)(2,1)S(1)} %copy-done.7, ...), custom_call_target="tpu_custom_call" | custom-call | flops 1400000000 | bytes 2000000 | tf_op jit(solution)/shard_map/temporal/pallas_call | solution.py:133
  29.1 0.0 copy-start
  29.1 0.0 copy-start.1
  29.2 3.6 %collective-permute-start.4 = (bf16[2,2,128,256]{3,2,1,0:T(8,128)(2,1)S(1)}, bf16[2,2,128,256]{3,2,1,0:T(8,128)(2,1)S(1)}, u32[]{:S(2)}, u32[]{:S(2)}) collective-permute-start(bf16[2,2,128,256]{3,2,1,0:T(8,128)(2,1)S(1)} %get-tuple-element.10), channel_id=1, source_target_pairs={{0,2},{1,3},{2,4},{3,5},{4,6},{5,7},{8,10},{9,11},{10,12},{11,13},... | collective-permute-start | bytes 786440 | tf_op jit(solution)/shard_map/ppermute | solution.py:273
  32.8 1.3 %collective-permute-start.5 = (bf16[2,2,128,256]{3,2,1,0:T(8,128)(2,1)S(1)}, bf16[2,2,128,256]{3,2,1,0:T(8,128)(2,1)S(1)}, u32[]{:S(2)}, u32[]{:S(2)}) collective-permute-start(bf16[2,2,128,256]{3,2,1,0:T(8,128)(2,1)S(1)} %get-tuple-element.9), channel_id=1, source_target_pairs={{2,0},{3,1},{4,2},{5,3},{6,4},{7,5},{10,8},{11,9},{12,10},{13,11},... | collective-permute-start | bytes 786440 | tf_op jit(solution)/shard_map/ppermute | solution.py:274
  34.1 4.5 %collective-permute-done.4.top_ref = bf16[2,2,128,256]{3,2,1,0:T(8,128)(2,1)S(1)} collective-permute-done((bf16[2,2,128,256]{3,2,1,0:T(8,128)(2,1)S(1)}, bf16[2,2,128,256]{3,2,1,0:T(8,128)(2,1)S(1)}, u32[]{:S(2)}, u32[]{:S(2)}) %collective-permute-start.4) | collective-permute-done | bytes 262176 | tf_op jit(solution)/shard_map/ppermute | solution.py:273
  38.6 4.1 %collective-permute-done.5.bottom_ref = bf16[2,2,128,256]{3,2,1,0:T(8,128)(2,1)S(1)} collective-permute-done((bf16[2,2,128,256]{3,2,1,0:T(8,128)(2,1)S(1)}, bf16[2,2,128,256]{3,2,1,0:T(8,128)(2,1)S(1)}, u32[]{:S(2)}, u32[]{:S(2)}) %collective-permute-start.5) | collective-permute-done | bytes 262176 | tf_op jit(solution)/shard_map/ppermute | solution.py:274
  42.8 7.5 %mlp.1 = bf16[2,2,2,128,256]{4,3,2,1,0:T(8,128)(2,1)S(1)} custom-call(s32[1]{0:T(128)} %bitcast.side_ref, bf16[2,2,2,128,256]{4,3,2,1,0:T(8,128)(2,1)S(1)} %temporal.1.rows_ref, bf16[2,2,128,256]{3,2,1,0:T(8,128)(2,1)S(1)} %collective-permute-done.4.top_ref, bf16[2,2,128,256]{3,2,1,0:T(8,128)(2,1)S(1)} %collective-permute-done.5.bottom_ref, ...), custom_call_target="tpu_custom_call" | custom-call | flops 2000000000 | bytes 3000000 | tf_op jit(solution)/shard_map/mlp/pallas_call | solution.py:198
  50.3 1.3 %collective-permute-start.6 = (bf16[2,120,256]{2,1,0:T(8,128)(2,1)S(1)}, bf16[2,120,256]{2,1,0:T(8,128)(2,1)S(1)}, u32[]{:S(2)}, u32[]{:S(2)}) collective-permute-start(bf16[2,120,256]{2,1,0:T(8,128)(2,1)S(1)} %get-tuple-element.7), channel_id=1, source_target_pairs={{16,0},{17,1},{18,2},{19,3},{20,4},{21,5},{22,6},{23,7},{24,8},{25... | collective-permute-start | bytes 368648 | tf_op jit(solution)/shard_map/ppermute | solution.py:281
  51.6 0.8 %collective-permute-start.7 = (bf16[2,120,256]{2,1,0:T(8,128)(2,1)S(1)}, bf16[2,120,256]{2,1,0:T(8,128)(2,1)S(1)}, u32[]{:S(2)}, u32[]{:S(2)}) collective-permute-start(bf16[2,120,256]{2,1,0:T(8,128)(2,1)S(1)} %get-tuple-element.6), channel_id=1, source_target_pairs={{1,0},{0,1},{3,2},{2,3},{5,4},{4,5},{7,6},{6,7},{9,8},{8,9},{11,10... | collective-permute-start | bytes 368648 | tf_op jit(solution)/shard_map/ppermute | solution.py:281
  52.4 1.4 %collective-permute-start.8 = (bf16[2,120,256]{2,1,0:T(8,128)(2,1)S(1)}, bf16[2,120,256]{2,1,0:T(8,128)(2,1)S(1)}, u32[]{:S(2)}, u32[]{:S(2)}) collective-permute-start(bf16[2,120,256]{2,1,0:T(8,128)(2,1)S(1)} %get-tuple-element.5), channel_id=1, source_target_pairs={{17,0},{16,1},{19,2},{18,3},{21,4},{20,5},{23,6},{22,7},{25,8},{24... | collective-permute-start | bytes 368648 | tf_op jit(solution)/shard_map/ppermute | solution.py:281
  53.9 2.6 %collective-permute-done.6 = bf16[2,120,256]{2,1,0:T(8,128)(2,1)S(1)} collective-permute-done((bf16[2,120,256]{2,1,0:T(8,128)(2,1)S(1)}, bf16[2,120,256]{2,1,0:T(8,128)(2,1)S(1)}, u32[]{:S(2)}, u32[]{:S(2)}) %collective-permute-start.6) | collective-permute-done | bytes 122912 | tf_op jit(solution)/shard_map/ppermute | solution.py:281
  56.5 2.0 %collective-permute-done.7 = bf16[2,120,256]{2,1,0:T(8,128)(2,1)S(1)} collective-permute-done((bf16[2,120,256]{2,1,0:T(8,128)(2,1)S(1)}, bf16[2,120,256]{2,1,0:T(8,128)(2,1)S(1)}, u32[]{:S(2)}, u32[]{:S(2)}) %collective-permute-start.7) | collective-permute-done | bytes 122912 | tf_op jit(solution)/shard_map/ppermute | solution.py:281
  58.5 0.0 copy-start.10
  58.5 0.0 collective-permute-done.8
  58.5 0.8 %copy-done.10 = bf16[2,1,1,480,256]{4,3,2,1,0:T(8,128)(2,1)} copy-done((bf16[2,1,1,480,256]{4,3,2,1,0:T(8,128)(2,1)}, bf16[2,1,1,480,256]{4,3,2,1,0:T(8,128)(2,1)S(1)}, u32[]{:S(2)}) %copy-start.10) | copy-done | bytes 491544
  59.3 0.7 %bitcast_dynamic-update-slice_fusion = bf16[2,1,1,480,256]{4,3,2,1,0:T(8,128)(2,1)} fusion(bf16[2,1,1,480,256]{4,3,2,1,0:T(8,128)(2,1)} %copy-done.10, s32[]{:T(128)S(6)} %select_n.45, bf16[2,120,256]{2,1,0:T(8,128)(2,1)S(1)} %collective-permute-done.8), kind=kLoop, calls=%fused_computation.10 | loop fusion | bytes 245764 | tf_op jit(solution)/shard_map/dynamic_update_slice | solution.py:282
  (19 shorter events, 0.2 us)
Async XLA Ops:
  0.0 1.0 %copy-start.2 = (bf16[2,1,1,480,256]{4,3,2,1,0:T(8,128)(2,1)S(1)}, bf16[2,1,1,480,256]{4,3,2,1,0:T(8,128)(2,1)}, u32[]{:S(2)}) copy-start(bf16[2,1,1,480,256]{4,3,2,1,0:T(8,128)(2,1)} %other_ref.1) | copy-start | bytes 1474564
  1.0 0.9 %copy-start.3 = (bf16[256,512]{1,0:T(8,128)(2,1)S(1)}, bf16[256,512]{1,0:T(8,128)(2,1)}, u32[]{:S(2)}) copy-start(bf16[256,512]{1,0:T(8,128)(2,1)} %qk_ref.2) | copy-start | bytes 786436
  2.0 0.9 %copy-start.5 = (bf16[256,256]{1,0:T(8,128)(2,1)S(1)}, bf16[256,256]{1,0:T(8,128)(2,1)}, u32[]{:S(2)}) copy-start(bf16[256,256]{1,0:T(8,128)(2,1)} %v_ref.2) | copy-start | bytes 393220
  2.9 0.9 %copy-start.6 = (bf16[256,256]{1,0:T(8,128)(2,1)S(1)}, bf16[256,256]{1,0:T(8,128)(2,1)}, u32[]{:S(2)}) copy-start(bf16[256,256]{1,0:T(8,128)(2,1)} %out_ref.2) | copy-start | bytes 393220
  12.9 6.9 %collective-permute-start = (bf16[2,128,256]{2,1,0:T(8,128)(2,1)S(1)}, bf16[2,128,256]{2,1,0:T(8,128)(2,1)S(1)}, u32[]{:S(2)}, u32[]{:S(2)}) collective-permute-start(bf16[2,128,256]{2,1,0:T(8,128)(2,1)S(1)} %get-tuple-element.14), channel_id=1, source_target_pairs={{0,16},{1,17},{2,18},{3,19},{4,20},{5,21},{6,22},{7,23},{8,24},{9,... | collective-permute-start | bytes 393224 | tf_op jit(solution)/shard_map/ppermute | solution.py:268
  15.9 7.8 %collective-permute-start.1 = (bf16[2,128,256]{2,1,0:T(8,128)(2,1)S(1)}, bf16[2,128,256]{2,1,0:T(8,128)(2,1)S(1)}, u32[]{:S(2)}, u32[]{:S(2)}) collective-permute-start(bf16[2,128,256]{2,1,0:T(8,128)(2,1)S(1)} %get-tuple-element.13), channel_id=1, source_target_pairs={{0,1},{1,0},{2,3},{3,2},{4,5},{5,4},{6,7},{7,6},{8,9},{9,8},{10,11... | collective-permute-start | bytes 393224 | tf_op jit(solution)/shard_map/ppermute | solution.py:268
  17.4 6.3 %collective-permute-start.2 = (bf16[2,128,256]{2,1,0:T(8,128)(2,1)S(1)}, bf16[2,128,256]{2,1,0:T(8,128)(2,1)S(1)}, u32[]{:S(2)}, u32[]{:S(2)}) collective-permute-start(bf16[2,128,256]{2,1,0:T(8,128)(2,1)S(1)} %get-tuple-element.12), channel_id=1, source_target_pairs={{0,17},{1,16},{2,19},{3,18},{4,21},{5,20},{6,23},{7,22},{8,25},{9,... | collective-permute-start | bytes 393224 | tf_op jit(solution)/shard_map/ppermute | solution.py:268
  23.7 2.1 %copy-start.4 = (bf16[256,512]{1,0:T(8,128)(2,1)S(1)}, bf16[256,512]{1,0:T(8,128)(2,1)}, u32[]{:S(2)}) copy-start(bf16[256,512]{1,0:T(8,128)(2,1)} %qk_ref.3) | copy-start | bytes 786436
  23.7 2.1 %copy-start.7 = (bf16[256,256]{1,0:T(8,128)(2,1)S(1)}, bf16[256,256]{1,0:T(8,128)(2,1)}, u32[]{:S(2)}) copy-start(bf16[256,256]{1,0:T(8,128)(2,1)} %v_ref.3) | copy-start | bytes 393220
  23.7 2.1 %copy-start.8 = (bf16[256,256]{1,0:T(8,128)(2,1)S(1)}, bf16[256,256]{1,0:T(8,128)(2,1)}, u32[]{:S(2)}) copy-start(bf16[256,256]{1,0:T(8,128)(2,1)} %out_ref.3) | copy-start | bytes 393220
  23.8 2.0 %collective-permute-start.3 = (bf16[2,2,2,128,256]{4,3,2,1,0:T(8,128)(2,1)S(1)}, bf16[2,2,2,128,256]{4,3,2,1,0:T(8,128)(2,1)S(1)}, u32[]{:S(2)}, u32[]{:S(2)}) collective-permute-start(bf16[2,2,2,128,256]{4,3,2,1,0:T(8,128)(2,1)S(1)} %bitcast.37), channel_id=1, source_target_pairs={{0,8},{8,0},{16,24},{24,16},{1,9},{9,1},{17,25},{25,17},{2,10},{10... | collective-permute-start | bytes 1572872 | tf_op jit(solution)/shard_map/ppermute | solution.py:271
  25.7 17.0 %copy-start.9 = (bf16[3,3,1024]{2,1,0:T(4,128)(2,1)S(1)}, bf16[3,3,1024]{2,1,0:T(4,128)(2,1)}, u32[]{:S(2)}) copy-start(bf16[3,3,1024]{2,1,0:T(4,128)(2,1)} %mix_ref.1) | copy-start | bytes 55300
  29.1 13.7 %copy-start = (bf16[256,1024]{1,0:T(8,128)(2,1)S(1)}, bf16[256,1024]{1,0:T(8,128)(2,1)}, u32[]{:S(2)}) copy-start(bf16[256,1024]{1,0:T(8,128)(2,1)} %up_ref.1) | copy-start | bytes 1572868
  29.1 13.6 %copy-start.1 = (bf16[1024,256]{1,0:T(8,128)(2,1)S(1)}, bf16[1024,256]{1,0:T(8,128)(2,1)}, u32[]{:S(2)}) copy-start(bf16[1024,256]{1,0:T(8,128)(2,1)} %down_ref.1) | copy-start | bytes 1572868
  29.2 9.5 %collective-permute-start.4 = (bf16[2,2,128,256]{3,2,1,0:T(8,128)(2,1)S(1)}, bf16[2,2,128,256]{3,2,1,0:T(8,128)(2,1)S(1)}, u32[]{:S(2)}, u32[]{:S(2)}) collective-permute-start(bf16[2,2,128,256]{3,2,1,0:T(8,128)(2,1)S(1)} %get-tuple-element.10), channel_id=1, source_target_pairs={{0,2},{1,3},{2,4},{3,5},{4,6},{5,7},{8,10},{9,11},{10,12},{11,13},... | collective-permute-start | bytes 786440 | tf_op jit(solution)/shard_map/ppermute | solution.py:273
  32.8 10.0 %collective-permute-start.5 = (bf16[2,2,128,256]{3,2,1,0:T(8,128)(2,1)S(1)}, bf16[2,2,128,256]{3,2,1,0:T(8,128)(2,1)S(1)}, u32[]{:S(2)}, u32[]{:S(2)}) collective-permute-start(bf16[2,2,128,256]{3,2,1,0:T(8,128)(2,1)S(1)} %get-tuple-element.9), channel_id=1, source_target_pairs={{2,0},{3,1},{4,2},{5,3},{6,4},{7,5},{10,8},{11,9},{12,10},{13,11},... | collective-permute-start | bytes 786440 | tf_op jit(solution)/shard_map/ppermute | solution.py:274
  50.3 6.1 %collective-permute-start.6 = (bf16[2,120,256]{2,1,0:T(8,128)(2,1)S(1)}, bf16[2,120,256]{2,1,0:T(8,128)(2,1)S(1)}, u32[]{:S(2)}, u32[]{:S(2)}) collective-permute-start(bf16[2,120,256]{2,1,0:T(8,128)(2,1)S(1)} %get-tuple-element.7), channel_id=1, source_target_pairs={{16,0},{17,1},{18,2},{19,3},{20,4},{21,5},{22,6},{23,7},{24,8},{25... | collective-permute-start | bytes 368648 | tf_op jit(solution)/shard_map/ppermute | solution.py:281
  51.6 6.9 %collective-permute-start.7 = (bf16[2,120,256]{2,1,0:T(8,128)(2,1)S(1)}, bf16[2,120,256]{2,1,0:T(8,128)(2,1)S(1)}, u32[]{:S(2)}, u32[]{:S(2)}) collective-permute-start(bf16[2,120,256]{2,1,0:T(8,128)(2,1)S(1)} %get-tuple-element.6), channel_id=1, source_target_pairs={{1,0},{0,1},{3,2},{2,3},{5,4},{4,5},{7,6},{6,7},{9,8},{8,9},{11,10... | collective-permute-start | bytes 368648 | tf_op jit(solution)/shard_map/ppermute | solution.py:281
  52.4 6.1 %collective-permute-start.8 = (bf16[2,120,256]{2,1,0:T(8,128)(2,1)S(1)}, bf16[2,120,256]{2,1,0:T(8,128)(2,1)S(1)}, u32[]{:S(2)}, u32[]{:S(2)}) collective-permute-start(bf16[2,120,256]{2,1,0:T(8,128)(2,1)S(1)} %get-tuple-element.5), channel_id=1, source_target_pairs={{17,0},{16,1},{19,2},{18,3},{21,4},{20,5},{23,6},{22,7},{25,8},{24... | collective-permute-start | bytes 368648 | tf_op jit(solution)/shard_map/ppermute | solution.py:281
  58.5 0.8 %copy-start.10 = (bf16[2,1,1,480,256]{4,3,2,1,0:T(8,128)(2,1)}, bf16[2,1,1,480,256]{4,3,2,1,0:T(8,128)(2,1)S(1)}, u32[]{:S(2)}) copy-start(bf16[2,1,1,480,256]{4,3,2,1,0:T(8,128)(2,1)S(1)} %bitcast_dynamic-update-slice_fusion.1) | copy-start | bytes 1474564

commit v2 on v1

v2 whole, which is shorter than its diff:
```python
import functools

import jax
import jax.numpy as jnp
from jax import lax
from jax.experimental import pallas as pl
from jax.experimental.pallas import tpu as pltpu
from jax.sharding import PartitionSpec as P

HEADS = 8
HEAD_DIM = 32
SCALE_LOG2 = HEAD_DIM ** (-0.5) * 1.4426950408889634
VMEM_LIMIT = 40 * 1024 * 1024


def round_up(value, unit):
    return (value + unit - 1) // unit * unit


def layer_norm(widened):
    centred = widened - jnp.mean(widened, axis=-1, keepdims=True)
    variance = jnp.mean(centred * centred, axis=-1, keepdims=True)
    return (centred * lax.rsqrt(variance + 1e-05)).astype(jnp.bfloat16)


def dot_dims(lhs, rhs, lhs_dim, rhs_dim):
    return lax.dot_general(
        lhs, rhs, (((lhs_dim,), (rhs_dim,)), ((), ())), preferred_element_type=jnp.float32
    )


def stereo_kernel(
    left, cols, window, video_hbm, qk_hbm, v_hbm, out_hbm, windows_ref, video_ref, qk_ref, v_ref, out_ref, sems
):
    copies = [
        pltpu.make_async_copy(source, target, sems.at[index])
        for index, (source, target) in enumerate(
            [(video_hbm, video_ref), (qk_hbm, qk_ref), (v_hbm, v_ref), (out_hbm, out_ref)]
        )
    ]
    for copy in copies:
        copy.start()
    for copy in copies:
        copy.wait()
    views = video_ref.shape[0]
    width, channels = video_ref.shape[-2:]
    rows = [video_ref[v].reshape(width, channels).astype(jnp.float32) for v in range(views)]
    normed = [layer_norm(view_rows) for view_rows in rows]
    queries = [dot_dims(n, qk_ref[:, :channels], 1, 0).astype(jnp.bfloat16) for n in normed]
    keys = [dot_dims(n, qk_ref[:, channels:], 1, 0).astype(jnp.bfloat16) for n in normed]
    values = [dot_dims(n, v_ref[...], 1, 0).astype(jnp.bfloat16) for n in normed]
    lane_head = lax.broadcasted_iota(jnp.int32, (width, 128), 1) // HEAD_DIM
    zero = jnp.zeros((), jnp.bfloat16)
    ones = jnp.ones((width, 128), jnp.bfloat16)
    owners = width // cols
    tail = round_up((owners - 1) * cols + window, 8) - width
    for view in range(views):
        groups = []
        for start in range(0, channels, 128):
            lanes = slice(start, start + 128)
            total = jnp.zeros((width, 128), jnp.float32)
            for head in range(128 // HEAD_DIM):
                mask = lane_head == head
                scores = dot_dims(
                    queries[view][:, lanes], jnp.where(mask, keys[1 - view][:, lanes], zero), 1, 1
                )
                top = jnp.max(scores, axis=1, keepdims=True)
                weights = jnp.exp2((scores - top) * SCALE_LOG2).astype(jnp.bfloat16)
                values_head = jnp.where(mask, values[1 - view][:, lanes], zero)
                mixed = dot_dims(weights, jnp.concatenate([values_head, ones], axis=1), 1, 0)
                total = total + mixed[:, :128] * (1.0 / mixed[:, 128:])
            groups.append(total.astype(jnp.bfloat16))
        update = dot_dims(jnp.concatenate(groups, axis=1), out_ref[...], 1, 0)
        section = rows[view] + update
        padded = jnp.concatenate([section, jnp.zeros((tail, channels), jnp.float32)], axis=0)
        padded = pltpu.roll(padded, left, 0)
        for owner in range(owners):
            windows_ref[view, owner] = padded[owner * cols : owner * cols + window].astype(
                jnp.bfloat16
            )


def stereo(video, owners, left, window, *weights):
    views = video.shape[0]
    width, channels = video.shape[-2:]
    operands = [pltpu.with_memory_space_constraint(array, pltpu.HBM) for array in (video, *weights)]
    return pl.pallas_call(
        functools.partial(stereo_kernel, left, width // owners, window),
        in_specs=[pl.BlockSpec(memory_space=pltpu.HBM)] * len(operands),
        out_specs=pl.BlockSpec(memory_space=pltpu.VMEM),
        out_shape=jax.ShapeDtypeStruct((views, owners, window, channels), jnp.bfloat16),
        scratch_shapes=[pltpu.VMEM(array.shape, array.dtype) for array in operands]
        + [pltpu.SemaphoreType.DMA((len(operands),))],
        compiler_params=pltpu.CompilerParams(vmem_limit_bytes=VMEM_LIMIT),
        cost_estimate=pl.CostEstimate(
            flops=2_400_000_000, bytes_accessed=2_000_000, transcendentals=4_000_000
        ),
        name="stereo",
    )(*operands)


def head_sum(product):
    channels, width = product.shape
    return jnp.sum(product.reshape(HEADS, HEAD_DIM, width), axis=1, keepdims=True)


def temporal_kernel(side_ref, own_ref, other_ref, qk_ref, v_ref, out_ref, section_ref):
    _, _, frames, window, channels = own_ref.shape
    side = side_ref[0]
    for slot in range(2):
        rows = own_ref[0, slot].reshape(frames * window, channels).astype(jnp.float32)
        rows_other = other_ref[0, slot].reshape(frames * window, channels).astype(jnp.float32)
        normed = layer_norm(rows)
        normed_all = jnp.concatenate([normed, layer_norm(rows_other)], axis=0)
        queries = dot_dims(qk_ref[:, :channels], normed, 0, 1).astype(jnp.bfloat16)
        keys = dot_dims(qk_ref[:, channels:], normed_all, 0, 1).astype(jnp.bfloat16)
        values = dot_dims(v_ref[...], normed_all, 0, 1).astype(jnp.bfloat16)
        attended = []
        for frame in range(frames):
            query = queries[:, frame * window : (frame + 1) * window].astype(jnp.float32)
            scores = [
                head_sum(
                    query * keys[:, other * window : (other + 1) * window].astype(jnp.float32)
                )
                for other in range(2 * frames)
            ]
            top = functools.reduce(jnp.maximum, scores)
            weights = [jnp.exp2((score - top) * SCALE_LOG2) for score in scores]
            inverse = 1.0 / functools.reduce(jnp.add, weights)
            mixed = jnp.zeros((HEADS, HEAD_DIM, window), jnp.float32)
            for other in range(2 * frames):
                value = values[:, other * window : (other + 1) * window].astype(jnp.float32)
                mixed = mixed + value.reshape(HEADS, HEAD_DIM, window) * (
                    weights[other] * inverse
                )
            attended.append(mixed.reshape(channels, window).astype(jnp.bfloat16))
        update = dot_dims(jnp.concatenate(attended, axis=1), out_ref[...], 0, 0)
        section = (rows + update).astype(jnp.bfloat16)
        section_ref[0, side ^ slot] = section.reshape(frames, window, channels)


def temporal(side, own, other, temporal_qk, temporal_v, temporal_out):
    block = pl.BlockSpec((1,) + own.shape[1:], lambda v, s: (v, 0, 0, 0, 0))
    whole = lambda array: pl.BlockSpec(array.shape, lambda v, s: (0,) * array.ndim)
    return pl.pallas_call(
        temporal_kernel,
        grid_spec=pltpu.PrefetchScalarGridSpec(
            num_scalar_prefetch=1,
            grid=(own.shape[0],),
            in_specs=[block, block, whole(temporal_qk), whole(temporal_v), whole(temporal_out)],
            out_specs=block,
        ),
        out_shape=jax.ShapeDtypeStruct(own.shape, jnp.bfloat16),
        compiler_params=pltpu.CompilerParams(vmem_limit_bytes=VMEM_LIMIT),
        cost_estimate=pl.CostEstimate(
            flops=own.shape[0] * 700_000_000, bytes_accessed=2_000_000, transcendentals=0
        ),
        name="temporal",
    )(side, own, other, temporal_qk, temporal_v, temporal_out)


def gelu(values):
    inner = values * (0.7978845608028654 + 0.035677408136300125 * (values * values))
    half = 0.5 * values
    return half + half * jnp.tanh(inner)


def mlp_mix(columns, window):
    return (
        pltpu.roll(columns[0], 1, 0) + columns[1] + pltpu.roll(columns[2], window - 1, 0)
    ).astype(jnp.bfloat16)


def inner_kernel(rows_ref, up_ref, mix_ref, down_ref, partial_ref):
    _, _, frames, window, channels = rows_ref.shape
    chunk = 256
    for frame in range(frames):
        rows = rows_ref[0, :, frame].reshape(2 * window, channels).astype(jnp.float32)
        normed = layer_norm(rows)
        total = rows
        for start in range(0, up_ref.shape[1], chunk):
            lanes = slice(start, start + chunk)
            hidden = gelu(dot_dims(normed, up_ref[:, lanes], 1, 0))
            hidden = hidden.astype(jnp.bfloat16).astype(jnp.float32)
            lines = [hidden[:window], hidden[window:]]
            taps = mix_ref[:, :, lanes].astype(jnp.float32)
            mixed = [
                mlp_mix(
                    [
                        lines[0] * taps[1 - line, b][None] + lines[1] * taps[2 - line, b][None]
                        for b in range(3)
                    ],
                    window,
                )
                for line in range(2)
            ]
            total = total + dot_dims(jnp.concatenate(mixed, axis=0), down_ref[lanes], 1, 0)
        partial_ref[0, :, frame] = total.reshape(2, window, channels)


def outer_kernel(
    left, side_ref, partial_ref, top_ref, bottom_ref, up_ref, mix_ref, down_ref, out_ref
):
    _, _, frames, window, channels = partial_ref.shape
    chunk = 256
    side = side_ref[0]
    for frame in range(frames):
        rows = jnp.concatenate([top_ref[0, frame], bottom_ref[0, frame]], axis=0)
        normed = layer_norm(rows.astype(jnp.float32))
        total = partial_ref[0, :, frame].reshape(2 * window, channels)
        for start in range(0, up_ref.shape[1], chunk):
            lanes = slice(start, start + chunk)
            hidden = gelu(dot_dims(normed, up_ref[:, lanes], 1, 0))
            hidden = hidden.astype(jnp.bfloat16).astype(jnp.float32)
            taps = mix_ref[:, :, lanes].astype(jnp.float32)
            mixed = [
                mlp_mix(
                    [
                        hidden[line * window : (line + 1) * window] * taps[2 * line, b][None]
                        for b in range(3)
                    ],
                    window,
                )
                for line in range(2)
            ]
            total = total + dot_dims(jnp.concatenate(mixed, axis=0), down_ref[lanes], 1, 0)
        for line in range(2):
            shifted = pltpu.roll(total[line * window : (line + 1) * window], window - left, 0)
            out_ref[0, side ^ line, frame] = shifted.astype(jnp.bfloat16)


def inner(rows, mlp_up, mix_kernel, mlp_down):
    block = pl.BlockSpec((1,) + rows.shape[1:], lambda v: (v, 0, 0, 0, 0))
    whole = lambda array: pl.BlockSpec(array.shape, lambda v: (0,) * array.ndim)
    return pl.pallas_call(
        inner_kernel,
        grid=(rows.shape[0],),
        in_specs=[block, whole(mlp_up), whole(mix_kernel), whole(mlp_down)],
        out_specs=block,
        out_shape=jax.ShapeDtypeStruct(rows.shape, jnp.float32),
        compiler_params=pltpu.CompilerParams(vmem_limit_bytes=VMEM_LIMIT),
        cost_estimate=pl.CostEstimate(
            flops=rows.shape[0] * 2_000_000_000, bytes_accessed=3_000_000, transcendentals=0
        ),
        name="inner",
    )(rows, mlp_up, mix_kernel, mlp_down)


def outer(side, left, partial, top, bottom, mlp_up, mix_kernel, mlp_down):
    block = pl.BlockSpec((1,) + partial.shape[1:], lambda v, s: (v, 0, 0, 0, 0))
    line = pl.BlockSpec((1,) + top.shape[1:], lambda v, s: (v, 0, 0, 0))
    whole = lambda array: pl.BlockSpec(array.shape, lambda v, s: (0,) * array.ndim)
    return pl.pallas_call(
        functools.partial(outer_kernel, left),
        grid_spec=pltpu.PrefetchScalarGridSpec(
            num_scalar_prefetch=1,
            grid=(partial.shape[0],),
            in_specs=[block, line, line, whole(mlp_up), whole(mix_kernel), whole(mlp_down)],
            out_specs=block,
        ),
        out_shape=jax.ShapeDtypeStruct(partial.shape, jnp.bfloat16),
        compiler_params=pltpu.CompilerParams(vmem_limit_bytes=VMEM_LIMIT),
        cost_estimate=pl.CostEstimate(
            flops=partial.shape[0] * 1_000_000_000, bytes_accessed=3_000_000, transcendentals=0
        ),
        name="outer",
    )(side, partial, top, bottom, mlp_up, mix_kernel, mlp_down)


def shards(
    video,
    stereo_qk,
    stereo_v,
    stereo_out,
    temporal_qk,
    temporal_v,
    temporal_out,
    mlp_up,
    mix_kernel,
    mlp_down,
):
    width, channels = video.shape[-2:]
    frame_size, rows_size = lax.axis_size("frame"), lax.axis_size("rows")
    pairs = frame_size // 2
    owners = frame_size
    cols = width // owners
    window = round_up(cols + 2, 16)
    left = (window - cols) // 2
    frame, row = lax.axis_index("frame"), lax.axis_index("rows")
    pair, side = frame // 2, row % 2
    side_arg = side.astype(jnp.int32)[None]
    both = ("frame", "rows")
    slots = [(s, p) for s in range(2) for p in range(pairs)]

    def owner_at(s, p):
        return lax.rem(pair + p, pairs) * 2 + (side ^ s)

    def chip_moves(s, p):
        return [
            (
                f * rows_size + r,
                ((f // 2 + p) % pairs * 2 + f % 2) * rows_size + (r ^ s),
            )
            for f in range(frame_size)
            for r in range(rows_size)
        ]

    siblings = [(f, f ^ 1) for f in range(frame_size)]
    upward = [(r, r + 2) for r in range(rows_size - 2)]
    downward = [(r + 2, r) for r in range(rows_size - 2)]
    windows = stereo(video, owners, left, window, stereo_qk, stereo_v, stereo_out)
    pieces = []
    for s, p in slots:
        piece = lax.dynamic_index_in_dim(windows, owner_at(s, p), 1, keepdims=False)
        if (s, p) != (0, 0):
            piece = lax.ppermute(piece, both, chip_moves(s, p))
        pieces.append(piece)
    own = jnp.stack(pieces, axis=1).reshape(-1, 2, pairs, window, channels)
    other = lax.ppermute(own, "frame", siblings)
    section = temporal(side_arg, own, other, temporal_qk, temporal_v, temporal_out)
    top = lax.ppermute(section[:, 1], "rows", upward)
    bottom = lax.ppermute(section[:, 0], "rows", downward)
    partial = inner(section, mlp_up, mix_kernel, mlp_down)
    result = outer(side_arg, left, partial, top, bottom, mlp_up, mix_kernel, mlp_down)
    output = jnp.zeros((video.shape[0], width, channels), jnp.bfloat16)
    for s, p in slots:
        piece = result[:, s, p, :cols]
        if (s, p) != (0, 0):
            back = [(j, i) for i, j in chip_moves(s, p)]
            piece = lax.ppermute(piece, both, back)
        output = lax.dynamic_update_slice(output, piece, (0, owner_at(s, p) * cols, 0))
    return output.reshape(video.shape)


def solution(mesh):
    in_specs = (P(None, "frame", "rows", None, None), P(), P(), P(), P(), P(), P(), P(), P(), P())
    out_specs = P(None, "frame", "rows", None, None)
    return jax.shard_map(shards, mesh=mesh, in_specs=in_specs, out_specs=out_specs, check_vma=False)
```

time: 60.2 us -> 50.7 us (0.84)
  waiting for transfers between devices: 21.3 us -> 16.4 us
  local copies, waits for them, and re-layouts: 5.42 us -> 1.63 us
  Pallas kernels: 19.8 us -> 19 us
    ppermute x1, waiting for transfers between devices: 4.52 us -> 0.01 us  [shards(): top = lax.ppermute(section[:, 1], 'rows', upward)]
    unnamed x22 -> x14, local copies, waits for them, and re-layouts: 4.58 us -> 0.79 us
    pallas_call x1, Pallas kernels: 9.02 us -> 6.92 us  [stereo(): pl.pallas_call(functools.partial(stereo_kernel, left, width // owners, wi...]
    pallas_call x1 -> x2, Pallas kernels: 7.45 us -> 8.77 us  [the longest x1 4.76 us: inner(): pl.pallas_call(inner_kernel, grid=(rows.shape[0],), in_specs=[block, whol...]
  transfers between devices with their start and end apart: 9 -> 9, of which waited for: 7 -> 6; matrix products, arithmetic and copies ran while one was open for 0% -> 0% of each run, Pallas kernels for 0% -> 9%
where the time goes in v2:
time: 50.7 us; the launch traced here: 50.6 us
  Pallas kernels  19 us (37%)
  waiting for transfers between devices  16.4 us (32%)
  starting transfers between devices  13.3 us (26%)
  local copies, waits for them, and re-layouts  1.63 us (3%)
    pallas_call x1, Pallas kernels, stereo(): pl.pallas_call(functools.partial(stereo_kernel, left, width // owners, wi...  6.92 us
    ppermute x3, waiting for transfers between devices, shards(): piece = lax.ppermute(piece, both, chip_moves(s, p))  6.24 us
    pallas_call x1, Pallas kernels, inner(): pl.pallas_call(inner_kernel, grid=(rows.shape[0],), in_specs=[block, whol...  4.76 us
    ppermute x3, waiting for transfers between devices, shards(): piece = lax.ppermute(piece, both, back)  4.57 us
    ppermute x3, starting transfers between devices, shards(): piece = lax.ppermute(piece, both, chip_moves(s, p))  4.54 us
    pallas_call x1, Pallas kernels, outer(): pl.pallas_call(functools.partial(outer_kernel, left), grid_spec=pltpu.Pre...  4.01 us
    ppermute x1, waiting for transfers between devices, shards(): bottom = lax.ppermute(section[:, 0], 'rows', downward)  3.67 us
    ppermute x1, starting transfers between devices, shards(): top = lax.ppermute(section[:, 1], 'rows', upward)  3.62 us
  transfers between devices with their start and end apart: 9, of which 6 were waited for; matrix products, arithmetic and copies ran while one was open for 0% of the time, Pallas kernels for 9%

profile of v2, /device:TPU:0, one launch (start us, length us, event | category | flops | bytes accessed | tf_op | source)
XLA Modules:
  0.0 50.6 jit_solution(1709921374274868068)
XLA Ops:
  0.0 6.9 %stereo.1 = bf16[2,4,128,256]{3,2,1,0:T(8,128)(2,1)S(1)} custom-call(bf16[2,1,1,480,256]{4,3,2,1,0:T(8,128)(2,1)} %video_hbm.1, bf16[256,512]{1,0:T(8,128)(2,1)} %qk_hbm.1, bf16[256,256]{1,0:T(8,128)(2,1)} %v_hbm.1, bf16[256,256]{1,0:T(8,128)(2,1)} %out_hbm.1), custom_call_target="tpu_custom_call" | custom-call | flops 2400000000 | bytes 2000000 | tf_op jit(solution)/shard_map/stereo/pallas_call | solution.py:87
  7.0 3.0 %collective-permute-start = (bf16[2,128,256]{2,1,0:T(8,128)(2,1)S(1)}, bf16[2,128,256]{2,1,0:T(8,128)(2,1)S(1)}, u32[]{:S(2)}, u32[]{:S(2)}) collective-permute-start(bf16[2,128,256]{2,1,0:T(8,128)(2,1)S(1)} %get-tuple-element.14), channel_id=1, source_target_pairs={{0,16},{1,17},{2,18},{3,19},{4,20},{5,21},{6,22},{7,23},{8,24},{9,... | collective-permute-start | bytes 393224 | tf_op jit(solution)/shard_map/ppermute | solution.py:316
  10.0 1.5 %collective-permute-start.1 = (bf16[2,128,256]{2,1,0:T(8,128)(2,1)S(1)}, bf16[2,128,256]{2,1,0:T(8,128)(2,1)S(1)}, u32[]{:S(2)}, u32[]{:S(2)}) collective-permute-start(bf16[2,128,256]{2,1,0:T(8,128)(2,1)S(1)} %get-tuple-element.13), channel_id=1, source_target_pairs={{0,1},{1,0},{2,3},{3,2},{4,5},{5,4},{6,7},{7,6},{8,9},{9,8},{10,11... | collective-permute-start | bytes 393224 | tf_op jit(solution)/shard_map/ppermute | solution.py:316
  11.5 0.0 collective-permute-start.2
  11.5 2.4 %collective-permute-done = bf16[2,128,256]{2,1,0:T(8,128)(2,1)S(1)} collective-permute-done((bf16[2,128,256]{2,1,0:T(8,128)(2,1)S(1)}, bf16[2,128,256]{2,1,0:T(8,128)(2,1)S(1)}, u32[]{:S(2)}, u32[]{:S(2)}) %collective-permute-start) | collective-permute-done | bytes 131104 | tf_op jit(solution)/shard_map/ppermute | solution.py:316
  13.9 3.9 %collective-permute-done.1 = bf16[2,128,256]{2,1,0:T(8,128)(2,1)S(1)} collective-permute-done((bf16[2,128,256]{2,1,0:T(8,128)(2,1)S(1)}, bf16[2,128,256]{2,1,0:T(8,128)(2,1)S(1)}, u32[]{:S(2)}, u32[]{:S(2)}) %collective-permute-start.1) | collective-permute-done | bytes 131104 | tf_op jit(solution)/shard_map/ppermute | solution.py:316
  17.8 0.0 collective-permute-done.2
  17.8 0.1 pad_maximum_fusion
  17.9 0.1 collective-permute-start.3
  17.9 1.9 %collective-permute-done.3.other_ref = bf16[2,2,2,128,256]{4,3,2,1,0:T(8,128)(2,1)S(1)} collective-permute-done((bf16[2,2,2,128,256]{4,3,2,1,0:T(8,128)(2,1)S(1)}, bf16[2,2,2,128,256]{4,3,2,1,0:T(8,128)(2,1)S(1)}, u32[]{:S(2)}, u32[]{:S(2)}) %collective-permute-start.3) | collective-permute-done | bytes 524320 | tf_op jit(solution)/shard_map/ppermute | solution.py:319
  19.8 0.0 copy-done.2
  19.8 0.0 copy-done.3
  19.8 0.0 copy-done.4
  19.8 0.0 copy-start.5
  19.9 3.3 %temporal.1.rows_ref = bf16[2,2,2,128,256]{4,3,2,1,0:T(8,128)(2,1)S(1)} custom-call(s32[1]{0:T(128)} %bitcast.side_ref, bf16[2,2,2,128,256]{4,3,2,1,0:T(8,128)(2,1)S(1)} %bitcast.38, bf16[2,2,2,128,256]{4,3,2,1,0:T(8,128)(2,1)S(1)} %collective-permute-done.3.other_ref, bf16[256,512]{1,0:T(8,128)(2,1)S(1)} %copy-done.2, bf16[256,256]{1,0:T(8,128)(2,1)S(1)} %copy-done.3, ...), custom_call_target="tpu_custom_call" | custom-call | flops 1400000000 | bytes 2000000 | tf_op jit(solution)/shard_map/temporal/pallas_call | solution.py:145
  23.2 0.0 copy-start
  23.2 0.0 copy-start.1
  23.3 3.6 %collective-permute-start.4 = (bf16[2,2,128,256]{3,2,1,0:T(8,128)(2,1)S(1)}, bf16[2,2,128,256]{3,2,1,0:T(8,128)(2,1)S(1)}, u32[]{:S(2)}, u32[]{:S(2)}) collective-permute-start(bf16[2,2,128,256]{3,2,1,0:T(8,128)(2,1)S(1)} %get-tuple-element.10), channel_id=1, source_target_pairs={{0,2},{1,3},{2,4},{3,5},{4,6},{5,7},{8,10},{9,11},{10,12},{11,13},... | collective-permute-start | bytes 786440 | tf_op jit(solution)/shard_map/ppermute | solution.py:321
  26.9 1.5 %collective-permute-start.5 = (bf16[2,2,128,256]{3,2,1,0:T(8,128)(2,1)S(1)}, bf16[2,2,128,256]{3,2,1,0:T(8,128)(2,1)S(1)}, u32[]{:S(2)}, u32[]{:S(2)}) collective-permute-start(bf16[2,2,128,256]{3,2,1,0:T(8,128)(2,1)S(1)} %get-tuple-element.9), channel_id=1, source_target_pairs={{2,0},{3,1},{4,2},{5,3},{6,4},{7,5},{10,8},{11,9},{12,10},{13,11},... | collective-permute-start | bytes 786440 | tf_op jit(solution)/shard_map/ppermute | solution.py:322
  28.4 4.8 %inner.1.partial_ref = f32[2,2,2,128,256]{4,3,2,1,0:T(8,128)S(1)} custom-call(bf16[2,2,2,128,256]{4,3,2,1,0:T(8,128)(2,1)S(1)} %temporal.1.rows_ref, bf16[256,1024]{1,0:T(8,128)(2,1)S(1)} %copy-done, bf16[3,3,1024]{2,1,0:T(4,128)(2,1)S(1)} %copy-done.5, bf16[1024,256]{1,0:T(8,128)(2,1)S(1)} %copy-done.1), custom_call_target="tpu_custom_call" | custom-call | flops 4000000000 | bytes 3000000 | tf_op jit(solution)/shard_map/inner/pallas_call | solution.py:235
  33.2 0.0 collective-permute-done.4.top_ref
  33.2 3.7 %collective-permute-done.5.bottom_ref = bf16[2,2,128,256]{3,2,1,0:T(8,128)(2,1)S(1)} collective-permute-done((bf16[2,2,128,256]{3,2,1,0:T(8,128)(2,1)S(1)}, bf16[2,2,128,256]{3,2,1,0:T(8,128)(2,1)S(1)}, u32[]{:S(2)}, u32[]{:S(2)}) %collective-permute-start.5) | collective-permute-done | bytes 262176 | tf_op jit(solution)/shard_map/ppermute | solution.py:322
  36.9 4.0 %outer.1 = bf16[2,2,2,128,256]{4,3,2,1,0:T(8,128)(2,1)S(1)} custom-call(s32[1]{0:T(128)} %bitcast.side_ref, f32[2,2,2,128,256]{4,3,2,1,0:T(8,128)S(1)} %inner.1.partial_ref, bf16[2,2,128,256]{3,2,1,0:T(8,128)(2,1)S(1)} %collective-permute-done.4.top_ref, bf16[2,2,128,256]{3,2,1,0:T(8,128)(2,1)S(1)} %collective-permute-done.5.bottom_ref, ...), custom_call_target="tpu_custom_call" | custom-call | flops 2000000000 | bytes 3000000 | tf_op jit(solution)/shard_map/outer/pallas_call | solution.py:253
  41.0 1.3 %collective-permute-start.6 = (bf16[2,120,256]{2,1,0:T(8,128)(2,1)S(1)}, bf16[2,120,256]{2,1,0:T(8,128)(2,1)S(1)}, u32[]{:S(2)}, u32[]{:S(2)}) collective-permute-start(bf16[2,120,256]{2,1,0:T(8,128)(2,1)S(1)} %get-tuple-element.7), channel_id=1, source_target_pairs={{16,0},{17,1},{18,2},{19,3},{20,4},{21,5},{22,6},{23,7},{24,8},{25... | collective-permute-start | bytes 368648 | tf_op jit(solution)/shard_map/ppermute | solution.py:330
  42.2 0.8 %collective-permute-start.7 = (bf16[2,120,256]{2,1,0:T(8,128)(2,1)S(1)}, bf16[2,120,256]{2,1,0:T(8,128)(2,1)S(1)}, u32[]{:S(2)}, u32[]{:S(2)}) collective-permute-start(bf16[2,120,256]{2,1,0:T(8,128)(2,1)S(1)} %get-tuple-element.6), channel_id=1, source_target_pairs={{1,0},{0,1},{3,2},{2,3},{5,4},{4,5},{7,6},{6,7},{9,8},{8,9},{11,10... | collective-permute-start | bytes 368648 | tf_op jit(solution)/shard_map/ppermute | solution.py:330
  43.1 1.4 %collective-permute-start.8 = (bf16[2,120,256]{2,1,0:T(8,128)(2,1)S(1)}, bf16[2,120,256]{2,1,0:T(8,128)(2,1)S(1)}, u32[]{:S(2)}, u32[]{:S(2)}) collective-permute-start(bf16[2,120,256]{2,1,0:T(8,128)(2,1)S(1)} %get-tuple-element.5), channel_id=1, source_target_pairs={{17,0},{16,1},{19,2},{18,3},{21,4},{20,5},{23,6},{22,7},{25,8},{24... | collective-permute-start | bytes 368648 | tf_op jit(solution)/shard_map/ppermute | solution.py:330
  44.5 2.6 %collective-permute-done.6 = bf16[2,120,256]{2,1,0:T(8,128)(2,1)S(1)} collective-permute-done((bf16[2,120,256]{2,1,0:T(8,128)(2,1)S(1)}, bf16[2,120,256]{2,1,0:T(8,128)(2,1)S(1)}, u32[]{:S(2)}, u32[]{:S(2)}) %collective-permute-start.6) | collective-permute-done | bytes 122912 | tf_op jit(solution)/shard_map/ppermute | solution.py:330
  47.1 2.0 %collective-permute-done.7 = bf16[2,120,256]{2,1,0:T(8,128)(2,1)S(1)} collective-permute-done((bf16[2,120,256]{2,1,0:T(8,128)(2,1)S(1)}, bf16[2,120,256]{2,1,0:T(8,128)(2,1)S(1)}, u32[]{:S(2)}, u32[]{:S(2)}) %collective-permute-start.7) | collective-permute-done | bytes 122912 | tf_op jit(solution)/shard_map/ppermute | solution.py:330
  49.1 0.0 copy-start.6
  49.1 0.0 collective-permute-done.8
  49.1 0.8 %copy-done.6 = bf16[2,1,1,480,256]{4,3,2,1,0:T(8,128)(2,1)} copy-done((bf16[2,1,1,480,256]{4,3,2,1,0:T(8,128)(2,1)}, bf16[2,1,1,480,256]{4,3,2,1,0:T(8,128)(2,1)S(1)}, u32[]{:S(2)}) %copy-start.6) | copy-done | bytes 491544
  49.9 0.7 %bitcast_dynamic-update-slice_fusion = bf16[2,1,1,480,256]{4,3,2,1,0:T(8,128)(2,1)} fusion(bf16[2,1,1,480,256]{4,3,2,1,0:T(8,128)(2,1)} %copy-done.6, s32[]{:T(128)S(6)} %select_n.45, bf16[2,120,256]{2,1,0:T(8,128)(2,1)S(1)} %collective-permute-done.8), kind=kLoop, calls=%fused_computation.10 | loop fusion | bytes 245764 | tf_op jit(solution)/shard_map/dynamic_update_slice | solution.py:331
  (12 shorter events, 0.2 us)
Async XLA Ops:
  7.0 6.9 %collective-permute-start = (bf16[2,128,256]{2,1,0:T(8,128)(2,1)S(1)}, bf16[2,128,256]{2,1,0:T(8,128)(2,1)S(1)}, u32[]{:S(2)}, u32[]{:S(2)}) collective-permute-start(bf16[2,128,256]{2,1,0:T(8,128)(2,1)S(1)} %get-tuple-element.14), channel_id=1, source_target_pairs={{0,16},{1,17},{2,18},{3,19},{4,20},{5,21},{6,22},{7,23},{8,24},{9,... | collective-permute-start | bytes 393224 | tf_op jit(solution)/shard_map/ppermute | solution.py:316
  10.0 7.8 %collective-permute-start.1 = (bf16[2,128,256]{2,1,0:T(8,128)(2,1)S(1)}, bf16[2,128,256]{2,1,0:T(8,128)(2,1)S(1)}, u32[]{:S(2)}, u32[]{:S(2)}) collective-permute-start(bf16[2,128,256]{2,1,0:T(8,128)(2,1)S(1)} %get-tuple-element.13), channel_id=1, source_target_pairs={{0,1},{1,0},{2,3},{3,2},{4,5},{5,4},{6,7},{7,6},{8,9},{9,8},{10,11... | collective-permute-start | bytes 393224 | tf_op jit(solution)/shard_map/ppermute | solution.py:316
  11.5 6.3 %collective-permute-start.2 = (bf16[2,128,256]{2,1,0:T(8,128)(2,1)S(1)}, bf16[2,128,256]{2,1,0:T(8,128)(2,1)S(1)}, u32[]{:S(2)}, u32[]{:S(2)}) collective-permute-start(bf16[2,128,256]{2,1,0:T(8,128)(2,1)S(1)} %get-tuple-element.12), channel_id=1, source_target_pairs={{0,17},{1,16},{2,19},{3,18},{4,21},{5,20},{6,23},{7,22},{8,25},{9,... | collective-permute-start | bytes 393224 | tf_op jit(solution)/shard_map/ppermute | solution.py:316
  17.8 2.1 %copy-start.2 = (bf16[256,512]{1,0:T(8,128)(2,1)S(1)}, bf16[256,512]{1,0:T(8,128)(2,1)}, u32[]{:S(2)}) copy-start(bf16[256,512]{1,0:T(8,128)(2,1)} %qk_ref.1) | copy-start | bytes 786436
  17.8 2.1 %copy-start.3 = (bf16[256,256]{1,0:T(8,128)(2,1)S(1)}, bf16[256,256]{1,0:T(8,128)(2,1)}, u32[]{:S(2)}) copy-start(bf16[256,256]{1,0:T(8,128)(2,1)} %v_ref.1) | copy-start | bytes 393220
  17.8 2.1 %copy-start.4 = (bf16[256,256]{1,0:T(8,128)(2,1)S(1)}, bf16[256,256]{1,0:T(8,128)(2,1)}, u32[]{:S(2)}) copy-start(bf16[256,256]{1,0:T(8,128)(2,1)} %out_ref.1) | copy-start | bytes 393220
  17.9 2.0 %collective-permute-start.3 = (bf16[2,2,2,128,256]{4,3,2,1,0:T(8,128)(2,1)S(1)}, bf16[2,2,2,128,256]{4,3,2,1,0:T(8,128)(2,1)S(1)}, u32[]{:S(2)}, u32[]{:S(2)}) collective-permute-start(bf16[2,2,2,128,256]{4,3,2,1,0:T(8,128)(2,1)S(1)} %bitcast.37), channel_id=1, source_target_pairs={{0,8},{8,0},{16,24},{24,16},{1,9},{9,1},{17,25},{25,17},{2,10},{10... | collective-permute-start | bytes 1572872 | tf_op jit(solution)/shard_map/ppermute | solution.py:319
  19.8 8.5 %copy-start.5 = (bf16[3,3,1024]{2,1,0:T(4,128)(2,1)S(1)}, bf16[3,3,1024]{2,1,0:T(4,128)(2,1)}, u32[]{:S(2)}) copy-start(bf16[3,3,1024]{2,1,0:T(4,128)(2,1)} %mix_ref.3) | copy-start | bytes 55300
  23.2 5.2 %copy-start = (bf16[256,1024]{1,0:T(8,128)(2,1)S(1)}, bf16[256,1024]{1,0:T(8,128)(2,1)}, u32[]{:S(2)}) copy-start(bf16[256,1024]{1,0:T(8,128)(2,1)} %up_ref.3) | copy-start | bytes 1572868
  23.2 5.2 %copy-start.1 = (bf16[1024,256]{1,0:T(8,128)(2,1)S(1)}, bf16[1024,256]{1,0:T(8,128)(2,1)}, u32[]{:S(2)}) copy-start(bf16[1024,256]{1,0:T(8,128)(2,1)} %down_ref.3) | copy-start | bytes 1572868
  23.3 9.9 %collective-permute-start.4 = (bf16[2,2,128,256]{3,2,1,0:T(8,128)(2,1)S(1)}, bf16[2,2,128,256]{3,2,1,0:T(8,128)(2,1)S(1)}, u32[]{:S(2)}, u32[]{:S(2)}) collective-permute-start(bf16[2,2,128,256]{3,2,1,0:T(8,128)(2,1)S(1)} %get-tuple-element.10), channel_id=1, source_target_pairs={{0,2},{1,3},{2,4},{3,5},{4,6},{5,7},{8,10},{9,11},{10,12},{11,13},... | collective-permute-start | bytes 786440 | tf_op jit(solution)/shard_map/ppermute | solution.py:321
  26.9 10.0 %collective-permute-start.5 = (bf16[2,2,128,256]{3,2,1,0:T(8,128)(2,1)S(1)}, bf16[2,2,128,256]{3,2,1,0:T(8,128)(2,1)S(1)}, u32[]{:S(2)}, u32[]{:S(2)}) collective-permute-start(bf16[2,2,128,256]{3,2,1,0:T(8,128)(2,1)S(1)} %get-tuple-element.9), channel_id=1, source_target_pairs={{2,0},{3,1},{4,2},{5,3},{6,4},{7,5},{10,8},{11,9},{12,10},{13,11},... | collective-permute-start | bytes 786440 | tf_op jit(solution)/shard_map/ppermute | solution.py:322
  41.0 6.1 %collective-permute-start.6 = (bf16[2,120,256]{2,1,0:T(8,128)(2,1)S(1)}, bf16[2,120,256]{2,1,0:T(8,128)(2,1)S(1)}, u32[]{:S(2)}, u32[]{:S(2)}) collective-permute-start(bf16[2,120,256]{2,1,0:T(8,128)(2,1)S(1)} %get-tuple-element.7), channel_id=1, source_target_pairs={{16,0},{17,1},{18,2},{19,3},{20,4},{21,5},{22,6},{23,7},{24,8},{25... | collective-permute-start | bytes 368648 | tf_op jit(solution)/shard_map/ppermute | solution.py:330
  42.2 6.9 %collective-permute-start.7 = (bf16[2,120,256]{2,1,0:T(8,128)(2,1)S(1)}, bf16[2,120,256]{2,1,0:T(8,128)(2,1)S(1)}, u32[]{:S(2)}, u32[]{:S(2)}) collective-permute-start(bf16[2,120,256]{2,1,0:T(8,128)(2,1)S(1)} %get-tuple-element.6), channel_id=1, source_target_pairs={{1,0},{0,1},{3,2},{2,3},{5,4},{4,5},{7,6},{6,7},{9,8},{8,9},{11,10... | collective-permute-start | bytes 368648 | tf_op jit(solution)/shard_map/ppermute | solution.py:330
  43.1 6.1 %collective-permute-start.8 = (bf16[2,120,256]{2,1,0:T(8,128)(2,1)S(1)}, bf16[2,120,256]{2,1,0:T(8,128)(2,1)S(1)}, u32[]{:S(2)}, u32[]{:S(2)}) collective-permute-start(bf16[2,120,256]{2,1,0:T(8,128)(2,1)S(1)} %get-tuple-element.5), channel_id=1, source_target_pairs={{17,0},{16,1},{19,2},{18,3},{21,4},{20,5},{23,6},{22,7},{25,8},{24... | collective-permute-start | bytes 368648 | tf_op jit(solution)/shard_map/ppermute | solution.py:330
  49.1 0.8 %copy-start.6 = (bf16[2,1,1,480,256]{4,3,2,1,0:T(8,128)(2,1)}, bf16[2,1,1,480,256]{4,3,2,1,0:T(8,128)(2,1)S(1)}, u32[]{:S(2)}) copy-start(bf16[2,1,1,480,256]{4,3,2,1,0:T(8,128)(2,1)S(1)} %bitcast_dynamic-update-slice_fusion.1) | copy-start | bytes 1474564

commit v3 on v1

v3 whole, which is shorter than its diff:
```python
import functools

import jax
import jax.numpy as jnp
from jax import lax
from jax.experimental import pallas as pl
from jax.experimental.pallas import tpu as pltpu
from jax.sharding import PartitionSpec as P

HEADS = 8
HEAD_DIM = 32
SCALE_LOG2 = HEAD_DIM ** (-0.5) * 1.4426950408889634
VMEM_LIMIT = 40 * 1024 * 1024


def round_up(value, unit):
    return (value + unit - 1) // unit * unit


def layer_norm(widened):
    centred = widened - jnp.mean(widened, axis=-1, keepdims=True)
    variance = jnp.mean(centred * centred, axis=-1, keepdims=True)
    return (centred * lax.rsqrt(variance + 1e-05)).astype(jnp.bfloat16)


def dot_dims(lhs, rhs, lhs_dim, rhs_dim):
    return lax.dot_general(
        lhs, rhs, (((lhs_dim,), (rhs_dim,)), ((), ())), preferred_element_type=jnp.float32
    )


def stereo_rows(left, cols, rows, rows_other, qk_ref, v_ref, out_ref, windows_ref):
    width, channels = rows.shape
    normed = layer_norm(rows)
    normed_other = layer_norm(rows_other)
    queries = dot_dims(normed, qk_ref[:, :channels], 1, 0).astype(jnp.bfloat16)
    keys = dot_dims(normed_other, qk_ref[:, channels:], 1, 0).astype(jnp.bfloat16)
    values = dot_dims(normed_other, v_ref[...], 1, 0).astype(jnp.bfloat16)
    lane_head = lax.broadcasted_iota(jnp.int32, (width, 128), 1) // HEAD_DIM
    zero = jnp.zeros((), jnp.bfloat16)
    ones = jnp.ones((width, 128), jnp.bfloat16)
    owners, window, _ = windows_ref.shape
    tail = round_up((owners - 1) * cols + window, 8) - width
    groups = []
    for start in range(0, channels, 128):
        lanes = slice(start, start + 128)
        total = jnp.zeros((width, 128), jnp.float32)
        for head in range(128 // HEAD_DIM):
            mask = lane_head == head
            scores = dot_dims(queries[:, lanes], jnp.where(mask, keys[:, lanes], zero), 1, 1)
            top = jnp.max(scores, axis=1, keepdims=True)
            weights = jnp.exp2((scores - top) * SCALE_LOG2).astype(jnp.bfloat16)
            values_head = jnp.where(mask, values[:, lanes], zero)
            mixed = dot_dims(weights, jnp.concatenate([values_head, ones], axis=1), 1, 0)
            total = total + mixed[:, :128] * (1.0 / mixed[:, 128:])
        groups.append(total.astype(jnp.bfloat16))
    update = dot_dims(jnp.concatenate(groups, axis=1), out_ref[...], 1, 0)
    padded = jnp.concatenate([rows + update, jnp.zeros((tail, channels), jnp.float32)], axis=0)
    padded = pltpu.roll(padded, left, 0)
    for owner in range(owners):
        windows_ref[owner] = padded[owner * cols : owner * cols + window].astype(jnp.bfloat16)


def first_kernel(left, cols, core_ref, *refs):
    count = (len(refs) - 2) // 2
    sources, windows_ref = refs[:count], refs[count]
    targets, sems = (refs[-2], *refs[count + 1 : -2]), refs[-1]
    copies = [
        pltpu.make_async_copy(source, target, sems.at[index])
        for index, (source, target) in enumerate(zip(sources, targets))
    ]
    for copy in copies:
        copy.start()
    for copy in copies[:4]:
        copy.wait()
    second_kernel(left, cols, core_ref, *targets[:4], windows_ref)
    for copy in copies[4:]:
        copy.wait()


def second_kernel(left, cols, core_ref, video_ref, qk_ref, v_ref, out_ref, windows_ref):
    core = core_ref[0]
    width, channels = video_ref.shape[-2:]
    rows = video_ref[core].reshape(width, channels).astype(jnp.float32)
    rows_other = video_ref[1 - core].reshape(width, channels).astype(jnp.float32)
    stereo_rows(left, cols, rows, rows_other, qk_ref, v_ref, out_ref, windows_ref)


def first_stereo(core, video, owners, left, window, *weights):
    width, channels = video.shape[-2:]
    operands = [pltpu.with_memory_space_constraint(array, pltpu.HBM) for array in (video, *weights)]
    vmem = pl.BlockSpec(memory_space=pltpu.VMEM)
    return pl.pallas_call(
        functools.partial(first_kernel, left, width // owners),
        in_specs=[pl.BlockSpec(memory_space=pltpu.SMEM)]
        + [pl.BlockSpec(memory_space=pltpu.HBM)] * len(operands),
        out_specs=[vmem] * len(operands),
        out_shape=[jax.ShapeDtypeStruct((owners, window, channels), jnp.bfloat16)]
        + [jax.ShapeDtypeStruct(array.shape, array.dtype) for array in weights],
        scratch_shapes=[
            pltpu.VMEM(video.shape, video.dtype),
            pltpu.SemaphoreType.DMA((len(operands),)),
        ],
        compiler_params=pltpu.CompilerParams(vmem_limit_bytes=VMEM_LIMIT),
        cost_estimate=pl.CostEstimate(
            flops=2_400_000_000, bytes_accessed=2_000_000, transcendentals=2_000_000
        ),
        name="stereo",
    )(core, *operands)


def head_sum(product):
    channels, width = product.shape
    return jnp.sum(product.reshape(HEADS, HEAD_DIM, width), axis=1, keepdims=True)


def temporal_kernel(pairs, *refs):
    pieces, (qk_ref, v_ref, out_ref, section_ref) = refs[:pairs], refs[pairs:]
    _, pair_size, window, channels = section_ref.shape
    frames = pairs * pair_size
    rows = jnp.concatenate(
        [piece[...].reshape(pair_size * window, channels) for piece in pieces], axis=0
    ).astype(jnp.float32)
    normed = layer_norm(rows)
    queries = dot_dims(qk_ref[:, :channels], normed, 0, 1).astype(jnp.bfloat16)
    keys = dot_dims(qk_ref[:, channels:], normed, 0, 1).astype(jnp.bfloat16)
    values = dot_dims(v_ref[...], normed, 0, 1).astype(jnp.bfloat16)
    attended = []
    for frame in range(frames):
        query = queries[:, frame * window : (frame + 1) * window].astype(jnp.float32)
        scores = [
            head_sum(query * keys[:, other * window : (other + 1) * window].astype(jnp.float32))
            for other in range(frames)
        ]
        top = functools.reduce(jnp.maximum, scores)
        weights = [jnp.exp2((score - top) * SCALE_LOG2) for score in scores]
        inverse = 1.0 / functools.reduce(jnp.add, weights)
        mixed = jnp.zeros((HEADS, HEAD_DIM, window), jnp.float32)
        for other in range(frames):
            value = values[:, other * window : (other + 1) * window].astype(jnp.float32)
            mixed = mixed + value.reshape(HEADS, HEAD_DIM, window) * (weights[other] * inverse)
        attended.append(mixed.reshape(channels, window).astype(jnp.bfloat16))
    update = dot_dims(jnp.concatenate(attended, axis=1), out_ref[...], 0, 0)
    section_ref[...] = (rows + update).astype(jnp.bfloat16).reshape(section_ref.shape)


def kernel_call(body, name, flops, out_shape, scalars, *operands):
    return pl.pallas_call(
        body,
        in_specs=[pl.BlockSpec(memory_space=pltpu.SMEM)] * len(scalars)
        + [pl.BlockSpec(memory_space=pltpu.VMEM)] * len(operands),
        out_specs=jax.tree.map(lambda _: pl.BlockSpec(memory_space=pltpu.VMEM), out_shape),
        out_shape=out_shape,
        compiler_params=pltpu.CompilerParams(vmem_limit_bytes=VMEM_LIMIT),
        cost_estimate=pl.CostEstimate(flops=flops, bytes_accessed=3_000_000, transcendentals=0),
        name=name,
    )(*scalars, *operands)


def gelu(values):
    inner = values * (0.7978845608028654 + 0.035677408136300125 * (values * values))
    half = 0.5 * values
    return half + half * jnp.tanh(inner)


def mlp_mix(columns, window):
    return (
        pltpu.roll(columns[0], 1, 0) + columns[1] + pltpu.roll(columns[2], window - 1, 0)
    ).astype(jnp.bfloat16)


CHUNK = 256


def mlp_hidden(normed, up_ref, start):
    hidden = gelu(dot_dims(normed, up_ref[:, start : start + CHUNK], 1, 0))
    return hidden.astype(jnp.bfloat16).astype(jnp.float32)


def inner_kernel(side_ref, own_ref, next_ref, up_ref, mix_ref, down_ref, *partial_refs):
    pairs, pair_size, window, channels = own_ref.shape
    other_tap = (2 - 2 * side_ref[0], 2 * side_ref[0])
    for pair in range(pairs):
        for member in range(pair_size):
            rows = jnp.concatenate([own_ref[pair, member], next_ref[pair, member]], axis=0)
            rows = rows.astype(jnp.float32)
            normed = layer_norm(rows)
            total = rows
            for start in range(0, up_ref.shape[1], CHUNK):
                lanes = slice(start, start + CHUNK)
                hidden = mlp_hidden(normed, up_ref, start)
                lines = [hidden[:window], hidden[window:]]
                same = mix_ref[1, :, lanes].astype(jnp.float32)
                mixed = []
                for slot in range(2):
                    across = mix_ref[other_tap[slot], :, lanes].astype(jnp.float32)
                    mixed.append(
                        mlp_mix(
                            [
                                lines[slot] * same[b][None] + lines[1 - slot] * across[b][None]
                                for b in range(3)
                            ],
                            window,
                        )
                    )
                total = total + dot_dims(jnp.concatenate(mixed, axis=0), down_ref[lanes], 1, 0)
            for slot in range(2):
                partial_refs[slot][pair, member] = total[slot * window : (slot + 1) * window]


def outer_kernel(
    left, slot, side_ref, edge_ref, partial_ref, halo_ref, up_ref, mix_ref, down_ref, own_ref, sibling_ref
):
    pairs, pair_size, window, channels = partial_ref.shape
    tap = 2 * side_ref[0] if slot == 0 else 2 - 2 * side_ref[0]
    for pair in range(pairs):
        rows = halo_ref[pair].reshape(pair_size * window, channels).astype(jnp.float32)
        normed = layer_norm(jnp.where(edge_ref[0] == 1, jnp.zeros_like(rows), rows))
        total = partial_ref[pair].reshape(pair_size * window, channels)
        for start in range(0, up_ref.shape[1], CHUNK):
            lanes = slice(start, start + CHUNK)
            hidden = mlp_hidden(normed, up_ref, start)
            across = mix_ref[tap, :, lanes].astype(jnp.float32)
            mixed = [
                mlp_mix(
                    [
                        hidden[member * window : (member + 1) * window] * across[b][None]
                        for b in range(3)
                    ],
                    window,
                )
                for member in range(pair_size)
            ]
            total = total + dot_dims(jnp.concatenate(mixed, axis=0), down_ref[lanes], 1, 0)
        for member, ref in enumerate((own_ref, sibling_ref)):
            shifted = pltpu.roll(total[member * window : (member + 1) * window], window - left, 0)
            ref[pair] = shifted.astype(jnp.bfloat16)


def shards(
    video,
    stereo_qk,
    stereo_v,
    stereo_out,
    temporal_qk,
    temporal_v,
    temporal_out,
    mlp_up,
    mix_kernel,
    mlp_down,
):
    width, channels = video.shape[-2:]
    frame_size, rows_size = lax.axis_size("frame"), lax.axis_size("rows")
    pairs = frame_size // 2
    owners = frame_size
    cols = width // owners
    window = round_up(cols + 2, 16)
    left = (window - cols) // 2
    frame, row = lax.axis_index("frame"), lax.axis_index("rows")
    pair, side = frame // 2, row % 2
    side_arg = side.astype(jnp.int32)[None]
    both = ("frame", "rows")
    slots = [(s, p) for s in range(2) for p in range(pairs)]

    def owner_at(s, p):
        return lax.rem(pair + p, pairs) * 2 + (side ^ s)

    def chip_moves(s, p):
        return [
            (
                f * rows_size + r,
                ((f // 2 + p) % pairs * 2 + f % 2) * rows_size + (r ^ s),
            )
            for f in range(frame_size)
            for r in range(rows_size)
        ]

    siblings = [(f, f ^ 1) for f in range(frame_size)]
    bands = rows_size // 2
    band_moves = []
    for slot in range(2):
        moves = []
        for r in range(rows_size):
            band = r // 2 + (1 if (r + slot) % 2 else -1)
            moves.append((r, band * 2 + r % 2 if 0 <= band < bands else r ^ 1))
        band_moves.append(moves)
    first_band, last_band = row // 2 == 0, row // 2 == bands - 1
    at_edge = (
        jnp.where(side == 0, last_band, first_band),
        jnp.where(side == 0, first_band, last_band),
    )
    edge_args = [edge.astype(jnp.int32)[None] for edge in at_edge]
    core_arg = (frame % 2).astype(jnp.int32)[None]
    sibling_video = lax.ppermute(video, "frame", siblings)
    windows, *weights = first_stereo(
        core_arg,
        video,
        owners,
        left,
        window,
        stereo_qk,
        stereo_v,
        stereo_out,
        temporal_qk,
        temporal_v,
        temporal_out,
    )
    sibling_windows = kernel_call(
        functools.partial(second_kernel, left, cols),
        "stereo",
        2_400_000_000,
        jax.ShapeDtypeStruct(windows.shape, windows.dtype),
        (core_arg,),
        sibling_video,
        *weights[:3],
    )
    pieces = {}
    for s, p in slots:
        index = owner_at(s, p)
        piece = jnp.stack(
            [
                lax.dynamic_index_in_dim(array, index, 0, keepdims=False)
                for array in (windows, sibling_windows)
            ]
        )
        if (s, p) != (0, 0):
            piece = lax.ppermute(piece, both, chip_moves(s, p))
        pieces[s, p] = piece
    shape = (pairs, 2, window, channels)
    sections, halos = [], []
    for s in range(2):
        section = kernel_call(
            functools.partial(temporal_kernel, pairs),
            "temporal",
            1_000_000_000,
            jax.ShapeDtypeStruct(shape, jnp.bfloat16),
            (),
            *[pieces[s, p] for p in range(pairs)],
            *weights[3:],
        )
        sections.append(section)
        halos.append(lax.ppermute(section, "rows", band_moves[s]))
    partials = kernel_call(
        inner_kernel,
        "inner",
        4_000_000_000,
        [jax.ShapeDtypeStruct(shape, jnp.float32)] * 2,
        (side_arg,),
        *sections,
        mlp_up,
        mix_kernel,
        mlp_down,
    )
    output = jnp.zeros((video.shape[0], width, channels), jnp.bfloat16)
    for s in (1, 0):
        own_out, sibling_out = kernel_call(
            functools.partial(outer_kernel, left, s),
            "outer",
            1_000_000_000,
            [jax.ShapeDtypeStruct((pairs, window, channels), jnp.bfloat16)] * 2,
            (side_arg, edge_args[1 - s]),
            partials[s],
            halos[1 - s],
            mlp_up,
            mix_kernel,
            mlp_down,
        )
        other_out = lax.ppermute(sibling_out, "frame", siblings)
        first_view = jnp.where(frame % 2 == 0, own_out, other_out)
        second_view = jnp.where(frame % 2 == 0, other_out, own_out)
        for p in range(pairs):
            piece = jnp.stack([first_view[p, :cols], second_view[p, :cols]])
            if (s, p) != (0, 0):
                back = [(j, i) for i, j in chip_moves(s, p)]
                piece = lax.ppermute(piece, both, back)
            output = lax.dynamic_update_slice(output, piece, (0, owner_at(s, p) * cols, 0))
    return output.reshape(video.shape)


def solution(mesh):
    in_specs = (P(None, "frame", "rows", None, None), P(), P(), P(), P(), P(), P(), P(), P(), P())
    out_specs = P(None, "frame", "rows", None, None)
    return jax.shard_map(shards, mesh=mesh, in_specs=in_specs, out_specs=out_specs, check_vma=False)
```

time: 60.2 us -> 45.4 us (0.75)
  waiting for transfers between devices: 21.3 us -> 13.3 us
  local copies, waits for them, and re-layouts: 5.42 us -> 1.6 us
  starting transfers between devices: 13.1 us -> 11.3 us
  Pallas kernels: 19.8 us -> 18.7 us
    ppermute x3 -> x5, waiting for transfers between devices: 10.5 us -> 0.99 us  [the longest x2 0.99 us: shards(): other_out = lax.ppermute(sibling_out, 'frame', siblings)]
    unnamed x22 -> x8, local copies, waits for them, and re-layouts: 4.58 us -> 0.78 us
    ppermute x3 -> x5, starting transfers between devices: 4.99 us -> 3.38 us  [the longest x2 2.31 us: shards(): halos.append(lax.ppermute(section, 'rows', band_moves[s]))]
    ppermute x3, waiting for transfers between devices: 4.57 us -> 5.76 us  [shards(): piece = lax.ppermute(piece, both, back)]
    pallas_call x3 -> x7, Pallas kernels: 19.8 us -> 18.7 us  [the longest x6 14.3 us: kernel_call(): pl.pallas_call(body, in_specs=[pl.BlockSpec(memory_space=pltpu.SMEM)] * l...]
  transfers between devices with their start and end apart: 9 -> 11, of which waited for: 7 -> 4; matrix products, arithmetic and copies ran while one was open for 0% -> 0% of each run, Pallas kernels for 0% -> 34%
where the time goes in v3:
time: 45.4 us; the launch traced here: 45.2 us
  Pallas kernels  18.7 us (41%)
  waiting for transfers between devices  13.3 us (29%)
  starting transfers between devices  11.3 us (25%)
  local copies, waits for them, and re-layouts  1.6 us (4%)
    pallas_call x6, Pallas kernels, kernel_call(): pl.pallas_call(body, in_specs=[pl.BlockSpec(memory_space=pltpu.SMEM)] * l...  14.3 us
    ppermute x3, waiting for transfers between devices, shards(): piece = lax.ppermute(piece, both, chip_moves(s, p))  6.51 us
    ppermute x3, waiting for transfers between devices, shards(): piece = lax.ppermute(piece, both, back)  5.76 us
    pallas_call x1, Pallas kernels, first_stereo(): pl.pallas_call(functools.partial(first_kernel, left, width // owners), in...  4.38 us
    ppermute x3, starting transfers between devices, shards(): piece = lax.ppermute(piece, both, chip_moves(s, p))  4.22 us
    ppermute x3, starting transfers between devices, shards(): piece = lax.ppermute(piece, both, back)  3.7 us
    ppermute x2, starting transfers between devices, shards(): halos.append(lax.ppermute(section, 'rows', band_moves[s]))  2.31 us
    ppermute x2, waiting for transfers between devices, shards(): other_out = lax.ppermute(sibling_out, 'frame', siblings)  0.99 us
  transfers between devices with their start and end apart: 11, of which 4 were waited for; matrix products, arithmetic and copies ran while one was open for 0% of the time, Pallas kernels for 34%

profile of v3, /device:TPU:0, one launch (start us, length us, event | category | flops | bytes accessed | tf_op | source)
XLA Modules:
  0.0 45.2 jit_solution(4276879551829769259)
XLA Ops:
  0.0 0.5 %collective-permute-start = (bf16[2,1,1,480,256]{4,3,2,1,0:T(8,128)(2,1)}, bf16[2,1,1,480,256]{4,3,2,1,0:T(8,128)(2,1)S(1)}, u32[]{:S(2)}, u32[]{:S(2)}) collective-permute-start(bf16[2,1,1,480,256]{4,3,2,1,0:T(8,128)(2,1)} %refs_0_.1), channel_id=1, source_target_pairs={{0,8},{8,0},{16,24},{24,16},{1,9},{9,1},{17,25},{25,17},{2,10},{10... | collective-permute-start | bytes 1474568 | tf_op jit(solution)/shard_map/ppermute | solution.py:294
  0.5 4.4 %stereo.2 = (bf16[4,128,256]{2,1,0:T(8,128)(2,1)S(1)}, bf16[256,512]{1,0:T(8,128)(2,1)S(1)}, bf16[256,256]{1,0:T(8,128)(2,1)S(1)}, bf16[256,256]{1,0:T(8,128)(2,...) custom-call(s32[1]{0:T(128)} %bitcast.2.core_ref, ...), custom_call_target="tpu_custom_call" | custom-call | flops 2400000000 | bytes 2000000 | tf_op jit(solution)/shard_map/stereo/pallas_call | solution.py:93
  4.9 3.1 %stereo.3 = bf16[4,128,256]{2,1,0:T(8,128)(2,1)S(1)} custom-call(s32[1]{0:T(128)} %bitcast.2.core_ref, bf16[2,1,1,480,256]{4,3,2,1,0:T(8,128)(2,1)S(1)} %collective-permute-done.video_ref, bf16[256,512]{1,0:T(8,128)(2,1)S(1)} %get-tuple-element.19.qk_ref, bf16[256,256]{1,0:T(8,128)(2,1)S(1)} %get-tuple-element.20.v_ref, ...), custom_call_target="tpu_custom_call" | custom-call | flops 2400000000 | bytes 3000000 | tf_op jit(solution)/shard_map/stereo/pallas_call | solution.py:148
  8.1 3.5 %collective-permute-start.3 = (bf16[2,128,256]{2,1,0:T(8,128)(2,1)S(1)}, bf16[2,128,256]{2,1,0:T(8,128)(2,1)S(1)}, u32[]{:S(2)}, u32[]{:S(2)}) collective-permute-start(bf16[2,128,256]{2,1,0:T(8,128)(2,1)S(1)} %pad_maximum_fusion.3), channel_id=1, source_target_pairs={{0,17},{1,16},{2,19},{3,18},{4,21},{5,20},{6,23},{7,22},{8,25},{9,... | collective-permute-start | bytes 393224 | tf_op jit(solution)/shard_map/ppermute | solution.py:327
  11.6 0.6 %collective-permute-start.1 = (bf16[2,128,256]{2,1,0:T(8,128)(2,1)S(1)}, bf16[2,128,256]{2,1,0:T(8,128)(2,1)S(1)}, u32[]{:S(2)}, u32[]{:S(2)}) collective-permute-start(bf16[2,128,256]{2,1,0:T(8,128)(2,1)S(1)} %pad_maximum_fusion.1), channel_id=1, source_target_pairs={{0,16},{1,17},{2,18},{3,19},{4,20},{5,21},{6,22},{7,23},{8,24},{9,... | collective-permute-start | bytes 393224 | tf_op jit(solution)/shard_map/ppermute | solution.py:327
  12.3 0.1 collective-permute-start.2
  12.4 6.5 %collective-permute-done.1.refs_1_ = bf16[2,128,256]{2,1,0:T(8,128)(2,1)S(1)} collective-permute-done((bf16[2,128,256]{2,1,0:T(8,128)(2,1)S(1)}, bf16[2,128,256]{2,1,0:T(8,128)(2,1)S(1)}, u32[]{:S(2)}, u32[]{:S(2)}) %collective-permute-start.1) | collective-permute-done | bytes 131104 | tf_op jit(solution)/shard_map/ppermute | solution.py:327
  18.9 1.4 %temporal.2.own_ref = bf16[2,2,128,256]{3,2,1,0:T(8,128)(2,1)S(1)} custom-call(bf16[2,128,256]{2,1,0:T(8,128)(2,1)S(1)} %pad_maximum_fusion.refs_0_, bf16[2,128,256]{2,1,0:T(8,128)(2,1)S(1)} %collective-permute-done.1.refs_1_, bf16[256,512]{1,0:T(8,128)(2,1)S(1)} %get-tuple-element.22.refs_2_, bf16[256,256]{1,0:T(8,128)(2,1)S(1)} %get-tuple-element.23.refs_3_, ...), custom_call_target="tpu_custom_call" | custom-call | flops 1000000000 | bytes 3000000 | tf_op jit(solution)/shard_map/temporal/pallas_call | solution.py:148
  20.3 0.0 copy-start
  20.3 0.0 copy-start.1
  20.3 0.0 copy-start.2
  20.3 0.3 collective-permute-start.4
  20.6 0.0 collective-permute-done.3.refs_1_
  20.6 0.0 collective-permute-done.2.refs_0_
  20.6 1.4 %temporal.3.next_ref = bf16[2,2,128,256]{3,2,1,0:T(8,128)(2,1)S(1)} custom-call(bf16[2,128,256]{2,1,0:T(8,128)(2,1)S(1)} %collective-permute-done.2.refs_0_, bf16[2,128,256]{2,1,0:T(8,128)(2,1)S(1)} %collective-permute-done.3.refs_1_, bf16[256,512]{1,0:T(8,128)(2,1)S(1)} %get-tuple-element.22.refs_2_, bf16[256,256]{1,0:T(8,128)(2,1)S(1)} %get-tuple-element.23.refs_3_, ...), custom_call_target="tpu_custom_call" | custom-call | flops 1000000000 | bytes 3000000 | tf_op jit(solution)/shard_map/temporal/pallas_call | solution.py:148
  22.0 2.0 %collective-permute-start.8 = (bf16[2,2,128,256]{3,2,1,0:T(8,128)(2,1)S(1)}, bf16[2,2,128,256]{3,2,1,0:T(8,128)(2,1)S(1)}, u32[]{:S(2)}, u32[]{:S(2)}) collective-permute-start(bf16[2,2,128,256]{3,2,1,0:T(8,128)(2,1)S(1)} %temporal.3.next_ref), channel_id=1, source_target_pairs={{0,2},{1,0},{2,4},{3,1},{4,6},{5,3},{6,7},{7,5},{8,10},{9,8},{10,1... | collective-permute-start | bytes 786440 | tf_op jit(solution)/shard_map/ppermute | solution.py:342
  24.0 4.4 %inner.1 = (f32[2,2,128,256]{3,2,1,0:T(8,128)S(1)}, f32[2,2,128,256]{3,2,1,0:T(8,128)S(1)}) custom-call(s32[1]{0:T(128)} %bitcast.side_ref, bf16[2,2,128,256]{3,2,1,0:T(8,128)(2,1)S(1)} %temporal.2.own_ref, bf16[2,2,128,256]{3,2,1,0:T(8,128)(2,1)S(1)} %temporal.3.next_ref, bf16[256,1024]{1,0:T(8,128)(2,1)S(1)} %copy-done, bf16[3,3,1024]{2,1,0:T(4,128)(2,1)S(1)} %copy-done.2, ...), custom_call_target="tpu_custom_call" | custom-call | flops 4000000000 | bytes 3000000 | tf_op jit(solution)/shard_map/inner/pallas_call | solution.py:148
  28.5 2.0 %outer.2 = (bf16[2,128,256]{2,1,0:T(8,128)(2,1)S(1)}, bf16[2,128,256]{2,1,0:T(8,128)(2,1)S(1)}) custom-call(s32[1]{0:T(128)} %bitcast.side_ref, s32[1]{0:T(128)} %bitcast.1.edge_ref, f32[2,2,128,256]{3,2,1,0:T(8,128)S(1)} %get-tuple-element.25.partial_ref, bf16[2,2,128,256]{3,2,1,0:T(8,128)(2,1)S(1)} %collective-permute-done.4.halo_ref, ...), custom_call_target="tpu_custom_call" | custom-call | flops 1000000000 | bytes 3000000 | tf_op jit(solution)/shard_map/outer/pallas_call | solution.py:148
  30.5 0.1 collective-permute-start.5
  30.5 0.0 collective-permute-done.8.halo_ref
  30.5 2.0 %outer.3 = (bf16[2,128,256]{2,1,0:T(8,128)(2,1)S(1)}, bf16[2,128,256]{2,1,0:T(8,128)(2,1)S(1)}) custom-call(s32[1]{0:T(128)} %bitcast.side_ref, s32[1]{0:T(128)} %bitcast.7.edge_ref, f32[2,2,128,256]{3,2,1,0:T(8,128)S(1)} %get-tuple-element.28.partial_ref, bf16[2,2,128,256]{3,2,1,0:T(8,128)(2,1)S(1)} %collective-permute-done.8.halo_ref, ...), custom_call_target="tpu_custom_call" | custom-call | flops 1000000000 | bytes 3000000 | tf_op jit(solution)/shard_map/outer/pallas_call | solution.py:148
  32.5 0.6 %collective-permute-start.9 = (bf16[2,128,256]{2,1,0:T(8,128)(2,1)S(1)}, bf16[2,128,256]{2,1,0:T(8,128)(2,1)S(1)}, u32[]{:S(2)}, u32[]{:S(2)}) collective-permute-start(bf16[2,128,256]{2,1,0:T(8,128)(2,1)S(1)} %get-tuple-element.30), channel_id=1, source_target_pairs={{0,8},{8,0},{16,24},{24,16},{1,9},{9,1},{17,25},{25,17},{2,10},{10... | collective-permute-start | bytes 393224 | tf_op jit(solution)/shard_map/ppermute | solution.py:368
  33.1 0.0 collective-permute-done.5
  33.1 1.0 %collective-permute-done.9 = bf16[2,128,256]{2,1,0:T(8,128)(2,1)S(1)} collective-permute-done((bf16[2,128,256]{2,1,0:T(8,128)(2,1)S(1)}, bf16[2,128,256]{2,1,0:T(8,128)(2,1)S(1)}, u32[]{:S(2)}, u32[]{:S(2)}) %collective-permute-start.9) | collective-permute-done | bytes 131104 | tf_op jit(solution)/shard_map/ppermute | solution.py:368
  34.2 1.1 %collective-permute-start.6 = (bf16[2,120,256]{2,1,0:T(8,128)(2,1)S(1)}, bf16[2,120,256]{2,1,0:T(8,128)(2,1)S(1)}, u32[]{:S(2)}, u32[]{:S(2)}) collective-permute-start(bf16[2,120,256]{2,1,0:T(8,128)(2,1)S(1)} %pad_maximum_fusion.4), channel_id=1, source_target_pairs={{1,0},{0,1},{3,2},{2,3},{5,4},{4,5},{7,6},{6,7},{9,8},{8,9},{11,10... | collective-permute-start | bytes 368648 | tf_op jit(solution)/shard_map/ppermute | solution.py:375
  35.3 1.6 %collective-permute-start.10 = (bf16[2,120,256]{2,1,0:T(8,128)(2,1)S(1)}, bf16[2,120,256]{2,1,0:T(8,128)(2,1)S(1)}, u32[]{:S(2)}, u32[]{:S(2)}) collective-permute-start(bf16[2,120,256]{2,1,0:T(8,128)(2,1)S(1)} %pad_maximum_fusion.6), channel_id=1, source_target_pairs={{16,0},{17,1},{18,2},{19,3},{20,4},{21,5},{22,6},{23,7},{24,8},{25... | collective-permute-start | bytes 368648 | tf_op jit(solution)/shard_map/ppermute | solution.py:375
  36.9 1.1 %collective-permute-start.7 = (bf16[2,120,256]{2,1,0:T(8,128)(2,1)S(1)}, bf16[2,120,256]{2,1,0:T(8,128)(2,1)S(1)}, u32[]{:S(2)}, u32[]{:S(2)}) collective-permute-start(bf16[2,120,256]{2,1,0:T(8,128)(2,1)S(1)} %pad_maximum_fusion.5), channel_id=1, source_target_pairs={{17,0},{16,1},{19,2},{18,3},{21,4},{20,5},{23,6},{22,7},{25,8},{24... | collective-permute-start | bytes 368648 | tf_op jit(solution)/shard_map/ppermute | solution.py:375
  37.9 1.9 %collective-permute-done.6 = bf16[2,120,256]{2,1,0:T(8,128)(2,1)S(1)} collective-permute-done((bf16[2,120,256]{2,1,0:T(8,128)(2,1)S(1)}, bf16[2,120,256]{2,1,0:T(8,128)(2,1)S(1)}, u32[]{:S(2)}, u32[]{:S(2)}) %collective-permute-start.6) | collective-permute-done | bytes 122912 | tf_op jit(solution)/shard_map/ppermute | solution.py:375
  39.9 3.8 %collective-permute-done.7 = bf16[2,120,256]{2,1,0:T(8,128)(2,1)S(1)} collective-permute-done((bf16[2,120,256]{2,1,0:T(8,128)(2,1)S(1)}, bf16[2,120,256]{2,1,0:T(8,128)(2,1)S(1)}, u32[]{:S(2)}, u32[]{:S(2)}) %collective-permute-start.7) | collective-permute-done | bytes 122912 | tf_op jit(solution)/shard_map/ppermute | solution.py:375
  43.8 0.0 copy-start.3
  43.8 0.8 %copy-done.3 = bf16[2,1,1,480,256]{4,3,2,1,0:T(8,128)(2,1)} copy-done((bf16[2,1,1,480,256]{4,3,2,1,0:T(8,128)(2,1)}, bf16[2,1,1,480,256]{4,3,2,1,0:T(8,128)(2,1)S(1)}, u32[]{:S(2)}) %copy-start.3) | copy-done | bytes 491544
  44.6 0.7 %bitcast_dynamic-update-slice_fusion = bf16[2,1,1,480,256]{4,3,2,1,0:T(8,128)(2,1)} fusion(bf16[2,1,1,480,256]{4,3,2,1,0:T(8,128)(2,1)} %copy-done.3, s32[]{:T(128)S(6)} %select_n.101, bf16[2,120,256]{2,1,0:T(8,128)(2,1)S(1)} %collective-permute-done.10), kind=kLoop, calls=%fused_computation.13 | loop fusion | bytes 245764 | tf_op jit(solution)/shard_map/dynamic_update_slice | solution.py:376
  (24 shorter events, 0.3 us)
Async XLA Ops:
  0.0 4.9 %collective-permute-start = (bf16[2,1,1,480,256]{4,3,2,1,0:T(8,128)(2,1)}, bf16[2,1,1,480,256]{4,3,2,1,0:T(8,128)(2,1)S(1)}, u32[]{:S(2)}, u32[]{:S(2)}) collective-permute-start(bf16[2,1,1,480,256]{4,3,2,1,0:T(8,128)(2,1)} %refs_0_.1), channel_id=1, source_target_pairs={{0,8},{8,0},{16,24},{24,16},{1,9},{9,1},{17,25},{25,17},{2,10},{10... | collective-permute-start | bytes 1474568 | tf_op jit(solution)/shard_map/ppermute | solution.py:294
  8.1 12.5 %collective-permute-start.3 = (bf16[2,128,256]{2,1,0:T(8,128)(2,1)S(1)}, bf16[2,128,256]{2,1,0:T(8,128)(2,1)S(1)}, u32[]{:S(2)}, u32[]{:S(2)}) collective-permute-start(bf16[2,128,256]{2,1,0:T(8,128)(2,1)S(1)} %pad_maximum_fusion.3), channel_id=1, source_target_pairs={{0,17},{1,16},{2,19},{3,18},{4,21},{5,20},{6,23},{7,22},{8,25},{9,... | collective-permute-start | bytes 393224 | tf_op jit(solution)/shard_map/ppermute | solution.py:327
  11.6 7.3 %collective-permute-start.1 = (bf16[2,128,256]{2,1,0:T(8,128)(2,1)S(1)}, bf16[2,128,256]{2,1,0:T(8,128)(2,1)S(1)}, u32[]{:S(2)}, u32[]{:S(2)}) collective-permute-start(bf16[2,128,256]{2,1,0:T(8,128)(2,1)S(1)} %pad_maximum_fusion.1), channel_id=1, source_target_pairs={{0,16},{1,17},{2,18},{3,19},{4,20},{5,21},{6,22},{7,23},{8,24},{9,... | collective-permute-start | bytes 393224 | tf_op jit(solution)/shard_map/ppermute | solution.py:327
  12.3 8.4 %collective-permute-start.2 = (bf16[2,128,256]{2,1,0:T(8,128)(2,1)S(1)}, bf16[2,128,256]{2,1,0:T(8,128)(2,1)S(1)}, u32[]{:S(2)}, u32[]{:S(2)}) collective-permute-start(bf16[2,128,256]{2,1,0:T(8,128)(2,1)S(1)} %pad_maximum_fusion.2), channel_id=1, source_target_pairs={{0,1},{1,0},{2,3},{3,2},{4,5},{5,4},{6,7},{7,6},{8,9},{9,8},{10,11... | collective-permute-start | bytes 393224 | tf_op jit(solution)/shard_map/ppermute | solution.py:327
  20.3 3.7 %copy-start = (bf16[256,1024]{1,0:T(8,128)(2,1)S(1)}, bf16[256,1024]{1,0:T(8,128)(2,1)}, u32[]{:S(2)}) copy-start(bf16[256,1024]{1,0:T(8,128)(2,1)} %up_ref.5) | copy-start | bytes 1572868
  20.3 3.7 %copy-start.1 = (bf16[1024,256]{1,0:T(8,128)(2,1)S(1)}, bf16[1024,256]{1,0:T(8,128)(2,1)}, u32[]{:S(2)}) copy-start(bf16[1024,256]{1,0:T(8,128)(2,1)} %down_ref.5) | copy-start | bytes 1572868
  20.3 3.7 %copy-start.2 = (bf16[3,3,1024]{2,1,0:T(4,128)(2,1)S(1)}, bf16[3,3,1024]{2,1,0:T(4,128)(2,1)}, u32[]{:S(2)}) copy-start(bf16[3,3,1024]{2,1,0:T(4,128)(2,1)} %mix_ref.5) | copy-start | bytes 55300
  20.3 8.2 %collective-permute-start.4 = (bf16[2,2,128,256]{3,2,1,0:T(8,128)(2,1)S(1)}, bf16[2,2,128,256]{3,2,1,0:T(8,128)(2,1)S(1)}, u32[]{:S(2)}, u32[]{:S(2)}) collective-permute-start(bf16[2,2,128,256]{3,2,1,0:T(8,128)(2,1)S(1)} %temporal.2.own_ref), channel_id=1, source_target_pairs={{0,1},{1,3},{2,0},{3,5},{4,2},{5,7},{6,4},{7,6},{8,9},{9,11},{10,8... | collective-permute-start | bytes 786440 | tf_op jit(solution)/shard_map/ppermute | solution.py:342
  22.0 8.5 %collective-permute-start.8 = (bf16[2,2,128,256]{3,2,1,0:T(8,128)(2,1)S(1)}, bf16[2,2,128,256]{3,2,1,0:T(8,128)(2,1)S(1)}, u32[]{:S(2)}, u32[]{:S(2)}) collective-permute-start(bf16[2,2,128,256]{3,2,1,0:T(8,128)(2,1)S(1)} %temporal.3.next_ref), channel_id=1, source_target_pairs={{0,2},{1,0},{2,4},{3,1},{4,6},{5,3},{6,7},{7,5},{8,10},{9,8},{10,1... | collective-permute-start | bytes 786440 | tf_op jit(solution)/shard_map/ppermute | solution.py:342
  30.5 2.6 %collective-permute-start.5 = (bf16[2,128,256]{2,1,0:T(8,128)(2,1)S(1)}, bf16[2,128,256]{2,1,0:T(8,128)(2,1)S(1)}, u32[]{:S(2)}, u32[]{:S(2)}) collective-permute-start(bf16[2,128,256]{2,1,0:T(8,128)(2,1)S(1)} %get-tuple-element.27), channel_id=1, source_target_pairs={{0,8},{8,0},{16,24},{24,16},{1,9},{9,1},{17,25},{25,17},{2,10},{10... | collective-permute-start | bytes 393224 | tf_op jit(solution)/shard_map/ppermute | solution.py:368
  32.5 1.5 %collective-permute-start.9 = (bf16[2,128,256]{2,1,0:T(8,128)(2,1)S(1)}, bf16[2,128,256]{2,1,0:T(8,128)(2,1)S(1)}, u32[]{:S(2)}, u32[]{:S(2)}) collective-permute-start(bf16[2,128,256]{2,1,0:T(8,128)(2,1)S(1)} %get-tuple-element.30), channel_id=1, source_target_pairs={{0,8},{8,0},{16,24},{24,16},{1,9},{9,1},{17,25},{25,17},{2,10},{10... | collective-permute-start | bytes 393224 | tf_op jit(solution)/shard_map/ppermute | solution.py:368
  34.2 5.7 %collective-permute-start.6 = (bf16[2,120,256]{2,1,0:T(8,128)(2,1)S(1)}, bf16[2,120,256]{2,1,0:T(8,128)(2,1)S(1)}, u32[]{:S(2)}, u32[]{:S(2)}) collective-permute-start(bf16[2,120,256]{2,1,0:T(8,128)(2,1)S(1)} %pad_maximum_fusion.4), channel_id=1, source_target_pairs={{1,0},{0,1},{3,2},{2,3},{5,4},{4,5},{7,6},{6,7},{9,8},{8,9},{11,10... | collective-permute-start | bytes 368648 | tf_op jit(solution)/shard_map/ppermute | solution.py:375
  35.3 8.5 %collective-permute-start.10 = (bf16[2,120,256]{2,1,0:T(8,128)(2,1)S(1)}, bf16[2,120,256]{2,1,0:T(8,128)(2,1)S(1)}, u32[]{:S(2)}, u32[]{:S(2)}) collective-permute-start(bf16[2,120,256]{2,1,0:T(8,128)(2,1)S(1)} %pad_maximum_fusion.6), channel_id=1, source_target_pairs={{16,0},{17,1},{18,2},{19,3},{20,4},{21,5},{22,6},{23,7},{24,8},{25... | collective-permute-start | bytes 368648 | tf_op jit(solution)/shard_map/ppermute | solution.py:375
  36.9 6.9 %collective-permute-start.7 = (bf16[2,120,256]{2,1,0:T(8,128)(2,1)S(1)}, bf16[2,120,256]{2,1,0:T(8,128)(2,1)S(1)}, u32[]{:S(2)}, u32[]{:S(2)}) collective-permute-start(bf16[2,120,256]{2,1,0:T(8,128)(2,1)S(1)} %pad_maximum_fusion.5), channel_id=1, source_target_pairs={{17,0},{16,1},{19,2},{18,3},{21,4},{20,5},{23,6},{22,7},{25,8},{24... | collective-permute-start | bytes 368648 | tf_op jit(solution)/shard_map/ppermute | solution.py:375
  43.8 0.8 %copy-start.3 = (bf16[2,1,1,480,256]{4,3,2,1,0:T(8,128)(2,1)}, bf16[2,1,1,480,256]{4,3,2,1,0:T(8,128)(2,1)S(1)}, u32[]{:S(2)}) copy-start(bf16[2,1,1,480,256]{4,3,2,1,0:T(8,128)(2,1)S(1)} %fusion) | copy-start | bytes 1474564

commit v4 on v3

--- a/solution.py
+++ b/solution.py
@@ -114,8 +114,8 @@
     return jnp.sum(product.reshape(HEADS, HEAD_DIM, width), axis=1, keepdims=True)
 
 
-def temporal_kernel(pairs, *refs):
-    pieces, (qk_ref, v_ref, out_ref, section_ref) = refs[:pairs], refs[pairs:]
+def temporal_kernel(pairs, order, *refs):
+    pieces, (qk_ref, v_ref, out_ref, section_ref) = refs[:pairs][::order], refs[pairs:]
     _, pair_size, window, channels = section_ref.shape
     frames = pairs * pair_size
     rows = jnp.concatenate(
@@ -144,26 +144,38 @@
     section_ref[...] = (rows + update).astype(jnp.bfloat16).reshape(section_ref.shape)
 
 
-def kernel_call(body, name, flops, out_shape, scalars, *operands):
+def kernel_call(body, name, flops, out_shape, scalars, *operands, after=()):
+    count = len(scalars) + len(operands)
+
+    def ordered_body(*refs):
+        body(*refs[:count], *refs[count + len(after) :])
+
     return pl.pallas_call(
-        body,
+        ordered_body,
         in_specs=[pl.BlockSpec(memory_space=pltpu.SMEM)] * len(scalars)
-        + [pl.BlockSpec(memory_space=pltpu.VMEM)] * len(operands),
+        + [pl.BlockSpec(memory_space=pltpu.VMEM)] * len(operands)
+        + [pl.BlockSpec(memory_space=pl.ANY)] * len(after),
         out_specs=jax.tree.map(lambda _: pl.BlockSpec(memory_space=pltpu.VMEM), out_shape),
         out_shape=out_shape,
         compiler_params=pltpu.CompilerParams(vmem_limit_bytes=VMEM_LIMIT),
         cost_estimate=pl.CostEstimate(flops=flops, bytes_accessed=3_000_000, transcendentals=0),
         name=name,
-    )(*scalars, *operands)
-
-
-def gelu(values):
-    inner = values * (0.7978845608028654 + 0.035677408136300125 * (values * values))
-    half = 0.5 * values
-    return half + half * jnp.tanh(inner)
+    )(*scalars, *operands, *after)
+
+
+def double_gelu(values):
+    inner = values * (
+        jnp.bfloat16(0.7978845608028654) + jnp.bfloat16(0.035677408136300125) * (values * values)
+    )
+    return values + values * jnp.tanh(inner)
+
+
+def half_taps(mix_ref, tap, lanes):
+    return mix_ref[tap, :, lanes] * jnp.bfloat16(0.5)
 
 
 def mlp_mix(columns, window):
+    columns = [column.astype(jnp.float32) for column in columns]
     return (
         pltpu.roll(columns[0], 1, 0) + columns[1] + pltpu.roll(columns[2], window - 1, 0)
     ).astype(jnp.bfloat16)
@@ -173,8 +185,8 @@
 
 
 def mlp_hidden(normed, up_ref, start):
-    hidden = gelu(dot_dims(normed, up_ref[:, start : start + CHUNK], 1, 0))
-    return hidden.astype(jnp.bfloat16).astype(jnp.float32)
+    product = dot_dims(normed, up_ref[:, start : start + CHUNK], 1, 0)
+    return double_gelu(product.astype(jnp.bfloat16))
 
 
 def inner_kernel(side_ref, own_ref, next_ref, up_ref, mix_ref, down_ref, *partial_refs):
@@ -190,10 +202,10 @@
                 lanes = slice(start, start + CHUNK)
                 hidden = mlp_hidden(normed, up_ref, start)
                 lines = [hidden[:window], hidden[window:]]
-                same = mix_ref[1, :, lanes].astype(jnp.float32)
+                same = half_taps(mix_ref, 1, lanes)
                 mixed = []
                 for slot in range(2):
-                    across = mix_ref[other_tap[slot], :, lanes].astype(jnp.float32)
+                    across = half_taps(mix_ref, other_tap[slot], lanes)
                     mixed.append(
                         mlp_mix(
                             [
@@ -220,7 +232,7 @@
         for start in range(0, up_ref.shape[1], CHUNK):
             lanes = slice(start, start + CHUNK)
             hidden = mlp_hidden(normed, up_ref, start)
-            across = mix_ref[tap, :, lanes].astype(jnp.float32)
+            across = half_taps(mix_ref, tap, lanes)
             mixed = [
                 mlp_mix(
                     [
@@ -330,13 +342,14 @@
     sections, halos = [], []
     for s in range(2):
         section = kernel_call(
-            functools.partial(temporal_kernel, pairs),
+            functools.partial(temporal_kernel, pairs, -1 if s else 1),
             "temporal",
             1_000_000_000,
             jax.ShapeDtypeStruct(shape, jnp.bfloat16),
             (),
-            *[pieces[s, p] for p in range(pairs)],
+            *[pieces[s, p] for p in range(pairs)][:: -1 if s else 1],
             *weights[3:],
+            after=sections[:],
         )
         sections.append(section)
         halos.append(lax.ppermute(section, "rows", band_moves[s]))
@@ -351,7 +364,8 @@
         mix_kernel,
         mlp_down,
     )
-    output = jnp.zeros((video.shape[0], width, channels), jnp.bfloat16)
+    results = {}
+    earlier = []
     for s in (1, 0):
         own_out, sibling_out = kernel_call(
             functools.partial(outer_kernel, left, s),
@@ -364,7 +378,9 @@
             mlp_up,
             mix_kernel,
             mlp_down,
+            after=earlier,
         )
+        earlier = [own_out]
         other_out = lax.ppermute(sibling_out, "frame", siblings)
         first_view = jnp.where(frame % 2 == 0, own_out, other_out)
         second_view = jnp.where(frame % 2 == 0, other_out, own_out)
@@ -373,8 +389,14 @@
             if (s, p) != (0, 0):
                 back = [(j, i) for i, j in chip_moves(s, p)]
                 piece = lax.ppermute(piece, both, back)
-            output = lax.dynamic_update_slice(output, piece, (0, owner_at(s, p) * cols, 0))
-    return output.reshape(video.shape)
+            results[s, p] = piece
+    strips = []
+    for owner in range(owners):
+        strip = results[slots[0]]
+        for slot in slots[1:]:
+            strip = jnp.where(owner_at(*slot) == owner, results[slot], strip)
+        strips.append(strip)
+    return jnp.concatenate(strips, axis=1).reshape(video.shape)
 
 
 def solution(mesh):

time: 45.4 us -> 41.6 us (0.916)
  waiting for transfers between devices: 13.3 us -> 11.1 us
  Pallas kernels: 18.7 us -> 16.6 us
  local copies, waits for them, and re-layouts: 1.6 us -> 0.12 us
  starting transfers between devices: 11.3 us -> 12.3 us
  other arithmetic: 0.15 us -> 1.05 us
    pallas_call x6, Pallas kernels: 14.3 us -> 12.3 us  [kernel_call(): pl.pallas_call(ordered_body, in_specs=[pl.BlockSpec(memory_space=pltpu.SM...]
    ppermute x3, waiting for transfers between devices: 6.51 us -> 4.65 us  [shards(): piece = lax.ppermute(piece, both, chip_moves(s, p))]
    ppermute x2, starting transfers between devices: 2.31 us -> 3.83 us  [shards(): halos.append(lax.ppermute(section, 'rows', band_moves[s]))]
    ppermute x2, waiting for transfers between devices: 0.99 us -> 0.01 us  [shards(): other_out = lax.ppermute(sibling_out, 'frame', siblings)]
    ppermute x2, waiting for transfers between devices: 0.01 us -> 0.92 us  [shards(): halos.append(lax.ppermute(section, 'rows', band_moves[s]))]
    reshape x0 -> x1, other arithmetic: none -> 0.81 us  [shards(): return jnp.concatenate(strips, axis=1).reshape(video.shape)]
    unnamed x8 -> x6, local copies, waits for them, and re-layouts: 0.78 us -> 0.02 us
    dynamic_update_slice x3 -> x0, local copies, waits for them, and re-layouts: 0.68 us -> none  [shards(): lax.dynamic_update_slice(output, piece, (0, owner_at(s, p) * cols, 0))]
  transfers between devices with their start and end apart: 11 -> 11, of which waited for: 4 -> 6; matrix products, arithmetic and copies ran while one was open for 0% -> 0% of each run, Pallas kernels for 34% -> 33%
where the time goes in v4:
time: 41.6 us; the launch traced here: 41.5 us
  Pallas kernels  16.6 us (40%)
  starting transfers between devices  12.3 us (30%)
  waiting for transfers between devices  11.1 us (27%)
  other arithmetic  1.05 us (3%)
    pallas_call x6, Pallas kernels, kernel_call(): pl.pallas_call(ordered_body, in_specs=[pl.BlockSpec(memory_space=pltpu.SM...  12.3 us
    ppermute x3, waiting for transfers between devices, shards(): piece = lax.ppermute(piece, both, back)  5.53 us
    ppermute x3, waiting for transfers between devices, shards(): piece = lax.ppermute(piece, both, chip_moves(s, p))  4.65 us
    pallas_call x1, Pallas kernels, first_stereo(): pl.pallas_call(functools.partial(first_kernel, left, width // owners), in...  4.38 us
    ppermute x3, starting transfers between devices, shards(): piece = lax.ppermute(piece, both, chip_moves(s, p))  4.22 us
    ppermute x2, starting transfers between devices, shards(): halos.append(lax.ppermute(section, 'rows', band_moves[s]))  3.83 us
    ppermute x3, starting transfers between devices, shards(): piece = lax.ppermute(piece, both, back)  3.68 us
    ppermute x2, waiting for transfers between devices, shards(): halos.append(lax.ppermute(section, 'rows', band_moves[s]))  0.92 us
  transfers between devices with their start and end apart: 11, of which 6 were waited for; matrix products, arithmetic and copies ran while one was open for 0% of the time, Pallas kernels for 33%

profile of v4, /device:TPU:0, one launch (start us, length us, event | category | flops | bytes accessed | tf_op | source)
XLA Modules:
  0.0 41.5 jit_solution(7818742676719095971)
XLA Ops:
  0.0 0.5 %collective-permute-start = (bf16[2,1,1,480,256]{4,3,2,1,0:T(8,128)(2,1)}, bf16[2,1,1,480,256]{4,3,2,1,0:T(8,128)(2,1)S(1)}, u32[]{:S(2)}, u32[]{:S(2)}) collective-permute-start(bf16[2,1,1,480,256]{4,3,2,1,0:T(8,128)(2,1)} %refs_0_.1), channel_id=1, source_target_pairs={{0,8},{8,0},{16,24},{24,16},{1,9},{9,1},{17,25},{25,17},{2,10},{10... | collective-permute-start | bytes 1474568 | tf_op jit(solution)/shard_map/ppermute | solution.py:306
  0.5 4.4 %stereo.2 = (bf16[4,128,256]{2,1,0:T(8,128)(2,1)S(1)}, bf16[256,512]{1,0:T(8,128)(2,1)S(1)}, bf16[256,256]{1,0:T(8,128)(2,1)S(1)}, bf16[256,256]{1,0:T(8,128)(2,...) custom-call(s32[1]{0:T(128)} %bitcast.2.core_ref.refs_0_, ...), custom_call_target="tpu_custom_call" | custom-call | flops 2400000000 | bytes 2000000 | tf_op jit(solution)/shard_map/stereo/pallas_call | solution.py:93
  4.9 0.0 collective-permute-done.refs_1_
  4.9 3.1 %stereo.3 = bf16[4,128,256]{2,1,0:T(8,128)(2,1)S(1)} custom-call(s32[1]{0:T(128)} %bitcast.2.core_ref.refs_0_, bf16[2,1,1,480,256]{4,3,2,1,0:T(8,128)(2,1)S(1)} %collective-permute-done.refs_1_, bf16[256,512]{1,0:T(8,128)(2,1)S(1)} %get-tuple-element.19.refs_2_, bf16[256,256]{1,0:T(8,128)(2,1)S(1)} %get-tuple-element.20.refs_3_, ...), custom_call_target="tpu_custom_call" | custom-call | flops 2400000000 | bytes 3000000 | tf_op jit(solution)/shard_map/stereo/pallas_call | solution.py:153
  8.1 2.6 %collective-permute-start.1 = (bf16[2,128,256]{2,1,0:T(8,128)(2,1)S(1)}, bf16[2,128,256]{2,1,0:T(8,128)(2,1)S(1)}, u32[]{:S(2)}, u32[]{:S(2)}) collective-permute-start(bf16[2,128,256]{2,1,0:T(8,128)(2,1)S(1)} %pad_maximum_fusion.1), channel_id=1, source_target_pairs={{0,16},{1,17},{2,18},{3,19},{4,20},{5,21},{6,22},{7,23},{8,24},{9,... | collective-permute-start | bytes 393224 | tf_op jit(solution)/shard_map/ppermute | solution.py:339
  10.7 1.6 %collective-permute-start.2 = (bf16[2,128,256]{2,1,0:T(8,128)(2,1)S(1)}, bf16[2,128,256]{2,1,0:T(8,128)(2,1)S(1)}, u32[]{:S(2)}, u32[]{:S(2)}) collective-permute-start(bf16[2,128,256]{2,1,0:T(8,128)(2,1)S(1)} %pad_maximum_fusion.2), channel_id=1, source_target_pairs={{0,17},{1,16},{2,19},{3,18},{4,21},{5,20},{6,23},{7,22},{8,25},{9,... | collective-permute-start | bytes 393224 | tf_op jit(solution)/shard_map/ppermute | solution.py:339
  12.2 0.1 collective-permute-start.3
  12.4 2.6 %collective-permute-done.1.refs_1_ = bf16[2,128,256]{2,1,0:T(8,128)(2,1)S(1)} collective-permute-done((bf16[2,128,256]{2,1,0:T(8,128)(2,1)S(1)}, bf16[2,128,256]{2,1,0:T(8,128)(2,1)S(1)}, u32[]{:S(2)}, u32[]{:S(2)}) %collective-permute-start.1) | collective-permute-done | bytes 131104 | tf_op jit(solution)/shard_map/ppermute | solution.py:339
  15.0 1.4 %temporal.2.refs_5_.refs_1_ = bf16[2,2,128,256]{3,2,1,0:T(8,128)(2,1)S(1)} custom-call(bf16[2,128,256]{2,1,0:T(8,128)(2,1)S(1)} %pad_maximum_fusion.refs_0_, bf16[2,128,256]{2,1,0:T(8,128)(2,1)S(1)} %collective-permute-done.1.refs_1_, bf16[256,512]{1,0:T(8,128)(2,1)S(1)} %get-tuple-element.22.refs_2_, bf16[256,256]{1,0:T(8,128)(2,1)S(1)} %get-tuple-element.23.refs_3_, ...), custom_call_target="tpu_custom_call" | custom-call | flops 1000000000 | bytes 3000000 | tf_op jit(solution)/shard_map/temporal/pallas_call | solution.py:153
  16.4 0.0 copy-start
  16.4 0.0 copy-start.1
  16.4 0.0 copy-start.2
  16.4 2.0 %collective-permute-start.4 = (bf16[2,2,128,256]{3,2,1,0:T(8,128)(2,1)S(1)}, bf16[2,2,128,256]{3,2,1,0:T(8,128)(2,1)S(1)}, u32[]{:S(2)}, u32[]{:S(2)}) collective-permute-start(bf16[2,2,128,256]{3,2,1,0:T(8,128)(2,1)S(1)} %temporal.2.refs_5_.refs_1_), channel_id=1, source_target_pairs={{0,1},{1,3},{2,0},{3,5},{4,2},{5,7},{6,4},{7,6},{8,9},{9,11},{10,8... | collective-permute-start | bytes 786440 | tf_op jit(solution)/shard_map/ppermute | solution.py:355
  18.4 0.5 %collective-permute-done.2.refs_0_ = bf16[2,128,256]{2,1,0:T(8,128)(2,1)S(1)} collective-permute-done((bf16[2,128,256]{2,1,0:T(8,128)(2,1)S(1)}, bf16[2,128,256]{2,1,0:T(8,128)(2,1)S(1)}, u32[]{:S(2)}, u32[]{:S(2)}) %collective-permute-start.2) | collective-permute-done | bytes 131104 | tf_op jit(solution)/shard_map/ppermute | solution.py:339
  18.9 1.5 %collective-permute-done.3.refs_1_ = bf16[2,128,256]{2,1,0:T(8,128)(2,1)S(1)} collective-permute-done((bf16[2,128,256]{2,1,0:T(8,128)(2,1)S(1)}, bf16[2,128,256]{2,1,0:T(8,128)(2,1)S(1)}, u32[]{:S(2)}, u32[]{:S(2)}) %collective-permute-start.3) | collective-permute-done | bytes 131104 | tf_op jit(solution)/shard_map/ppermute | solution.py:339
  20.5 1.4 %temporal.3.refs_2_ = bf16[2,2,128,256]{3,2,1,0:T(8,128)(2,1)S(1)} custom-call(bf16[2,128,256]{2,1,0:T(8,128)(2,1)S(1)} %collective-permute-done.2.refs_0_, bf16[2,128,256]{2,1,0:T(8,128)(2,1)S(1)} %collective-permute-done.3.refs_1_, bf16[256,512]{1,0:T(8,128)(2,1)S(1)} %get-tuple-element.22.refs_2_, bf16[256,256]{1,0:T(8,128)(2,1)S(1)} %get-tuple-element.23.refs_3_, ...), custom_call_target="tpu_custom_call" | custom-call | flops 1000000000 | bytes 3000000 | tf_op jit(solution)/shard_map/temporal/pallas_call | solution.py:153
  21.9 1.8 %collective-permute-start.8 = (bf16[2,2,128,256]{3,2,1,0:T(8,128)(2,1)S(1)}, bf16[2,2,128,256]{3,2,1,0:T(8,128)(2,1)S(1)}, u32[]{:S(2)}, u32[]{:S(2)}) collective-permute-start(bf16[2,2,128,256]{3,2,1,0:T(8,128)(2,1)S(1)} %temporal.3.refs_2_), channel_id=1, source_target_pairs={{0,2},{1,0},{2,4},{3,1},{4,6},{5,3},{6,7},{7,5},{8,10},{9,8},{10,1... | collective-permute-start | bytes 786440 | tf_op jit(solution)/shard_map/ppermute | solution.py:355
  23.7 3.2 %inner.1 = (f32[2,2,128,256]{3,2,1,0:T(8,128)S(1)}, f32[2,2,128,256]{3,2,1,0:T(8,128)S(1)}) custom-call(s32[1]{0:T(128)} %bitcast.refs_0_, bf16[2,2,128,256]{3,2,1,0:T(8,128)(2,1)S(1)} %temporal.2.refs_5_.refs_1_, bf16[2,2,128,256]{3,2,1,0:T(8,128)(2,1)S(1)} %temporal.3.refs_2_, bf16[256,1024]{1,0:T(8,128)(2,1)S(1)} %copy-done, ...), custom_call_target="tpu_custom_call" | custom-call | flops 4000000000 | bytes 3000000 | tf_op jit(solution)/shard_map/inner/pallas_call | solution.py:153
  26.9 0.0 collective-permute-done.4.refs_3_
  26.9 1.6 %outer.2 = (bf16[2,128,256]{2,1,0:T(8,128)(2,1)S(1)}, bf16[2,128,256]{2,1,0:T(8,128)(2,1)S(1)}) custom-call(s32[1]{0:T(128)} %bitcast.refs_0_, s32[1]{0:T(128)} %bitcast.1.refs_1_, f32[2,2,128,256]{3,2,1,0:T(8,128)S(1)} %get-tuple-element.25.refs_2_, bf16[2,2,128,256]{3,2,1,0:T(8,128)(2,1)S(1)} %collective-permute-done.4.refs_3_, ...), custom_call_target="tpu_custom_call" | custom-call | flops 1000000000 | bytes 3000000 | tf_op jit(solution)/shard_map/outer/pallas_call | solution.py:153
  28.5 0.1 collective-permute-start.5
  28.6 0.9 %collective-permute-done.8.refs_3_ = bf16[2,2,128,256]{3,2,1,0:T(8,128)(2,1)S(1)} collective-permute-done((bf16[2,2,128,256]{3,2,1,0:T(8,128)(2,1)S(1)}, bf16[2,2,128,256]{3,2,1,0:T(8,128)(2,1)S(1)}, u32[]{:S(2)}, u32[]{:S(2)}) %collective-permute-start.8) | collective-permute-done | bytes 262176 | tf_op jit(solution)/shard_map/ppermute | solution.py:355
  29.5 1.6 %outer.3 = (bf16[2,128,256]{2,1,0:T(8,128)(2,1)S(1)}, bf16[2,128,256]{2,1,0:T(8,128)(2,1)S(1)}) custom-call(s32[1]{0:T(128)} %bitcast.refs_0_, s32[1]{0:T(128)} %bitcast.3.refs_1_, f32[2,2,128,256]{3,2,1,0:T(8,128)S(1)} %get-tuple-element.28.refs_2_, bf16[2,2,128,256]{3,2,1,0:T(8,128)(2,1)S(1)} %collective-permute-done.8.refs_3_, ...), custom_call_target="tpu_custom_call" | custom-call | flops 1000000000 | bytes 3000000 | tf_op jit(solution)/shard_map/outer/pallas_call | solution.py:153
  31.1 0.1 collective-permute-start.9
  31.1 0.0 collective-permute-done.5
  31.2 1.5 %collective-permute-start.6 = (bf16[2,120,256]{2,1,0:T(8,128)(2,1)S(1)}, bf16[2,120,256]{2,1,0:T(8,128)(2,1)S(1)}, u32[]{:S(2)}, u32[]{:S(2)}) collective-permute-start(bf16[2,120,256]{2,1,0:T(8,128)(2,1)S(1)} %pad_maximum_fusion.4), channel_id=1, source_target_pairs={{17,0},{16,1},{19,2},{18,3},{21,4},{20,5},{23,6},{22,7},{25,8},{24... | collective-permute-start | bytes 368648 | tf_op jit(solution)/shard_map/ppermute | solution.py:391
  32.8 1.6 %collective-permute-start.7 = (bf16[2,120,256]{2,1,0:T(8,128)(2,1)S(1)}, bf16[2,120,256]{2,1,0:T(8,128)(2,1)S(1)}, u32[]{:S(2)}, u32[]{:S(2)}) collective-permute-start(bf16[2,120,256]{2,1,0:T(8,128)(2,1)S(1)} %pad_maximum_fusion.5), channel_id=1, source_target_pairs={{1,0},{0,1},{3,2},{2,3},{5,4},{4,5},{7,6},{6,7},{9,8},{8,9},{11,10... | collective-permute-start | bytes 368648 | tf_op jit(solution)/shard_map/ppermute | solution.py:391
  34.4 0.6 %collective-permute-start.10 = (bf16[2,120,256]{2,1,0:T(8,128)(2,1)S(1)}, bf16[2,120,256]{2,1,0:T(8,128)(2,1)S(1)}, u32[]{:S(2)}, u32[]{:S(2)}) collective-permute-start(bf16[2,120,256]{2,1,0:T(8,128)(2,1)S(1)} %pad_maximum_fusion.6), channel_id=1, source_target_pairs={{16,0},{17,1},{18,2},{19,3},{20,4},{21,5},{22,6},{23,7},{24,8},{25... | collective-permute-start | bytes 368648 | tf_op jit(solution)/shard_map/ppermute | solution.py:391
  35.0 3.3 %collective-permute-done.6 = bf16[2,120,256]{2,1,0:T(8,128)(2,1)S(1)} collective-permute-done((bf16[2,120,256]{2,1,0:T(8,128)(2,1)S(1)}, bf16[2,120,256]{2,1,0:T(8,128)(2,1)S(1)}, u32[]{:S(2)}, u32[]{:S(2)}) %collective-permute-start.6) | collective-permute-done | bytes 122912 | tf_op jit(solution)/shard_map/ppermute | solution.py:391
  38.4 2.2 %collective-permute-done.7 = bf16[2,120,256]{2,1,0:T(8,128)(2,1)S(1)} collective-permute-done((bf16[2,120,256]{2,1,0:T(8,128)(2,1)S(1)}, bf16[2,120,256]{2,1,0:T(8,128)(2,1)S(1)}, u32[]{:S(2)}, u32[]{:S(2)}) %collective-permute-start.7) | collective-permute-done | bytes 122912 | tf_op jit(solution)/shard_map/ppermute | solution.py:391
  40.6 0.1 select_select_fusion.3
  40.6 0.8 %maximum_bitcast_fusion = bf16[2,1,1,480,256]{4,3,2,1,0:T(8,128)(2,1)} fusion(bf16[2,120,256]{2,1,0:T(8,128)(2,1)S(1)} %get-tuple-element.32, bf16[2,120,256]{2,1,0:T(8,128)(2,1)S(1)} %get-tuple-element.33, bf16[2,120,256]{2,1,0:T(8,128)(2,1)S(1)} %select_select_fusion.2, bf16[2,120,256]{2,1,0:T(8,128)(2,1)S(1)} %get-tuple-element.31), kind=kLoop, calls=%fused_computation | loop fusion | flops 1966080 | bytes 983040 | tf_op jit(solution)/shard_map/reshape | solution.py:399
  (19 shorter events, 0.3 us)
Async XLA Ops:
  0.0 4.9 %collective-permute-start = (bf16[2,1,1,480,256]{4,3,2,1,0:T(8,128)(2,1)}, bf16[2,1,1,480,256]{4,3,2,1,0:T(8,128)(2,1)S(1)}, u32[]{:S(2)}, u32[]{:S(2)}) collective-permute-start(bf16[2,1,1,480,256]{4,3,2,1,0:T(8,128)(2,1)} %refs_0_.1), channel_id=1, source_target_pairs={{0,8},{8,0},{16,24},{24,16},{1,9},{9,1},{17,25},{25,17},{2,10},{10... | collective-permute-start | bytes 1474568 | tf_op jit(solution)/shard_map/ppermute | solution.py:306
  8.1 6.9 %collective-permute-start.1 = (bf16[2,128,256]{2,1,0:T(8,128)(2,1)S(1)}, bf16[2,128,256]{2,1,0:T(8,128)(2,1)S(1)}, u32[]{:S(2)}, u32[]{:S(2)}) collective-permute-start(bf16[2,128,256]{2,1,0:T(8,128)(2,1)S(1)} %pad_maximum_fusion.1), channel_id=1, source_target_pairs={{0,16},{1,17},{2,18},{3,19},{4,20},{5,21},{6,22},{7,23},{8,24},{9,... | collective-permute-start | bytes 393224 | tf_op jit(solution)/shard_map/ppermute | solution.py:339
  10.7 8.3 %collective-permute-start.2 = (bf16[2,128,256]{2,1,0:T(8,128)(2,1)S(1)}, bf16[2,128,256]{2,1,0:T(8,128)(2,1)S(1)}, u32[]{:S(2)}, u32[]{:S(2)}) collective-permute-start(bf16[2,128,256]{2,1,0:T(8,128)(2,1)S(1)} %pad_maximum_fusion.2), channel_id=1, source_target_pairs={{0,17},{1,16},{2,19},{3,18},{4,21},{5,20},{6,23},{7,22},{8,25},{9,... | collective-permute-start | bytes 393224 | tf_op jit(solution)/shard_map/ppermute | solution.py:339
  12.2 8.2 %collective-permute-start.3 = (bf16[2,128,256]{2,1,0:T(8,128)(2,1)S(1)}, bf16[2,128,256]{2,1,0:T(8,128)(2,1)S(1)}, u32[]{:S(2)}, u32[]{:S(2)}) collective-permute-start(bf16[2,128,256]{2,1,0:T(8,128)(2,1)S(1)} %pad_maximum_fusion.3), channel_id=1, source_target_pairs={{0,1},{1,0},{2,3},{3,2},{4,5},{5,4},{6,7},{7,6},{8,9},{9,8},{10,11... | collective-permute-start | bytes 393224 | tf_op jit(solution)/shard_map/ppermute | solution.py:339
  16.4 7.3 %copy-start = (bf16[256,1024]{1,0:T(8,128)(2,1)S(1)}, bf16[256,1024]{1,0:T(8,128)(2,1)}, u32[]{:S(2)}) copy-start(bf16[256,1024]{1,0:T(8,128)(2,1)} %refs_4_.7) | copy-start | bytes 1572868
  16.4 7.3 %copy-start.1 = (bf16[1024,256]{1,0:T(8,128)(2,1)S(1)}, bf16[1024,256]{1,0:T(8,128)(2,1)}, u32[]{:S(2)}) copy-start(bf16[1024,256]{1,0:T(8,128)(2,1)} %refs_6_.5) | copy-start | bytes 1572868
  16.4 7.3 %copy-start.2 = (bf16[3,3,1024]{2,1,0:T(4,128)(2,1)S(1)}, bf16[3,3,1024]{2,1,0:T(4,128)(2,1)}, u32[]{:S(2)}) copy-start(bf16[3,3,1024]{2,1,0:T(4,128)(2,1)} %refs_5_.7) | copy-start | bytes 55300
  16.4 10.5 %collective-permute-start.4 = (bf16[2,2,128,256]{3,2,1,0:T(8,128)(2,1)S(1)}, bf16[2,2,128,256]{3,2,1,0:T(8,128)(2,1)S(1)}, u32[]{:S(2)}, u32[]{:S(2)}) collective-permute-start(bf16[2,2,128,256]{3,2,1,0:T(8,128)(2,1)S(1)} %temporal.2.refs_5_.refs_1_), channel_id=1, source_target_pairs={{0,1},{1,3},{2,0},{3,5},{4,2},{5,7},{6,4},{7,6},{8,9},{9,11},{10,8... | collective-permute-start | bytes 786440 | tf_op jit(solution)/shard_map/ppermute | solution.py:355
  21.9 7.6 %collective-permute-start.8 = (bf16[2,2,128,256]{3,2,1,0:T(8,128)(2,1)S(1)}, bf16[2,2,128,256]{3,2,1,0:T(8,128)(2,1)S(1)}, u32[]{:S(2)}, u32[]{:S(2)}) collective-permute-start(bf16[2,2,128,256]{3,2,1,0:T(8,128)(2,1)S(1)} %temporal.3.refs_2_), channel_id=1, source_target_pairs={{0,2},{1,0},{2,4},{3,1},{4,6},{5,3},{6,7},{7,5},{8,10},{9,8},{10,1... | collective-permute-start | bytes 786440 | tf_op jit(solution)/shard_map/ppermute | solution.py:355
  28.5 2.7 %collective-permute-start.5 = (bf16[2,128,256]{2,1,0:T(8,128)(2,1)S(1)}, bf16[2,128,256]{2,1,0:T(8,128)(2,1)S(1)}, u32[]{:S(2)}, u32[]{:S(2)}) collective-permute-start(bf16[2,128,256]{2,1,0:T(8,128)(2,1)S(1)} %get-tuple-element.27), channel_id=1, source_target_pairs={{0,8},{8,0},{16,24},{24,16},{1,9},{9,1},{17,25},{25,17},{2,10},{10... | collective-permute-start | bytes 393224 | tf_op jit(solution)/shard_map/ppermute | solution.py:384
  31.1 3.3 %collective-permute-start.9 = (bf16[2,128,256]{2,1,0:T(8,128)(2,1)S(1)}, bf16[2,128,256]{2,1,0:T(8,128)(2,1)S(1)}, u32[]{:S(2)}, u32[]{:S(2)}) collective-permute-start(bf16[2,128,256]{2,1,0:T(8,128)(2,1)S(1)} %get-tuple-element.30), channel_id=1, source_target_pairs={{0,8},{8,0},{16,24},{24,16},{1,9},{9,1},{17,25},{25,17},{2,10},{10... | collective-permute-start | bytes 393224 | tf_op jit(solution)/shard_map/ppermute | solution.py:384
  31.2 7.1 %collective-permute-start.6 = (bf16[2,120,256]{2,1,0:T(8,128)(2,1)S(1)}, bf16[2,120,256]{2,1,0:T(8,128)(2,1)S(1)}, u32[]{:S(2)}, u32[]{:S(2)}) collective-permute-start(bf16[2,120,256]{2,1,0:T(8,128)(2,1)S(1)} %pad_maximum_fusion.4), channel_id=1, source_target_pairs={{17,0},{16,1},{19,2},{18,3},{21,4},{20,5},{23,6},{22,7},{25,8},{24... | collective-permute-start | bytes 368648 | tf_op jit(solution)/shard_map/ppermute | solution.py:391
  32.8 7.8 %collective-permute-start.7 = (bf16[2,120,256]{2,1,0:T(8,128)(2,1)S(1)}, bf16[2,120,256]{2,1,0:T(8,128)(2,1)S(1)}, u32[]{:S(2)}, u32[]{:S(2)}) collective-permute-start(bf16[2,120,256]{2,1,0:T(8,128)(2,1)S(1)} %pad_maximum_fusion.5), channel_id=1, source_target_pairs={{1,0},{0,1},{3,2},{2,3},{5,4},{4,5},{7,6},{6,7},{9,8},{8,9},{11,10... | collective-permute-start | bytes 368648 | tf_op jit(solution)/shard_map/ppermute | solution.py:391
  34.4 6.1 %collective-permute-start.10 = (bf16[2,120,256]{2,1,0:T(8,128)(2,1)S(1)}, bf16[2,120,256]{2,1,0:T(8,128)(2,1)S(1)}, u32[]{:S(2)}, u32[]{:S(2)}) collective-permute-start(bf16[2,120,256]{2,1,0:T(8,128)(2,1)S(1)} %pad_maximum_fusion.6), channel_id=1, source_target_pairs={{16,0},{17,1},{18,2},{19,3},{20,4},{21,5},{22,6},{23,7},{24,8},{25... | collective-permute-start | bytes 368648 | tf_op jit(solution)/shard_map/ppermute | solution.py:391

commit v5 on v4

--- a/solution.py
+++ b/solution.py
@@ -122,8 +122,8 @@
         [piece[...].reshape(pair_size * window, channels) for piece in pieces], axis=0
     ).astype(jnp.float32)
     normed = layer_norm(rows)
-    queries = dot_dims(qk_ref[:, :channels], normed, 0, 1).astype(jnp.bfloat16)
-    keys = dot_dims(qk_ref[:, channels:], normed, 0, 1).astype(jnp.bfloat16)
+    pairs_t = dot_dims(qk_ref[...], normed, 0, 1).astype(jnp.bfloat16)
+    queries, keys = pairs_t[:channels], pairs_t[channels:]
     values = dot_dims(v_ref[...], normed, 0, 1).astype(jnp.bfloat16)
     attended = []
     for frame in range(frames):
@@ -221,7 +221,7 @@
 
 
 def outer_kernel(
-    left, slot, side_ref, edge_ref, partial_ref, halo_ref, up_ref, mix_ref, down_ref, own_ref, sibling_ref
+    left, slot, side_ref, edge_ref, partial_ref, halo_ref, up_ref, mix_ref, down_ref, out_ref
 ):
     pairs, pair_size, window, channels = partial_ref.shape
     tap = 2 * side_ref[0] if slot == 0 else 2 - 2 * side_ref[0]
@@ -244,9 +244,9 @@
                 for member in range(pair_size)
             ]
             total = total + dot_dims(jnp.concatenate(mixed, axis=0), down_ref[lanes], 1, 0)
-        for member, ref in enumerate((own_ref, sibling_ref)):
+        for member in range(pair_size):
             shifted = pltpu.roll(total[member * window : (member + 1) * window], window - left, 0)
-            ref[pair] = shifted.astype(jnp.bfloat16)
+            out_ref[pair, member] = shifted.astype(jnp.bfloat16)
 
 
 def shards(
@@ -364,14 +364,13 @@
         mix_kernel,
         mlp_down,
     )
-    results = {}
-    earlier = []
+    results, crossed, earlier = {}, {}, []
     for s in (1, 0):
-        own_out, sibling_out = kernel_call(
+        finished = kernel_call(
             functools.partial(outer_kernel, left, s),
             "outer",
             1_000_000_000,
-            [jax.ShapeDtypeStruct((pairs, window, channels), jnp.bfloat16)] * 2,
+            jax.ShapeDtypeStruct(shape, jnp.bfloat16),
             (side_arg, edge_args[1 - s]),
             partials[s],
             halos[1 - s],
@@ -380,23 +379,28 @@
             mlp_down,
             after=earlier,
         )
-        earlier = [own_out]
-        other_out = lax.ppermute(sibling_out, "frame", siblings)
-        first_view = jnp.where(frame % 2 == 0, own_out, other_out)
-        second_view = jnp.where(frame % 2 == 0, other_out, own_out)
+        earlier = [finished]
         for p in range(pairs):
-            piece = jnp.stack([first_view[p, :cols], second_view[p, :cols]])
+            piece = finished[p, :, :cols]
             if (s, p) != (0, 0):
                 back = [(j, i) for i, j in chip_moves(s, p)]
                 piece = lax.ppermute(piece, both, back)
             results[s, p] = piece
-    strips = []
+    for group in (slots[:1] + slots[pairs:pairs + 1], slots[1:pairs] + slots[pairs + 1:]):
+        sent = jnp.stack([results[slot][1] for slot in group])
+        received = lax.ppermute(sent, "frame", siblings)
+        for index, slot in enumerate(group):
+            crossed[slot] = received[index]
+    strips = [[], []]
     for owner in range(owners):
-        strip = results[slots[0]]
+        own, other = results[slots[0]][0], crossed[slots[0]]
         for slot in slots[1:]:
-            strip = jnp.where(owner_at(*slot) == owner, results[slot], strip)
-        strips.append(strip)
-    return jnp.concatenate(strips, axis=1).reshape(video.shape)
+            here = owner_at(*slot) == owner
+            own = jnp.where(here, results[slot][0], own)
+            other = jnp.where(here, crossed[slot], other)
+        strips[0].append(jnp.where(frame % 2 == 0, own, other))
+        strips[1].append(jnp.where(frame % 2 == 0, other, own))
+    return jnp.stack([jnp.concatenate(strip) for strip in strips]).reshape(video.shape)
 
 
 def solution(mesh):

time: 41.6 us -> 40.7 us (0.978)
  waiting for transfers between devices: 11.1 us -> 10.3 us
    ppermute x3, waiting for transfers between devices: 5.53 us -> 4.23 us  [shards(): piece = lax.ppermute(piece, both, back)]
    ppermute x2, waiting for transfers between devices: 0.01 us -> 1.28 us  [shards(): received = lax.ppermute(sent, 'frame', siblings)]
    ppermute x2, waiting for transfers between devices: 0.92 us -> 0.01 us  [shards(): halos.append(lax.ppermute(section, 'rows', band_moves[s]))]
  transfers between devices with their start and end apart: 11 -> 11, of which waited for: 6 -> 7; matrix products, arithmetic and copies ran while one was open for 0% -> 0% of each run, Pallas kernels for 33% -> 33%
where the time goes in v5:
time: 40.7 us; the launch traced here: 40.6 us
  Pallas kernels  16.5 us (41%)
  starting transfers between devices  12.3 us (30%)
  waiting for transfers between devices  10.3 us (25%)
  other arithmetic  1.14 us (3%)
    pallas_call x6, Pallas kernels, kernel_call(): pl.pallas_call(ordered_body, in_specs=[pl.BlockSpec(memory_space=pltpu.SM...  12.1 us
    ppermute x3, waiting for transfers between devices, shards(): piece = lax.ppermute(piece, both, chip_moves(s, p))  4.76 us
    pallas_call x1, Pallas kernels, first_stereo(): pl.pallas_call(functools.partial(first_kernel, left, width // owners), in...  4.38 us
    ppermute x3, waiting for transfers between devices, shards(): piece = lax.ppermute(piece, both, back)  4.23 us
    ppermute x3, starting transfers between devices, shards(): piece = lax.ppermute(piece, both, chip_moves(s, p))  4.22 us
    ppermute x2, starting transfers between devices, shards(): halos.append(lax.ppermute(section, 'rows', band_moves[s]))  3.83 us
    ppermute x3, starting transfers between devices, shards(): piece = lax.ppermute(piece, both, back)  3.62 us
    ppermute x2, waiting for transfers between devices, shards(): received = lax.ppermute(sent, 'frame', siblings)  1.28 us
  transfers between devices with their start and end apart: 11, of which 7 were waited for; matrix products, arithmetic and copies ran while one was open for 0% of the time, Pallas kernels for 33%

profile of v5, /device:TPU:0, one launch (start us, length us, event | category | flops | bytes accessed | tf_op | source)
XLA Modules:
  0.0 40.6 jit_solution(14298293702433244591)
XLA Ops:
  0.0 0.5 %collective-permute-start = (bf16[2,1,1,480,256]{4,3,2,1,0:T(8,128)(2,1)}, bf16[2,1,1,480,256]{4,3,2,1,0:T(8,128)(2,1)S(1)}, u32[]{:S(2)}, u32[]{:S(2)}) collective-permute-start(bf16[2,1,1,480,256]{4,3,2,1,0:T(8,128)(2,1)} %refs_0_.1), channel_id=1, source_target_pairs={{0,8},{8,0},{16,24},{24,16},{1,9},{9,1},{17,25},{25,17},{2,10},{10... | collective-permute-start | bytes 1474568 | tf_op jit(solution)/shard_map/ppermute | solution.py:306
  0.5 4.4 %stereo.2 = (bf16[4,128,256]{2,1,0:T(8,128)(2,1)S(1)}, bf16[256,512]{1,0:T(8,128)(2,1)S(1)}, bf16[256,256]{1,0:T(8,128)(2,1)S(1)}, bf16[256,256]{1,0:T(8,128)(2,...) custom-call(s32[1]{0:T(128)} %bitcast.2.core_ref.refs_0_, ...), custom_call_target="tpu_custom_call" | custom-call | flops 2400000000 | bytes 2000000 | tf_op jit(solution)/shard_map/stereo/pallas_call | solution.py:93
  4.9 3.1 %stereo.3 = bf16[4,128,256]{2,1,0:T(8,128)(2,1)S(1)} custom-call(s32[1]{0:T(128)} %bitcast.2.core_ref.refs_0_, bf16[2,1,1,480,256]{4,3,2,1,0:T(8,128)(2,1)S(1)} %collective-permute-done.refs_1_, bf16[256,512]{1,0:T(8,128)(2,1)S(1)} %get-tuple-element.15.refs_2_, bf16[256,256]{1,0:T(8,128)(2,1)S(1)} %get-tuple-element.16.refs_3_, ...), custom_call_target="tpu_custom_call" | custom-call | flops 2400000000 | bytes 3000000 | tf_op jit(solution)/shard_map/stereo/pallas_call | solution.py:153
  8.1 2.6 %collective-permute-start.1 = (bf16[2,128,256]{2,1,0:T(8,128)(2,1)S(1)}, bf16[2,128,256]{2,1,0:T(8,128)(2,1)S(1)}, u32[]{:S(2)}, u32[]{:S(2)}) collective-permute-start(bf16[2,128,256]{2,1,0:T(8,128)(2,1)S(1)} %pad_maximum_fusion.1), channel_id=1, source_target_pairs={{0,16},{1,17},{2,18},{3,19},{4,20},{5,21},{6,22},{7,23},{8,24},{9,... | collective-permute-start | bytes 393224 | tf_op jit(solution)/shard_map/ppermute | solution.py:339
  10.7 1.6 %collective-permute-start.2 = (bf16[2,128,256]{2,1,0:T(8,128)(2,1)S(1)}, bf16[2,128,256]{2,1,0:T(8,128)(2,1)S(1)}, u32[]{:S(2)}, u32[]{:S(2)}) collective-permute-start(bf16[2,128,256]{2,1,0:T(8,128)(2,1)S(1)} %pad_maximum_fusion.2), channel_id=1, source_target_pairs={{0,17},{1,16},{2,19},{3,18},{4,21},{5,20},{6,23},{7,22},{8,25},{9,... | collective-permute-start | bytes 393224 | tf_op jit(solution)/shard_map/ppermute | solution.py:339
  12.3 0.1 collective-permute-start.3
  12.4 2.6 %collective-permute-done.1.refs_1_ = bf16[2,128,256]{2,1,0:T(8,128)(2,1)S(1)} collective-permute-done((bf16[2,128,256]{2,1,0:T(8,128)(2,1)S(1)}, bf16[2,128,256]{2,1,0:T(8,128)(2,1)S(1)}, u32[]{:S(2)}, u32[]{:S(2)}) %collective-permute-start.1) | collective-permute-done | bytes 131104 | tf_op jit(solution)/shard_map/ppermute | solution.py:339
  15.0 1.3 %temporal.2.refs_5_.refs_1_ = bf16[2,2,128,256]{3,2,1,0:T(8,128)(2,1)S(1)} custom-call(bf16[2,128,256]{2,1,0:T(8,128)(2,1)S(1)} %pad_maximum_fusion.refs_0_, bf16[2,128,256]{2,1,0:T(8,128)(2,1)S(1)} %collective-permute-done.1.refs_1_, bf16[256,512]{1,0:T(8,128)(2,1)S(1)} %get-tuple-element.18.refs_2_, bf16[256,256]{1,0:T(8,128)(2,1)S(1)} %get-tuple-element.19.refs_3_, ...), custom_call_target="tpu_custom_call" | custom-call | flops 1000000000 | bytes 3000000 | tf_op jit(solution)/shard_map/temporal/pallas_call | solution.py:153
  16.3 0.0 copy-start
  16.3 0.0 copy-start.1
  16.3 0.0 copy-start.2
  16.3 2.0 %collective-permute-start.4 = (bf16[2,2,128,256]{3,2,1,0:T(8,128)(2,1)S(1)}, bf16[2,2,128,256]{3,2,1,0:T(8,128)(2,1)S(1)}, u32[]{:S(2)}, u32[]{:S(2)}) collective-permute-start(bf16[2,2,128,256]{3,2,1,0:T(8,128)(2,1)S(1)} %temporal.2.refs_5_.refs_1_), channel_id=1, source_target_pairs={{0,1},{1,3},{2,0},{3,5},{4,2},{5,7},{6,4},{7,6},{8,9},{9,11},{10,8... | collective-permute-start | bytes 786440 | tf_op jit(solution)/shard_map/ppermute | solution.py:355
  18.3 0.6 %collective-permute-done.2.refs_0_ = bf16[2,128,256]{2,1,0:T(8,128)(2,1)S(1)} collective-permute-done((bf16[2,128,256]{2,1,0:T(8,128)(2,1)S(1)}, bf16[2,128,256]{2,1,0:T(8,128)(2,1)S(1)}, u32[]{:S(2)}, u32[]{:S(2)}) %collective-permute-start.2) | collective-permute-done | bytes 131104 | tf_op jit(solution)/shard_map/ppermute | solution.py:339
  19.0 1.5 %collective-permute-done.3.refs_1_ = bf16[2,128,256]{2,1,0:T(8,128)(2,1)S(1)} collective-permute-done((bf16[2,128,256]{2,1,0:T(8,128)(2,1)S(1)}, bf16[2,128,256]{2,1,0:T(8,128)(2,1)S(1)}, u32[]{:S(2)}, u32[]{:S(2)}) %collective-permute-start.3) | collective-permute-done | bytes 131104 | tf_op jit(solution)/shard_map/ppermute | solution.py:339
  20.5 1.3 %temporal.3.refs_2_ = bf16[2,2,128,256]{3,2,1,0:T(8,128)(2,1)S(1)} custom-call(bf16[2,128,256]{2,1,0:T(8,128)(2,1)S(1)} %collective-permute-done.2.refs_0_, bf16[2,128,256]{2,1,0:T(8,128)(2,1)S(1)} %collective-permute-done.3.refs_1_, bf16[256,512]{1,0:T(8,128)(2,1)S(1)} %get-tuple-element.18.refs_2_, bf16[256,256]{1,0:T(8,128)(2,1)S(1)} %get-tuple-element.19.refs_3_, ...), custom_call_target="tpu_custom_call" | custom-call | flops 1000000000 | bytes 3000000 | tf_op jit(solution)/shard_map/temporal/pallas_call | solution.py:153
  21.8 1.8 %collective-permute-start.7 = (bf16[2,2,128,256]{3,2,1,0:T(8,128)(2,1)S(1)}, bf16[2,2,128,256]{3,2,1,0:T(8,128)(2,1)S(1)}, u32[]{:S(2)}, u32[]{:S(2)}) collective-permute-start(bf16[2,2,128,256]{3,2,1,0:T(8,128)(2,1)S(1)} %temporal.3.refs_2_), channel_id=1, source_target_pairs={{0,2},{1,0},{2,4},{3,1},{4,6},{5,3},{6,7},{7,5},{8,10},{9,8},{10,1... | collective-permute-start | bytes 786440 | tf_op jit(solution)/shard_map/ppermute | solution.py:355
  23.6 3.3 %inner.1 = (f32[2,2,128,256]{3,2,1,0:T(8,128)S(1)}, f32[2,2,128,256]{3,2,1,0:T(8,128)S(1)}) custom-call(s32[1]{0:T(128)} %bitcast.refs_0_, bf16[2,2,128,256]{3,2,1,0:T(8,128)(2,1)S(1)} %temporal.2.refs_5_.refs_1_, bf16[2,2,128,256]{3,2,1,0:T(8,128)(2,1)S(1)} %temporal.3.refs_2_, bf16[256,1024]{1,0:T(8,128)(2,1)S(1)} %copy-done, ...), custom_call_target="tpu_custom_call" | custom-call | flops 4000000000 | bytes 3000000 | tf_op jit(solution)/shard_map/inner/pallas_call | solution.py:153
  26.9 0.0 collective-permute-done.4.refs_3_
  26.9 1.6 %outer.2.refs_7_ = bf16[2,2,128,256]{3,2,1,0:T(8,128)(2,1)S(1)} custom-call(s32[1]{0:T(128)} %bitcast.refs_0_, s32[1]{0:T(128)} %bitcast.1.refs_1_, f32[2,2,128,256]{3,2,1,0:T(8,128)S(1)} %get-tuple-element.21.refs_2_, bf16[2,2,128,256]{3,2,1,0:T(8,128)(2,1)S(1)} %collective-permute-done.4.refs_3_, bf16[256,1024]{1,0:T(8,128)(2,1)S(1)} %copy-done, ...), custom_call_target="tpu_custom_call" | custom-call | flops 1000000000 | bytes 3000000 | tf_op jit(solution)/shard_map/outer/pallas_call | solution.py:153
  28.5 0.5 %collective-permute-start.6 = (bf16[2,120,256]{2,1,0:T(8,128)(2,1)S(1)}, bf16[2,120,256]{2,1,0:T(8,128)(2,1)S(1)}, u32[]{:S(2)}, u32[]{:S(2)}) collective-permute-start(bf16[2,120,256]{2,1,0:T(8,128)(2,1)S(1)} %get-tuple-element.36), channel_id=1, source_target_pairs={{1,0},{0,1},{3,2},{2,3},{5,4},{4,5},{7,6},{6,7},{9,8},{8,9},{11,10... | collective-permute-start | bytes 368648 | tf_op jit(solution)/shard_map/ppermute | solution.py:387
  29.0 2.5 %collective-permute-start.5 = (bf16[2,120,256]{2,1,0:T(8,128)(2,1)S(1)}, bf16[2,120,256]{2,1,0:T(8,128)(2,1)S(1)}, u32[]{:S(2)}, u32[]{:S(2)}) collective-permute-start(bf16[2,120,256]{2,1,0:T(8,128)(2,1)S(1)} %get-tuple-element.35), channel_id=1, source_target_pairs={{17,0},{16,1},{19,2},{18,3},{21,4},{20,5},{23,6},{22,7},{25,8},{24... | collective-permute-start | bytes 368648 | tf_op jit(solution)/shard_map/ppermute | solution.py:387
  31.5 0.0 collective-permute-done.7.refs_3_
  31.5 1.6 %outer.3 = bf16[2,2,128,256]{3,2,1,0:T(8,128)(2,1)S(1)} custom-call(s32[1]{0:T(128)} %bitcast.refs_0_, s32[1]{0:T(128)} %bitcast.7.refs_1_, f32[2,2,128,256]{3,2,1,0:T(8,128)S(1)} %get-tuple-element.22.refs_2_, bf16[2,2,128,256]{3,2,1,0:T(8,128)(2,1)S(1)} %collective-permute-done.7.refs_3_, bf16[256,1024]{1,0:T(8,128)(2,1)S(1)} %copy-done, ...), custom_call_target="tpu_custom_call" | custom-call | flops 1000000000 | bytes 3000000 | tf_op jit(solution)/shard_map/outer/pallas_call | solution.py:153
  33.1 0.6 %collective-permute-start.8 = (bf16[2,120,256]{2,1,0:T(8,128)(2,1)S(1)}, bf16[2,120,256]{2,1,0:T(8,128)(2,1)S(1)}, u32[]{:S(2)}, u32[]{:S(2)}) collective-permute-start(bf16[2,120,256]{2,1,0:T(8,128)(2,1)S(1)} %slice_bitcast_fusion), channel_id=1, source_target_pairs={{16,0},{17,1},{18,2},{19,3},{20,4},{21,5},{22,6},{23,7},{24,8},{25... | collective-permute-start | bytes 368648 | tf_op jit(solution)/shard_map/ppermute | solution.py:387
  33.7 1.3 %collective-permute-done.6 = bf16[2,120,256]{2,1,0:T(8,128)(2,1)S(1)} collective-permute-done((bf16[2,120,256]{2,1,0:T(8,128)(2,1)S(1)}, bf16[2,120,256]{2,1,0:T(8,128)(2,1)S(1)}, u32[]{:S(2)}, u32[]{:S(2)}) %collective-permute-start.6) | collective-permute-done | bytes 122912 | tf_op jit(solution)/shard_map/ppermute | solution.py:387
  35.1 0.1 collective-permute-start.10
  35.2 0.5 %collective-permute-done.5 = bf16[2,120,256]{2,1,0:T(8,128)(2,1)S(1)} collective-permute-done((bf16[2,120,256]{2,1,0:T(8,128)(2,1)S(1)}, bf16[2,120,256]{2,1,0:T(8,128)(2,1)S(1)}, u32[]{:S(2)}, u32[]{:S(2)}) %collective-permute-start.5) | collective-permute-done | bytes 122912 | tf_op jit(solution)/shard_map/ppermute | solution.py:387
  35.6 2.4 %collective-permute-done.8 = bf16[2,120,256]{2,1,0:T(8,128)(2,1)S(1)} collective-permute-done((bf16[2,120,256]{2,1,0:T(8,128)(2,1)S(1)}, bf16[2,120,256]{2,1,0:T(8,128)(2,1)S(1)}, u32[]{:S(2)}, u32[]{:S(2)}) %collective-permute-start.8) | collective-permute-done | bytes 122912 | tf_op jit(solution)/shard_map/ppermute | solution.py:387
  38.1 0.1 collective-permute-start.9
  38.2 0.0 collective-permute-done.10
  38.2 1.3 %collective-permute-done.9 = bf16[2,120,256]{2,1,0:T(8,128)(2,1)S(1)} collective-permute-done((bf16[2,120,256]{2,1,0:T(8,128)(2,1)S(1)}, bf16[2,120,256]{2,1,0:T(8,128)(2,1)S(1)}, u32[]{:S(2)}, u32[]{:S(2)}) %collective-permute-start.9) | collective-permute-done | bytes 122912 | tf_op jit(solution)/shard_map/ppermute | solution.py:391
  39.7 0.8 %maximum_bitcast_fusion = bf16[2,1,1,480,256]{4,3,2,1,0:T(8,128)(2,1)} fusion(bf16[1,480,256]{2,1,0:T(8,128)(2,1)S(1)} %maximum_bitcast_fusion.2, bf16[1,480,256]{2,1,0:T(8,128)(2,1)S(1)} %maximum_bitcast_fusion.1), kind=kLoop, calls=%fused_computation | loop fusion | flops 245760 | bytes 983040 | tf_op jit(solution)/shard_map/reshape | solution.py:403
  (26 shorter events, 0.4 us)
Async XLA Ops:
  0.0 4.9 %collective-permute-start = (bf16[2,1,1,480,256]{4,3,2,1,0:T(8,128)(2,1)}, bf16[2,1,1,480,256]{4,3,2,1,0:T(8,128)(2,1)S(1)}, u32[]{:S(2)}, u32[]{:S(2)}) collective-permute-start(bf16[2,1,1,480,256]{4,3,2,1,0:T(8,128)(2,1)} %refs_0_.1), channel_id=1, source_target_pairs={{0,8},{8,0},{16,24},{24,16},{1,9},{9,1},{17,25},{25,17},{2,10},{10... | collective-permute-start | bytes 1474568 | tf_op jit(solution)/shard_map/ppermute | solution.py:306
  8.1 6.9 %collective-permute-start.1 = (bf16[2,128,256]{2,1,0:T(8,128)(2,1)S(1)}, bf16[2,128,256]{2,1,0:T(8,128)(2,1)S(1)}, u32[]{:S(2)}, u32[]{:S(2)}) collective-permute-start(bf16[2,128,256]{2,1,0:T(8,128)(2,1)S(1)} %pad_maximum_fusion.1), channel_id=1, source_target_pairs={{0,16},{1,17},{2,18},{3,19},{4,20},{5,21},{6,22},{7,23},{8,24},{9,... | collective-permute-start | bytes 393224 | tf_op jit(solution)/shard_map/ppermute | solution.py:339
  10.7 8.3 %collective-permute-start.2 = (bf16[2,128,256]{2,1,0:T(8,128)(2,1)S(1)}, bf16[2,128,256]{2,1,0:T(8,128)(2,1)S(1)}, u32[]{:S(2)}, u32[]{:S(2)}) collective-permute-start(bf16[2,128,256]{2,1,0:T(8,128)(2,1)S(1)} %pad_maximum_fusion.2), channel_id=1, source_target_pairs={{0,17},{1,16},{2,19},{3,18},{4,21},{5,20},{6,23},{7,22},{8,25},{9,... | collective-permute-start | bytes 393224 | tf_op jit(solution)/shard_map/ppermute | solution.py:339
  12.3 8.2 %collective-permute-start.3 = (bf16[2,128,256]{2,1,0:T(8,128)(2,1)S(1)}, bf16[2,128,256]{2,1,0:T(8,128)(2,1)S(1)}, u32[]{:S(2)}, u32[]{:S(2)}) collective-permute-start(bf16[2,128,256]{2,1,0:T(8,128)(2,1)S(1)} %pad_maximum_fusion.3), channel_id=1, source_target_pairs={{0,1},{1,0},{2,3},{3,2},{4,5},{5,4},{6,7},{7,6},{8,9},{9,8},{10,11... | collective-permute-start | bytes 393224 | tf_op jit(solution)/shard_map/ppermute | solution.py:339
  16.3 7.3 %copy-start = (bf16[256,1024]{1,0:T(8,128)(2,1)S(1)}, bf16[256,1024]{1,0:T(8,128)(2,1)}, u32[]{:S(2)}) copy-start(bf16[256,1024]{1,0:T(8,128)(2,1)} %refs_4_.7) | copy-start | bytes 1572868
  16.3 7.3 %copy-start.1 = (bf16[1024,256]{1,0:T(8,128)(2,1)S(1)}, bf16[1024,256]{1,0:T(8,128)(2,1)}, u32[]{:S(2)}) copy-start(bf16[1024,256]{1,0:T(8,128)(2,1)} %refs_6_.5) | copy-start | bytes 1572868
  16.3 7.3 %copy-start.2 = (bf16[3,3,1024]{2,1,0:T(4,128)(2,1)S(1)}, bf16[3,3,1024]{2,1,0:T(4,128)(2,1)}, u32[]{:S(2)}) copy-start(bf16[3,3,1024]{2,1,0:T(4,128)(2,1)} %refs_5_.7) | copy-start | bytes 55300
  16.3 10.5 %collective-permute-start.4 = (bf16[2,2,128,256]{3,2,1,0:T(8,128)(2,1)S(1)}, bf16[2,2,128,256]{3,2,1,0:T(8,128)(2,1)S(1)}, u32[]{:S(2)}, u32[]{:S(2)}) collective-permute-start(bf16[2,2,128,256]{3,2,1,0:T(8,128)(2,1)S(1)} %temporal.2.refs_5_.refs_1_), channel_id=1, source_target_pairs={{0,1},{1,3},{2,0},{3,5},{4,2},{5,7},{6,4},{7,6},{8,9},{9,11},{10,8... | collective-permute-start | bytes 786440 | tf_op jit(solution)/shard_map/ppermute | solution.py:355
  21.8 9.8 %collective-permute-start.7 = (bf16[2,2,128,256]{3,2,1,0:T(8,128)(2,1)S(1)}, bf16[2,2,128,256]{3,2,1,0:T(8,128)(2,1)S(1)}, u32[]{:S(2)}, u32[]{:S(2)}) collective-permute-start(bf16[2,2,128,256]{3,2,1,0:T(8,128)(2,1)S(1)} %temporal.3.refs_2_), channel_id=1, source_target_pairs={{0,2},{1,0},{2,4},{3,1},{4,6},{5,3},{6,7},{7,5},{8,10},{9,8},{10,1... | collective-permute-start | bytes 786440 | tf_op jit(solution)/shard_map/ppermute | solution.py:355
  28.5 6.6 %collective-permute-start.6 = (bf16[2,120,256]{2,1,0:T(8,128)(2,1)S(1)}, bf16[2,120,256]{2,1,0:T(8,128)(2,1)S(1)}, u32[]{:S(2)}, u32[]{:S(2)}) collective-permute-start(bf16[2,120,256]{2,1,0:T(8,128)(2,1)S(1)} %get-tuple-element.36), channel_id=1, source_target_pairs={{1,0},{0,1},{3,2},{2,3},{5,4},{4,5},{7,6},{6,7},{9,8},{8,9},{11,10... | collective-permute-start | bytes 368648 | tf_op jit(solution)/shard_map/ppermute | solution.py:387
  29.0 6.6 %collective-permute-start.5 = (bf16[2,120,256]{2,1,0:T(8,128)(2,1)S(1)}, bf16[2,120,256]{2,1,0:T(8,128)(2,1)S(1)}, u32[]{:S(2)}, u32[]{:S(2)}) collective-permute-start(bf16[2,120,256]{2,1,0:T(8,128)(2,1)S(1)} %get-tuple-element.35), channel_id=1, source_target_pairs={{17,0},{16,1},{19,2},{18,3},{21,4},{20,5},{23,6},{22,7},{25,8},{24... | collective-permute-start | bytes 368648 | tf_op jit(solution)/shard_map/ppermute | solution.py:387
  33.1 4.9 %collective-permute-start.8 = (bf16[2,120,256]{2,1,0:T(8,128)(2,1)S(1)}, bf16[2,120,256]{2,1,0:T(8,128)(2,1)S(1)}, u32[]{:S(2)}, u32[]{:S(2)}) collective-permute-start(bf16[2,120,256]{2,1,0:T(8,128)(2,1)S(1)} %slice_bitcast_fusion), channel_id=1, source_target_pairs={{16,0},{17,1},{18,2},{19,3},{20,4},{21,5},{22,6},{23,7},{24,8},{25... | collective-permute-start | bytes 368648 | tf_op jit(solution)/shard_map/ppermute | solution.py:387
  35.1 3.1 %collective-permute-start.10 = (bf16[2,120,256]{2,1,0:T(8,128)(2,1)S(1)}, bf16[2,120,256]{2,1,0:T(8,128)(2,1)S(1)}, u32[]{:S(2)}, u32[]{:S(2)}) collective-permute-start(bf16[2,120,256]{2,1,0:T(8,128)(2,1)S(1)} %pad_maximum_fusion.5), channel_id=1, source_target_pairs={{0,8},{8,0},{16,24},{24,16},{1,9},{9,1},{17,25},{25,17},{2,10},{10... | collective-permute-start | bytes 368648 | tf_op jit(solution)/shard_map/ppermute | solution.py:391
  38.1 1.4 %collective-permute-start.9 = (bf16[2,120,256]{2,1,0:T(8,128)(2,1)S(1)}, bf16[2,120,256]{2,1,0:T(8,128)(2,1)S(1)}, u32[]{:S(2)}, u32[]{:S(2)}) collective-permute-start(bf16[2,120,256]{2,1,0:T(8,128)(2,1)S(1)} %pad_maximum_fusion.4), channel_id=1, source_target_pairs={{0,8},{8,0},{16,24},{24,16},{1,9},{9,1},{17,25},{25,17},{2,10},{10... | collective-permute-start | bytes 368648 | tf_op jit(solution)/shard_map/ppermute | solution.py:391

commit v6 on v5

--- a/solution.py
+++ b/solution.py
@@ -221,11 +221,11 @@
 
 
 def outer_kernel(
-    left, slot, side_ref, edge_ref, partial_ref, halo_ref, up_ref, mix_ref, down_ref, out_ref
+    left, slot, chosen, side_ref, edge_ref, partial_ref, halo_ref, up_ref, mix_ref, down_ref, out_ref
 ):
-    pairs, pair_size, window, channels = partial_ref.shape
+    _, pair_size, window, channels = partial_ref.shape
     tap = 2 * side_ref[0] if slot == 0 else 2 - 2 * side_ref[0]
-    for pair in range(pairs):
+    for place, pair in enumerate(chosen):
         rows = halo_ref[pair].reshape(pair_size * window, channels).astype(jnp.float32)
         normed = layer_norm(jnp.where(edge_ref[0] == 1, jnp.zeros_like(rows), rows))
         total = partial_ref[pair].reshape(pair_size * window, channels)
@@ -246,7 +246,7 @@
             total = total + dot_dims(jnp.concatenate(mixed, axis=0), down_ref[lanes], 1, 0)
         for member in range(pair_size):
             shifted = pltpu.roll(total[member * window : (member + 1) * window], window - left, 0)
-            out_ref[pair, member] = shifted.astype(jnp.bfloat16)
+            out_ref[place, member] = shifted.astype(jnp.bfloat16)
 
 
 def shards(
@@ -365,12 +365,13 @@
         mlp_down,
     )
     results, crossed, earlier = {}, {}, []
-    for s in (1, 0):
+    calls = [(1, list(range(pairs))), (0, list(range(1, pairs))), (0, [0])]
+    for s, chosen in calls:
         finished = kernel_call(
-            functools.partial(outer_kernel, left, s),
+            functools.partial(outer_kernel, left, s, chosen),
             "outer",
-            1_000_000_000,
-            jax.ShapeDtypeStruct(shape, jnp.bfloat16),
+            500_000_000 * len(chosen),
+            jax.ShapeDtypeStruct((len(chosen),) + shape[1:], jnp.bfloat16),
             (side_arg, edge_args[1 - s]),
             partials[s],
             halos[1 - s],
@@ -380,8 +381,8 @@
             after=earlier,
         )
         earlier = [finished]
-        for p in range(pairs):
-            piece = finished[p, :, :cols]
+        for place, p in enumerate(chosen):
+            piece = finished[place, :, :cols]
             if (s, p) != (0, 0):
                 back = [(j, i) for i, j in chip_moves(s, p)]
                 piece = lax.ppermute(piece, both, back)

time: 40.7 us -> 40.1 us (0.985)
  waiting for transfers between devices: 10.3 us -> 9.34 us
    ppermute x3, waiting for transfers between devices: 4.23 us -> 3.29 us  [shards(): piece = lax.ppermute(piece, both, back)]
    pallas_call x6 -> x7, Pallas kernels: 12.1 us -> 12.4 us  [kernel_call(): pl.pallas_call(ordered_body, in_specs=[pl.BlockSpec(memory_space=pltpu.SM...]
  transfers between devices with their start and end apart: 11 -> 11, of which waited for: 7 -> 7; matrix products, arithmetic and copies ran while one was open for 0% -> 0% of each run, Pallas kernels for 33% -> 34%
where the time goes in v6:
time: 40.1 us; the launch traced here: 40 us
  Pallas kernels  16.8 us (42%)
  starting transfers between devices  12.3 us (31%)
  waiting for transfers between devices  9.34 us (23%)
  other arithmetic  1.14 us (3%)
    pallas_call x7, Pallas kernels, kernel_call(): pl.pallas_call(ordered_body, in_specs=[pl.BlockSpec(memory_space=pltpu.SM...  12.4 us
    ppermute x3, waiting for transfers between devices, shards(): piece = lax.ppermute(piece, both, chip_moves(s, p))  4.76 us
    pallas_call x1, Pallas kernels, first_stereo(): pl.pallas_call(functools.partial(first_kernel, left, width // owners), in...  4.38 us
    ppermute x3, starting transfers between devices, shards(): piece = lax.ppermute(piece, both, chip_moves(s, p))  4.22 us
    ppermute x2, starting transfers between devices, shards(): halos.append(lax.ppermute(section, 'rows', band_moves[s]))  3.84 us
    ppermute x3, starting transfers between devices, shards(): piece = lax.ppermute(piece, both, back)  3.62 us
    ppermute x3, waiting for transfers between devices, shards(): piece = lax.ppermute(piece, both, back)  3.29 us
    ppermute x2, waiting for transfers between devices, shards(): received = lax.ppermute(sent, 'frame', siblings)  1.28 us
  transfers between devices with their start and end apart: 11, of which 7 were waited for; matrix products, arithmetic and copies ran while one was open for 0% of the time, Pallas kernels for 34%

profile of v6, /device:TPU:0, one launch (start us, length us, event | category | flops | bytes accessed | tf_op | source)
XLA Modules:
  0.0 40.0 jit_solution(6212365070555186710)
XLA Ops:
  0.0 0.5 %collective-permute-start = (bf16[2,1,1,480,256]{4,3,2,1,0:T(8,128)(2,1)}, bf16[2,1,1,480,256]{4,3,2,1,0:T(8,128)(2,1)S(1)}, u32[]{:S(2)}, u32[]{:S(2)}) collective-permute-start(bf16[2,1,1,480,256]{4,3,2,1,0:T(8,128)(2,1)} %refs_0_.1), channel_id=1, source_target_pairs={{0,8},{8,0},{16,24},{24,16},{1,9},{9,1},{17,25},{25,17},{2,10},{10... | collective-permute-start | bytes 1474568 | tf_op jit(solution)/shard_map/ppermute | solution.py:306
  0.5 4.4 %stereo.2 = (bf16[4,128,256]{2,1,0:T(8,128)(2,1)S(1)}, bf16[256,512]{1,0:T(8,128)(2,1)S(1)}, bf16[256,256]{1,0:T(8,128)(2,1)S(1)}, bf16[256,256]{1,0:T(8,128)(2,...) custom-call(s32[1]{0:T(128)} %bitcast.2.core_ref.refs_0_, ...), custom_call_target="tpu_custom_call" | custom-call | flops 2400000000 | bytes 2000000 | tf_op jit(solution)/shard_map/stereo/pallas_call | solution.py:93
  4.9 0.0 collective-permute-done.refs_1_
  4.9 3.1 %stereo.3 = bf16[4,128,256]{2,1,0:T(8,128)(2,1)S(1)} custom-call(s32[1]{0:T(128)} %bitcast.2.core_ref.refs_0_, bf16[2,1,1,480,256]{4,3,2,1,0:T(8,128)(2,1)S(1)} %collective-permute-done.refs_1_, bf16[256,512]{1,0:T(8,128)(2,1)S(1)} %get-tuple-element.15.refs_2_, bf16[256,256]{1,0:T(8,128)(2,1)S(1)} %get-tuple-element.16.refs_3_, ...), custom_call_target="tpu_custom_call" | custom-call | flops 2400000000 | bytes 3000000 | tf_op jit(solution)/shard_map/stereo/pallas_call | solution.py:153
  8.1 2.6 %collective-permute-start.1 = (bf16[2,128,256]{2,1,0:T(8,128)(2,1)S(1)}, bf16[2,128,256]{2,1,0:T(8,128)(2,1)S(1)}, u32[]{:S(2)}, u32[]{:S(2)}) collective-permute-start(bf16[2,128,256]{2,1,0:T(8,128)(2,1)S(1)} %pad_maximum_fusion.1), channel_id=1, source_target_pairs={{0,16},{1,17},{2,18},{3,19},{4,20},{5,21},{6,22},{7,23},{8,24},{9,... | collective-permute-start | bytes 393224 | tf_op jit(solution)/shard_map/ppermute | solution.py:339
  10.7 1.6 %collective-permute-start.2 = (bf16[2,128,256]{2,1,0:T(8,128)(2,1)S(1)}, bf16[2,128,256]{2,1,0:T(8,128)(2,1)S(1)}, u32[]{:S(2)}, u32[]{:S(2)}) collective-permute-start(bf16[2,128,256]{2,1,0:T(8,128)(2,1)S(1)} %pad_maximum_fusion.2), channel_id=1, source_target_pairs={{0,17},{1,16},{2,19},{3,18},{4,21},{5,20},{6,23},{7,22},{8,25},{9,... | collective-permute-start | bytes 393224 | tf_op jit(solution)/shard_map/ppermute | solution.py:339
  12.2 0.1 collective-permute-start.3
  12.4 2.6 %collective-permute-done.1.refs_1_ = bf16[2,128,256]{2,1,0:T(8,128)(2,1)S(1)} collective-permute-done((bf16[2,128,256]{2,1,0:T(8,128)(2,1)S(1)}, bf16[2,128,256]{2,1,0:T(8,128)(2,1)S(1)}, u32[]{:S(2)}, u32[]{:S(2)}) %collective-permute-start.1) | collective-permute-done | bytes 131104 | tf_op jit(solution)/shard_map/ppermute | solution.py:339
  15.0 1.3 %temporal.2.refs_5_.refs_1_ = bf16[2,2,128,256]{3,2,1,0:T(8,128)(2,1)S(1)} custom-call(bf16[2,128,256]{2,1,0:T(8,128)(2,1)S(1)} %pad_maximum_fusion.refs_0_, bf16[2,128,256]{2,1,0:T(8,128)(2,1)S(1)} %collective-permute-done.1.refs_1_, bf16[256,512]{1,0:T(8,128)(2,1)S(1)} %get-tuple-element.18.refs_2_, bf16[256,256]{1,0:T(8,128)(2,1)S(1)} %get-tuple-element.19.refs_3_, ...), custom_call_target="tpu_custom_call" | custom-call | flops 1000000000 | bytes 3000000 | tf_op jit(solution)/shard_map/temporal/pallas_call | solution.py:153
  16.3 0.0 copy-start
  16.3 0.0 copy-start.1
  16.3 0.0 copy-start.2
  16.3 2.0 %collective-permute-start.4 = (bf16[2,2,128,256]{3,2,1,0:T(8,128)(2,1)S(1)}, bf16[2,2,128,256]{3,2,1,0:T(8,128)(2,1)S(1)}, u32[]{:S(2)}, u32[]{:S(2)}) collective-permute-start(bf16[2,2,128,256]{3,2,1,0:T(8,128)(2,1)S(1)} %temporal.2.refs_5_.refs_1_), channel_id=1, source_target_pairs={{0,1},{1,3},{2,0},{3,5},{4,2},{5,7},{6,4},{7,6},{8,9},{9,11},{10,8... | collective-permute-start | bytes 786440 | tf_op jit(solution)/shard_map/ppermute | solution.py:355
  18.3 0.6 %collective-permute-done.2.refs_0_ = bf16[2,128,256]{2,1,0:T(8,128)(2,1)S(1)} collective-permute-done((bf16[2,128,256]{2,1,0:T(8,128)(2,1)S(1)}, bf16[2,128,256]{2,1,0:T(8,128)(2,1)S(1)}, u32[]{:S(2)}, u32[]{:S(2)}) %collective-permute-start.2) | collective-permute-done | bytes 131104 | tf_op jit(solution)/shard_map/ppermute | solution.py:339
  18.9 1.5 %collective-permute-done.3.refs_1_ = bf16[2,128,256]{2,1,0:T(8,128)(2,1)S(1)} collective-permute-done((bf16[2,128,256]{2,1,0:T(8,128)(2,1)S(1)}, bf16[2,128,256]{2,1,0:T(8,128)(2,1)S(1)}, u32[]{:S(2)}, u32[]{:S(2)}) %collective-permute-start.3) | collective-permute-done | bytes 131104 | tf_op jit(solution)/shard_map/ppermute | solution.py:339
  20.5 1.3 %temporal.3.refs_2_ = bf16[2,2,128,256]{3,2,1,0:T(8,128)(2,1)S(1)} custom-call(bf16[2,128,256]{2,1,0:T(8,128)(2,1)S(1)} %collective-permute-done.2.refs_0_, bf16[2,128,256]{2,1,0:T(8,128)(2,1)S(1)} %collective-permute-done.3.refs_1_, bf16[256,512]{1,0:T(8,128)(2,1)S(1)} %get-tuple-element.18.refs_2_, bf16[256,256]{1,0:T(8,128)(2,1)S(1)} %get-tuple-element.19.refs_3_, ...), custom_call_target="tpu_custom_call" | custom-call | flops 1000000000 | bytes 3000000 | tf_op jit(solution)/shard_map/temporal/pallas_call | solution.py:153
  21.7 1.8 %collective-permute-start.7 = (bf16[2,2,128,256]{3,2,1,0:T(8,128)(2,1)S(1)}, bf16[2,2,128,256]{3,2,1,0:T(8,128)(2,1)S(1)}, u32[]{:S(2)}, u32[]{:S(2)}) collective-permute-start(bf16[2,2,128,256]{3,2,1,0:T(8,128)(2,1)S(1)} %temporal.3.refs_2_), channel_id=1, source_target_pairs={{0,2},{1,0},{2,4},{3,1},{4,6},{5,3},{6,7},{7,5},{8,10},{9,8},{10,1... | collective-permute-start | bytes 786440 | tf_op jit(solution)/shard_map/ppermute | solution.py:355
  23.6 3.3 %inner.1 = (f32[2,2,128,256]{3,2,1,0:T(8,128)S(1)}, f32[2,2,128,256]{3,2,1,0:T(8,128)S(1)}) custom-call(s32[1]{0:T(128)} %bitcast.refs_0_, bf16[2,2,128,256]{3,2,1,0:T(8,128)(2,1)S(1)} %temporal.2.refs_5_.refs_1_, bf16[2,2,128,256]{3,2,1,0:T(8,128)(2,1)S(1)} %temporal.3.refs_2_, bf16[256,1024]{1,0:T(8,128)(2,1)S(1)} %copy-done, ...), custom_call_target="tpu_custom_call" | custom-call | flops 4000000000 | bytes 3000000 | tf_op jit(solution)/shard_map/inner/pallas_call | solution.py:153
  26.9 0.0 collective-permute-done.4.refs_3_
  26.9 1.6 %outer.3.refs_7_ = bf16[2,2,128,256]{3,2,1,0:T(8,128)(2,1)S(1)} custom-call(s32[1]{0:T(128)} %bitcast.refs_0_, s32[1]{0:T(128)} %bitcast.1.refs_1_, f32[2,2,128,256]{3,2,1,0:T(8,128)S(1)} %get-tuple-element.21.refs_2_, bf16[2,2,128,256]{3,2,1,0:T(8,128)(2,1)S(1)} %collective-permute-done.4.refs_3_, bf16[256,1024]{1,0:T(8,128)(2,1)S(1)} %copy-done, ...), custom_call_target="tpu_custom_call" | custom-call | flops 1000000000 | bytes 3000000 | tf_op jit(solution)/shard_map/outer/pallas_call | solution.py:153
  28.5 0.5 %collective-permute-start.6 = (bf16[2,120,256]{2,1,0:T(8,128)(2,1)S(1)}, bf16[2,120,256]{2,1,0:T(8,128)(2,1)S(1)}, u32[]{:S(2)}, u32[]{:S(2)}) collective-permute-start(bf16[2,120,256]{2,1,0:T(8,128)(2,1)S(1)} %get-tuple-element.36), channel_id=1, source_target_pairs={{1,0},{0,1},{3,2},{2,3},{5,4},{4,5},{7,6},{6,7},{9,8},{8,9},{11,10... | collective-permute-start | bytes 368648 | tf_op jit(solution)/shard_map/ppermute | solution.py:388
  29.0 2.5 %collective-permute-start.5 = (bf16[2,120,256]{2,1,0:T(8,128)(2,1)S(1)}, bf16[2,120,256]{2,1,0:T(8,128)(2,1)S(1)}, u32[]{:S(2)}, u32[]{:S(2)}) collective-permute-start(bf16[2,120,256]{2,1,0:T(8,128)(2,1)S(1)} %get-tuple-element.35), channel_id=1, source_target_pairs={{17,0},{16,1},{19,2},{18,3},{21,4},{20,5},{23,6},{22,7},{25,8},{24... | collective-permute-start | bytes 368648 | tf_op jit(solution)/shard_map/ppermute | solution.py:388
  31.5 0.9 %outer.4.refs_7_ = bf16[1,2,128,256]{3,2,1,0:T(8,128)(2,1)S(1)} custom-call(s32[1]{0:T(128)} %bitcast.refs_0_, s32[1]{0:T(128)} %bitcast.7.refs_1_, f32[2,2,128,256]{3,2,1,0:T(8,128)S(1)} %get-tuple-element.22.refs_2_, bf16[2,2,128,256]{3,2,1,0:T(8,128)(2,1)S(1)} %collective-permute-done.7.refs_3_, bf16[256,1024]{1,0:T(8,128)(2,1)S(1)} %copy-done, ...), custom_call_target="tpu_custom_call" | custom-call | flops 500000000 | bytes 3000000 | tf_op jit(solution)/shard_map/outer/pallas_call | solution.py:153
  32.5 0.6 %collective-permute-start.8 = (bf16[2,120,256]{2,1,0:T(8,128)(2,1)S(1)}, bf16[2,120,256]{2,1,0:T(8,128)(2,1)S(1)}, u32[]{:S(2)}, u32[]{:S(2)}) collective-permute-start(bf16[2,120,256]{2,1,0:T(8,128)(2,1)S(1)} %slice_bitcast_fusion), channel_id=1, source_target_pairs={{16,0},{17,1},{18,2},{19,3},{20,4},{21,5},{22,6},{23,7},{24,8},{25... | collective-permute-start | bytes 368648 | tf_op jit(solution)/shard_map/ppermute | solution.py:388
  33.1 0.9 %outer.5 = bf16[1,2,128,256]{3,2,1,0:T(8,128)(2,1)S(1)} custom-call(s32[1]{0:T(128)} %bitcast.refs_0_, s32[1]{0:T(128)} %bitcast.7.refs_1_, f32[2,2,128,256]{3,2,1,0:T(8,128)S(1)} %get-tuple-element.22.refs_2_, bf16[2,2,128,256]{3,2,1,0:T(8,128)(2,1)S(1)} %collective-permute-done.7.refs_3_, bf16[256,1024]{1,0:T(8,128)(2,1)S(1)} %copy-done, ...), custom_call_target="tpu_custom_call" | custom-call | flops 500000000 | bytes 3000000 | tf_op jit(solution)/shard_map/outer/pallas_call | solution.py:153
  34.0 0.5 %collective-permute-done.6 = bf16[2,120,256]{2,1,0:T(8,128)(2,1)S(1)} collective-permute-done((bf16[2,120,256]{2,1,0:T(8,128)(2,1)S(1)}, bf16[2,120,256]{2,1,0:T(8,128)(2,1)S(1)}, u32[]{:S(2)}, u32[]{:S(2)}) %collective-permute-start.6) | collective-permute-done | bytes 122912 | tf_op jit(solution)/shard_map/ppermute | solution.py:388
  34.6 0.1 collective-permute-start.10
  34.7 1.4 %collective-permute-done.5 = bf16[2,120,256]{2,1,0:T(8,128)(2,1)S(1)} collective-permute-done((bf16[2,120,256]{2,1,0:T(8,128)(2,1)S(1)}, bf16[2,120,256]{2,1,0:T(8,128)(2,1)S(1)}, u32[]{:S(2)}, u32[]{:S(2)}) %collective-permute-start.5) | collective-permute-done | bytes 122912 | tf_op jit(solution)/shard_map/ppermute | solution.py:388
  36.0 1.4 %collective-permute-done.8 = bf16[2,120,256]{2,1,0:T(8,128)(2,1)S(1)} collective-permute-done((bf16[2,120,256]{2,1,0:T(8,128)(2,1)S(1)}, bf16[2,120,256]{2,1,0:T(8,128)(2,1)S(1)}, u32[]{:S(2)}, u32[]{:S(2)}) %collective-permute-start.8) | collective-permute-done | bytes 122912 | tf_op jit(solution)/shard_map/ppermute | solution.py:388
  37.5 0.1 collective-permute-start.9
  37.6 1.3 %collective-permute-done.9 = bf16[2,120,256]{2,1,0:T(8,128)(2,1)S(1)} collective-permute-done((bf16[2,120,256]{2,1,0:T(8,128)(2,1)S(1)}, bf16[2,120,256]{2,1,0:T(8,128)(2,1)S(1)}, u32[]{:S(2)}, u32[]{:S(2)}) %collective-permute-start.9) | collective-permute-done | bytes 122912 | tf_op jit(solution)/shard_map/ppermute | solution.py:392
  39.1 0.8 %maximum_bitcast_fusion = bf16[2,1,1,480,256]{4,3,2,1,0:T(8,128)(2,1)} fusion(bf16[1,480,256]{2,1,0:T(8,128)(2,1)S(1)} %maximum_bitcast_fusion.2, bf16[1,480,256]{2,1,0:T(8,128)(2,1)S(1)} %maximum_bitcast_fusion.1), kind=kLoop, calls=%fused_computation | loop fusion | flops 245760 | bytes 983040 | tf_op jit(solution)/shard_map/reshape | solution.py:404
  (27 shorter events, 0.4 us)
Async XLA Ops:
  0.0 4.9 %collective-permute-start = (bf16[2,1,1,480,256]{4,3,2,1,0:T(8,128)(2,1)}, bf16[2,1,1,480,256]{4,3,2,1,0:T(8,128)(2,1)S(1)}, u32[]{:S(2)}, u32[]{:S(2)}) collective-permute-start(bf16[2,1,1,480,256]{4,3,2,1,0:T(8,128)(2,1)} %refs_0_.1), channel_id=1, source_target_pairs={{0,8},{8,0},{16,24},{24,16},{1,9},{9,1},{17,25},{25,17},{2,10},{10... | collective-permute-start | bytes 1474568 | tf_op jit(solution)/shard_map/ppermute | solution.py:306
  8.1 6.9 %collective-permute-start.1 = (bf16[2,128,256]{2,1,0:T(8,128)(2,1)S(1)}, bf16[2,128,256]{2,1,0:T(8,128)(2,1)S(1)}, u32[]{:S(2)}, u32[]{:S(2)}) collective-permute-start(bf16[2,128,256]{2,1,0:T(8,128)(2,1)S(1)} %pad_maximum_fusion.1), channel_id=1, source_target_pairs={{0,16},{1,17},{2,18},{3,19},{4,20},{5,21},{6,22},{7,23},{8,24},{9,... | collective-permute-start | bytes 393224 | tf_op jit(solution)/shard_map/ppermute | solution.py:339
  10.7 8.3 %collective-permute-start.2 = (bf16[2,128,256]{2,1,0:T(8,128)(2,1)S(1)}, bf16[2,128,256]{2,1,0:T(8,128)(2,1)S(1)}, u32[]{:S(2)}, u32[]{:S(2)}) collective-permute-start(bf16[2,128,256]{2,1,0:T(8,128)(2,1)S(1)} %pad_maximum_fusion.2), channel_id=1, source_target_pairs={{0,17},{1,16},{2,19},{3,18},{4,21},{5,20},{6,23},{7,22},{8,25},{9,... | collective-permute-start | bytes 393224 | tf_op jit(solution)/shard_map/ppermute | solution.py:339
  12.2 8.2 %collective-permute-start.3 = (bf16[2,128,256]{2,1,0:T(8,128)(2,1)S(1)}, bf16[2,128,256]{2,1,0:T(8,128)(2,1)S(1)}, u32[]{:S(2)}, u32[]{:S(2)}) collective-permute-start(bf16[2,128,256]{2,1,0:T(8,128)(2,1)S(1)} %pad_maximum_fusion.3), channel_id=1, source_target_pairs={{0,1},{1,0},{2,3},{3,2},{4,5},{5,4},{6,7},{7,6},{8,9},{9,8},{10,11... | collective-permute-start | bytes 393224 | tf_op jit(solution)/shard_map/ppermute | solution.py:339
  16.3 7.3 %copy-start = (bf16[256,1024]{1,0:T(8,128)(2,1)S(1)}, bf16[256,1024]{1,0:T(8,128)(2,1)}, u32[]{:S(2)}) copy-start(bf16[256,1024]{1,0:T(8,128)(2,1)} %refs_4_.9) | copy-start | bytes 1572868
  16.3 7.3 %copy-start.1 = (bf16[1024,256]{1,0:T(8,128)(2,1)S(1)}, bf16[1024,256]{1,0:T(8,128)(2,1)}, u32[]{:S(2)}) copy-start(bf16[1024,256]{1,0:T(8,128)(2,1)} %refs_6_.7) | copy-start | bytes 1572868
  16.3 7.3 %copy-start.2 = (bf16[3,3,1024]{2,1,0:T(4,128)(2,1)S(1)}, bf16[3,3,1024]{2,1,0:T(4,128)(2,1)}, u32[]{:S(2)}) copy-start(bf16[3,3,1024]{2,1,0:T(4,128)(2,1)} %refs_5_.9) | copy-start | bytes 55300
  16.3 10.6 %collective-permute-start.4 = (bf16[2,2,128,256]{3,2,1,0:T(8,128)(2,1)S(1)}, bf16[2,2,128,256]{3,2,1,0:T(8,128)(2,1)S(1)}, u32[]{:S(2)}, u32[]{:S(2)}) collective-permute-start(bf16[2,2,128,256]{3,2,1,0:T(8,128)(2,1)S(1)} %temporal.2.refs_5_.refs_1_), channel_id=1, source_target_pairs={{0,1},{1,3},{2,0},{3,5},{4,2},{5,7},{6,4},{7,6},{8,9},{9,11},{10,8... | collective-permute-start | bytes 786440 | tf_op jit(solution)/shard_map/ppermute | solution.py:355
  21.7 9.8 %collective-permute-start.7 = (bf16[2,2,128,256]{3,2,1,0:T(8,128)(2,1)S(1)}, bf16[2,2,128,256]{3,2,1,0:T(8,128)(2,1)S(1)}, u32[]{:S(2)}, u32[]{:S(2)}) collective-permute-start(bf16[2,2,128,256]{3,2,1,0:T(8,128)(2,1)S(1)} %temporal.3.refs_2_), channel_id=1, source_target_pairs={{0,2},{1,0},{2,4},{3,1},{4,6},{5,3},{6,7},{7,5},{8,10},{9,8},{10,1... | collective-permute-start | bytes 786440 | tf_op jit(solution)/shard_map/ppermute | solution.py:355
  28.5 6.1 %collective-permute-start.6 = (bf16[2,120,256]{2,1,0:T(8,128)(2,1)S(1)}, bf16[2,120,256]{2,1,0:T(8,128)(2,1)S(1)}, u32[]{:S(2)}, u32[]{:S(2)}) collective-permute-start(bf16[2,120,256]{2,1,0:T(8,128)(2,1)S(1)} %get-tuple-element.36), channel_id=1, source_target_pairs={{1,0},{0,1},{3,2},{2,3},{5,4},{4,5},{7,6},{6,7},{9,8},{8,9},{11,10... | collective-permute-start | bytes 368648 | tf_op jit(solution)/shard_map/ppermute | solution.py:388
  29.0 7.0 %collective-permute-start.5 = (bf16[2,120,256]{2,1,0:T(8,128)(2,1)S(1)}, bf16[2,120,256]{2,1,0:T(8,128)(2,1)S(1)}, u32[]{:S(2)}, u32[]{:S(2)}) collective-permute-start(bf16[2,120,256]{2,1,0:T(8,128)(2,1)S(1)} %get-tuple-element.35), channel_id=1, source_target_pairs={{17,0},{16,1},{19,2},{18,3},{21,4},{20,5},{23,6},{22,7},{25,8},{24... | collective-permute-start | bytes 368648 | tf_op jit(solution)/shard_map/ppermute | solution.py:388
  32.5 5.0 %collective-permute-start.8 = (bf16[2,120,256]{2,1,0:T(8,128)(2,1)S(1)}, bf16[2,120,256]{2,1,0:T(8,128)(2,1)S(1)}, u32[]{:S(2)}, u32[]{:S(2)}) collective-permute-start(bf16[2,120,256]{2,1,0:T(8,128)(2,1)S(1)} %slice_bitcast_fusion), channel_id=1, source_target_pairs={{16,0},{17,1},{18,2},{19,3},{20,4},{21,5},{22,6},{23,7},{24,8},{25... | collective-permute-start | bytes 368648 | tf_op jit(solution)/shard_map/ppermute | solution.py:388
  34.6 3.0 %collective-permute-start.10 = (bf16[2,120,256]{2,1,0:T(8,128)(2,1)S(1)}, bf16[2,120,256]{2,1,0:T(8,128)(2,1)S(1)}, u32[]{:S(2)}, u32[]{:S(2)}) collective-permute-start(bf16[2,120,256]{2,1,0:T(8,128)(2,1)S(1)} %pad_maximum_fusion.5), channel_id=1, source_target_pairs={{0,8},{8,0},{16,24},{24,16},{1,9},{9,1},{17,25},{25,17},{2,10},{10... | collective-permute-start | bytes 368648 | tf_op jit(solution)/shard_map/ppermute | solution.py:392
  37.5 1.4 %collective-permute-start.9 = (bf16[2,120,256]{2,1,0:T(8,128)(2,1)S(1)}, bf16[2,120,256]{2,1,0:T(8,128)(2,1)S(1)}, u32[]{:S(2)}, u32[]{:S(2)}) collective-permute-start(bf16[2,120,256]{2,1,0:T(8,128)(2,1)S(1)} %pad_maximum_fusion.4), channel_id=1, source_target_pairs={{0,8},{8,0},{16,24},{24,16},{1,9},{9,1},{17,25},{25,17},{2,10},{10... | collective-permute-start | bytes 368648 | tf_op jit(solution)/shard_map/ppermute | solution.py:392

commit v7 on v6

--- a/solution.py
+++ b/solution.py
@@ -342,12 +342,12 @@
     sections, halos = [], []
     for s in range(2):
         section = kernel_call(
-            functools.partial(temporal_kernel, pairs, -1 if s else 1),
+            functools.partial(temporal_kernel, pairs, 1),
             "temporal",
             1_000_000_000,
             jax.ShapeDtypeStruct(shape, jnp.bfloat16),
             (),
-            *[pieces[s, p] for p in range(pairs)][:: -1 if s else 1],
+            *[pieces[s, p] for p in range(pairs)],
             *weights[3:],
             after=sections[:],
         )

time: 40.1 us -> 38.9 us (0.970)
  waiting for transfers between devices: 9.34 us -> 8.14 us
    ppermute x3, waiting for transfers between devices: 4.76 us -> 3.49 us  [shards(): piece = lax.ppermute(piece, both, chip_moves(s, p))]
  transfers between devices with their start and end apart: 11 -> 11, of which waited for: 7 -> 6; matrix products, arithmetic and copies ran while one was open for 0% -> 0% of each run, Pallas kernels for 34% -> 35%
where the time goes in v7:
time: 38.9 us; the launch traced here: 38.7 us
  Pallas kernels  16.8 us (43%)
  starting transfers between devices  12.2 us (31%)
  waiting for transfers between devices  8.14 us (21%)
  other arithmetic  1.14 us (3%)
    pallas_call x7, Pallas kernels, kernel_call(): pl.pallas_call(ordered_body, in_specs=[pl.BlockSpec(memory_space=pltpu.SM...  12.4 us
    pallas_call x1, Pallas kernels, first_stereo(): pl.pallas_call(functools.partial(first_kernel, left, width // owners), in...  4.38 us
    ppermute x3, starting transfers between devices, shards(): piece = lax.ppermute(piece, both, chip_moves(s, p))  4.21 us
    ppermute x2, starting transfers between devices, shards(): halos.append(lax.ppermute(section, 'rows', band_moves[s]))  3.81 us
    ppermute x3, starting transfers between devices, shards(): piece = lax.ppermute(piece, both, back)  3.62 us
    ppermute x3, waiting for transfers between devices, shards(): piece = lax.ppermute(piece, both, chip_moves(s, p))  3.49 us
    ppermute x3, waiting for transfers between devices, shards(): piece = lax.ppermute(piece, both, back)  3.36 us
    ppermute x2, waiting for transfers between devices, shards(): received = lax.ppermute(sent, 'frame', siblings)  1.28 us
  transfers between devices with their start and end apart: 11, of which 6 were waited for; matrix products, arithmetic and copies ran while one was open for 0% of the time, Pallas kernels for 35%

profile of v7, /device:TPU:0, one launch (start us, length us, event | category | flops | bytes accessed | tf_op | source)
XLA Modules:
  0.0 38.7 jit_solution(12635401483749158600)
XLA Ops:
  0.0 0.5 %collective-permute-start = (bf16[2,1,1,480,256]{4,3,2,1,0:T(8,128)(2,1)}, bf16[2,1,1,480,256]{4,3,2,1,0:T(8,128)(2,1)S(1)}, u32[]{:S(2)}, u32[]{:S(2)}) collective-permute-start(bf16[2,1,1,480,256]{4,3,2,1,0:T(8,128)(2,1)} %refs_0_.1), channel_id=1, source_target_pairs={{0,8},{8,0},{16,24},{24,16},{1,9},{9,1},{17,25},{25,17},{2,10},{10... | collective-permute-start | bytes 1474568 | tf_op jit(solution)/shard_map/ppermute | solution.py:306
  0.5 4.4 %stereo.2 = (bf16[4,128,256]{2,1,0:T(8,128)(2,1)S(1)}, bf16[256,512]{1,0:T(8,128)(2,1)S(1)}, bf16[256,256]{1,0:T(8,128)(2,1)S(1)}, bf16[256,256]{1,0:T(8,128)(2,...) custom-call(s32[1]{0:T(128)} %bitcast.2.core_ref.refs_0_, ...), custom_call_target="tpu_custom_call" | custom-call | flops 2400000000 | bytes 2000000 | tf_op jit(solution)/shard_map/stereo/pallas_call | solution.py:93
  4.9 0.0 collective-permute-done.refs_1_
  4.9 3.1 %stereo.3 = bf16[4,128,256]{2,1,0:T(8,128)(2,1)S(1)} custom-call(s32[1]{0:T(128)} %bitcast.2.core_ref.refs_0_, bf16[2,1,1,480,256]{4,3,2,1,0:T(8,128)(2,1)S(1)} %collective-permute-done.refs_1_, bf16[256,512]{1,0:T(8,128)(2,1)S(1)} %get-tuple-element.15.refs_2_, bf16[256,256]{1,0:T(8,128)(2,1)S(1)} %get-tuple-element.16.refs_3_, ...), custom_call_target="tpu_custom_call" | custom-call | flops 2400000000 | bytes 3000000 | tf_op jit(solution)/shard_map/stereo/pallas_call | solution.py:153
  8.1 2.6 %collective-permute-start.1 = (bf16[2,128,256]{2,1,0:T(8,128)(2,1)S(1)}, bf16[2,128,256]{2,1,0:T(8,128)(2,1)S(1)}, u32[]{:S(2)}, u32[]{:S(2)}) collective-permute-start(bf16[2,128,256]{2,1,0:T(8,128)(2,1)S(1)} %pad_maximum_fusion.1), channel_id=1, source_target_pairs={{0,16},{1,17},{2,18},{3,19},{4,20},{5,21},{6,22},{7,23},{8,24},{9,... | collective-permute-start | bytes 393224 | tf_op jit(solution)/shard_map/ppermute | solution.py:339
  10.7 1.6 %collective-permute-start.2 = (bf16[2,128,256]{2,1,0:T(8,128)(2,1)S(1)}, bf16[2,128,256]{2,1,0:T(8,128)(2,1)S(1)}, u32[]{:S(2)}, u32[]{:S(2)}) collective-permute-start(bf16[2,128,256]{2,1,0:T(8,128)(2,1)S(1)} %pad_maximum_fusion.2), channel_id=1, source_target_pairs={{0,1},{1,0},{2,3},{3,2},{4,5},{5,4},{6,7},{7,6},{8,9},{9,8},{10,11... | collective-permute-start | bytes 393224 | tf_op jit(solution)/shard_map/ppermute | solution.py:339
  12.3 0.1 collective-permute-start.3
  12.4 2.4 %collective-permute-done.1.refs_1_ = bf16[2,128,256]{2,1,0:T(8,128)(2,1)S(1)} collective-permute-done((bf16[2,128,256]{2,1,0:T(8,128)(2,1)S(1)}, bf16[2,128,256]{2,1,0:T(8,128)(2,1)S(1)}, u32[]{:S(2)}, u32[]{:S(2)}) %collective-permute-start.1) | collective-permute-done | bytes 131104 | tf_op jit(solution)/shard_map/ppermute | solution.py:339
  14.8 1.3 %temporal.2.refs_5_.refs_1_ = bf16[2,2,128,256]{3,2,1,0:T(8,128)(2,1)S(1)} custom-call(bf16[2,128,256]{2,1,0:T(8,128)(2,1)S(1)} %pad_maximum_fusion.refs_0_, bf16[2,128,256]{2,1,0:T(8,128)(2,1)S(1)} %collective-permute-done.1.refs_1_, bf16[256,512]{1,0:T(8,128)(2,1)S(1)} %get-tuple-element.18.refs_2_, bf16[256,256]{1,0:T(8,128)(2,1)S(1)} %get-tuple-element.19.refs_3_, ...), custom_call_target="tpu_custom_call" | custom-call | flops 1000000000 | bytes 3000000 | tf_op jit(solution)/shard_map/temporal/pallas_call | solution.py:153
  16.1 0.0 copy-start
  16.1 0.0 copy-start.1
  16.1 0.0 copy-start.2
  16.1 2.0 %collective-permute-start.4 = (bf16[2,2,128,256]{3,2,1,0:T(8,128)(2,1)S(1)}, bf16[2,2,128,256]{3,2,1,0:T(8,128)(2,1)S(1)}, u32[]{:S(2)}, u32[]{:S(2)}) collective-permute-start(bf16[2,2,128,256]{3,2,1,0:T(8,128)(2,1)S(1)} %temporal.2.refs_5_.refs_1_), channel_id=1, source_target_pairs={{0,1},{1,3},{2,0},{3,5},{4,2},{5,7},{6,4},{7,6},{8,9},{9,11},{10,8... | collective-permute-start | bytes 786440 | tf_op jit(solution)/shard_map/ppermute | solution.py:355
  18.1 1.0 %collective-permute-done.2.refs_0_ = bf16[2,128,256]{2,1,0:T(8,128)(2,1)S(1)} collective-permute-done((bf16[2,128,256]{2,1,0:T(8,128)(2,1)S(1)}, bf16[2,128,256]{2,1,0:T(8,128)(2,1)S(1)}, u32[]{:S(2)}, u32[]{:S(2)}) %collective-permute-start.2) | collective-permute-done | bytes 131104 | tf_op jit(solution)/shard_map/ppermute | solution.py:339
  19.2 0.0 collective-permute-done.3.refs_1_
  19.2 1.3 %temporal.3.refs_2_ = bf16[2,2,128,256]{3,2,1,0:T(8,128)(2,1)S(1)} custom-call(bf16[2,128,256]{2,1,0:T(8,128)(2,1)S(1)} %collective-permute-done.2.refs_0_, bf16[2,128,256]{2,1,0:T(8,128)(2,1)S(1)} %collective-permute-done.3.refs_1_, bf16[256,512]{1,0:T(8,128)(2,1)S(1)} %get-tuple-element.18.refs_2_, bf16[256,256]{1,0:T(8,128)(2,1)S(1)} %get-tuple-element.19.refs_3_, ...), custom_call_target="tpu_custom_call" | custom-call | flops 1000000000 | bytes 3000000 | tf_op jit(solution)/shard_map/temporal/pallas_call | solution.py:153
  20.4 1.8 %collective-permute-start.7 = (bf16[2,2,128,256]{3,2,1,0:T(8,128)(2,1)S(1)}, bf16[2,2,128,256]{3,2,1,0:T(8,128)(2,1)S(1)}, u32[]{:S(2)}, u32[]{:S(2)}) collective-permute-start(bf16[2,2,128,256]{3,2,1,0:T(8,128)(2,1)S(1)} %temporal.3.refs_2_), channel_id=1, source_target_pairs={{0,2},{1,0},{2,4},{3,1},{4,6},{5,3},{6,7},{7,5},{8,10},{9,8},{10,1... | collective-permute-start | bytes 786440 | tf_op jit(solution)/shard_map/ppermute | solution.py:355
  22.3 3.3 %inner.1 = (f32[2,2,128,256]{3,2,1,0:T(8,128)S(1)}, f32[2,2,128,256]{3,2,1,0:T(8,128)S(1)}) custom-call(s32[1]{0:T(128)} %bitcast.refs_0_, bf16[2,2,128,256]{3,2,1,0:T(8,128)(2,1)S(1)} %temporal.2.refs_5_.refs_1_, bf16[2,2,128,256]{3,2,1,0:T(8,128)(2,1)S(1)} %temporal.3.refs_2_, bf16[256,1024]{1,0:T(8,128)(2,1)S(1)} %copy-done, ...), custom_call_target="tpu_custom_call" | custom-call | flops 4000000000 | bytes 3000000 | tf_op jit(solution)/shard_map/inner/pallas_call | solution.py:153
  25.6 1.6 %outer.3.refs_7_ = bf16[2,2,128,256]{3,2,1,0:T(8,128)(2,1)S(1)} custom-call(s32[1]{0:T(128)} %bitcast.refs_0_, s32[1]{0:T(128)} %bitcast.1.refs_1_, f32[2,2,128,256]{3,2,1,0:T(8,128)S(1)} %get-tuple-element.21.refs_2_, bf16[2,2,128,256]{3,2,1,0:T(8,128)(2,1)S(1)} %collective-permute-done.4.refs_3_, bf16[256,1024]{1,0:T(8,128)(2,1)S(1)} %copy-done, ...), custom_call_target="tpu_custom_call" | custom-call | flops 1000000000 | bytes 3000000 | tf_op jit(solution)/shard_map/outer/pallas_call | solution.py:153
  27.2 0.8 %collective-permute-start.6 = (bf16[2,120,256]{2,1,0:T(8,128)(2,1)S(1)}, bf16[2,120,256]{2,1,0:T(8,128)(2,1)S(1)}, u32[]{:S(2)}, u32[]{:S(2)}) collective-permute-start(bf16[2,120,256]{2,1,0:T(8,128)(2,1)S(1)} %get-tuple-element.36), channel_id=1, source_target_pairs={{1,0},{0,1},{3,2},{2,3},{5,4},{4,5},{7,6},{6,7},{9,8},{8,9},{11,10... | collective-permute-start | bytes 368648 | tf_op jit(solution)/shard_map/ppermute | solution.py:388
  28.0 1.9 %collective-permute-start.5 = (bf16[2,120,256]{2,1,0:T(8,128)(2,1)S(1)}, bf16[2,120,256]{2,1,0:T(8,128)(2,1)S(1)}, u32[]{:S(2)}, u32[]{:S(2)}) collective-permute-start(bf16[2,120,256]{2,1,0:T(8,128)(2,1)S(1)} %get-tuple-element.35), channel_id=1, source_target_pairs={{17,0},{16,1},{19,2},{18,3},{21,4},{20,5},{23,6},{22,7},{25,8},{24... | collective-permute-start | bytes 368648 | tf_op jit(solution)/shard_map/ppermute | solution.py:388
  29.9 0.9 %outer.4.refs_7_ = bf16[1,2,128,256]{3,2,1,0:T(8,128)(2,1)S(1)} custom-call(s32[1]{0:T(128)} %bitcast.refs_0_, s32[1]{0:T(128)} %bitcast.7.refs_1_, f32[2,2,128,256]{3,2,1,0:T(8,128)S(1)} %get-tuple-element.22.refs_2_, bf16[2,2,128,256]{3,2,1,0:T(8,128)(2,1)S(1)} %collective-permute-done.7.refs_3_, bf16[256,1024]{1,0:T(8,128)(2,1)S(1)} %copy-done, ...), custom_call_target="tpu_custom_call" | custom-call | flops 500000000 | bytes 3000000 | tf_op jit(solution)/shard_map/outer/pallas_call | solution.py:153
  30.8 0.9 %collective-permute-start.8 = (bf16[2,120,256]{2,1,0:T(8,128)(2,1)S(1)}, bf16[2,120,256]{2,1,0:T(8,128)(2,1)S(1)}, u32[]{:S(2)}, u32[]{:S(2)}) collective-permute-start(bf16[2,120,256]{2,1,0:T(8,128)(2,1)S(1)} %slice_bitcast_fusion), channel_id=1, source_target_pairs={{16,0},{17,1},{18,2},{19,3},{20,4},{21,5},{22,6},{23,7},{24,8},{25... | collective-permute-start | bytes 368648 | tf_op jit(solution)/shard_map/ppermute | solution.py:388
  31.8 0.9 %outer.5 = bf16[1,2,128,256]{3,2,1,0:T(8,128)(2,1)S(1)} custom-call(s32[1]{0:T(128)} %bitcast.refs_0_, s32[1]{0:T(128)} %bitcast.7.refs_1_, f32[2,2,128,256]{3,2,1,0:T(8,128)S(1)} %get-tuple-element.22.refs_2_, bf16[2,2,128,256]{3,2,1,0:T(8,128)(2,1)S(1)} %collective-permute-done.7.refs_3_, bf16[256,1024]{1,0:T(8,128)(2,1)S(1)} %copy-done, ...), custom_call_target="tpu_custom_call" | custom-call | flops 500000000 | bytes 3000000 | tf_op jit(solution)/shard_map/outer/pallas_call | solution.py:153
  32.8 0.6 %collective-permute-done.6 = bf16[2,120,256]{2,1,0:T(8,128)(2,1)S(1)} collective-permute-done((bf16[2,120,256]{2,1,0:T(8,128)(2,1)S(1)}, bf16[2,120,256]{2,1,0:T(8,128)(2,1)S(1)}, u32[]{:S(2)}, u32[]{:S(2)}) %collective-permute-start.6) | collective-permute-done | bytes 122912 | tf_op jit(solution)/shard_map/ppermute | solution.py:388
  33.3 0.1 collective-permute-start.10
  33.4 1.5 %collective-permute-done.5 = bf16[2,120,256]{2,1,0:T(8,128)(2,1)S(1)} collective-permute-done((bf16[2,120,256]{2,1,0:T(8,128)(2,1)S(1)}, bf16[2,120,256]{2,1,0:T(8,128)(2,1)S(1)}, u32[]{:S(2)}, u32[]{:S(2)}) %collective-permute-start.5) | collective-permute-done | bytes 122912 | tf_op jit(solution)/shard_map/ppermute | solution.py:388
  34.9 1.3 %collective-permute-done.8 = bf16[2,120,256]{2,1,0:T(8,128)(2,1)S(1)} collective-permute-done((bf16[2,120,256]{2,1,0:T(8,128)(2,1)S(1)}, bf16[2,120,256]{2,1,0:T(8,128)(2,1)S(1)}, u32[]{:S(2)}, u32[]{:S(2)}) %collective-permute-start.8) | collective-permute-done | bytes 122912 | tf_op jit(solution)/shard_map/ppermute | solution.py:388
  36.3 0.1 collective-permute-start.9
  36.4 0.0 collective-permute-done.10
  36.4 1.3 %collective-permute-done.9 = bf16[2,120,256]{2,1,0:T(8,128)(2,1)S(1)} collective-permute-done((bf16[2,120,256]{2,1,0:T(8,128)(2,1)S(1)}, bf16[2,120,256]{2,1,0:T(8,128)(2,1)S(1)}, u32[]{:S(2)}, u32[]{:S(2)}) %collective-permute-start.9) | collective-permute-done | bytes 122912 | tf_op jit(solution)/shard_map/ppermute | solution.py:392
  37.9 0.8 %maximum_bitcast_fusion = bf16[2,1,1,480,256]{4,3,2,1,0:T(8,128)(2,1)} fusion(bf16[1,480,256]{2,1,0:T(8,128)(2,1)S(1)} %maximum_bitcast_fusion.2, bf16[1,480,256]{2,1,0:T(8,128)(2,1)S(1)} %maximum_bitcast_fusion.1), kind=kLoop, calls=%fused_computation | loop fusion | flops 245760 | bytes 983040 | tf_op jit(solution)/shard_map/reshape | solution.py:404
  (27 shorter events, 0.4 us)
Async XLA Ops:
  0.0 4.9 %collective-permute-start = (bf16[2,1,1,480,256]{4,3,2,1,0:T(8,128)(2,1)}, bf16[2,1,1,480,256]{4,3,2,1,0:T(8,128)(2,1)S(1)}, u32[]{:S(2)}, u32[]{:S(2)}) collective-permute-start(bf16[2,1,1,480,256]{4,3,2,1,0:T(8,128)(2,1)} %refs_0_.1), channel_id=1, source_target_pairs={{0,8},{8,0},{16,24},{24,16},{1,9},{9,1},{17,25},{25,17},{2,10},{10... | collective-permute-start | bytes 1474568 | tf_op jit(solution)/shard_map/ppermute | solution.py:306
  8.1 6.7 %collective-permute-start.1 = (bf16[2,128,256]{2,1,0:T(8,128)(2,1)S(1)}, bf16[2,128,256]{2,1,0:T(8,128)(2,1)S(1)}, u32[]{:S(2)}, u32[]{:S(2)}) collective-permute-start(bf16[2,128,256]{2,1,0:T(8,128)(2,1)S(1)} %pad_maximum_fusion.1), channel_id=1, source_target_pairs={{0,16},{1,17},{2,18},{3,19},{4,20},{5,21},{6,22},{7,23},{8,24},{9,... | collective-permute-start | bytes 393224 | tf_op jit(solution)/shard_map/ppermute | solution.py:339
  10.7 8.5 %collective-permute-start.2 = (bf16[2,128,256]{2,1,0:T(8,128)(2,1)S(1)}, bf16[2,128,256]{2,1,0:T(8,128)(2,1)S(1)}, u32[]{:S(2)}, u32[]{:S(2)}) collective-permute-start(bf16[2,128,256]{2,1,0:T(8,128)(2,1)S(1)} %pad_maximum_fusion.2), channel_id=1, source_target_pairs={{0,1},{1,0},{2,3},{3,2},{4,5},{5,4},{6,7},{7,6},{8,9},{9,8},{10,11... | collective-permute-start | bytes 393224 | tf_op jit(solution)/shard_map/ppermute | solution.py:339
  12.3 6.9 %collective-permute-start.3 = (bf16[2,128,256]{2,1,0:T(8,128)(2,1)S(1)}, bf16[2,128,256]{2,1,0:T(8,128)(2,1)S(1)}, u32[]{:S(2)}, u32[]{:S(2)}) collective-permute-start(bf16[2,128,256]{2,1,0:T(8,128)(2,1)S(1)} %pad_maximum_fusion.3), channel_id=1, source_target_pairs={{0,17},{1,16},{2,19},{3,18},{4,21},{5,20},{6,23},{7,22},{8,25},{9,... | collective-permute-start | bytes 393224 | tf_op jit(solution)/shard_map/ppermute | solution.py:339
  16.1 6.2 %copy-start = (bf16[256,1024]{1,0:T(8,128)(2,1)S(1)}, bf16[256,1024]{1,0:T(8,128)(2,1)}, u32[]{:S(2)}) copy-start(bf16[256,1024]{1,0:T(8,128)(2,1)} %refs_4_.9) | copy-start | bytes 1572868
  16.1 6.2 %copy-start.1 = (bf16[1024,256]{1,0:T(8,128)(2,1)S(1)}, bf16[1024,256]{1,0:T(8,128)(2,1)}, u32[]{:S(2)}) copy-start(bf16[1024,256]{1,0:T(8,128)(2,1)} %refs_6_.7) | copy-start | bytes 1572868
  16.1 6.2 %copy-start.2 = (bf16[3,3,1024]{2,1,0:T(4,128)(2,1)S(1)}, bf16[3,3,1024]{2,1,0:T(4,128)(2,1)}, u32[]{:S(2)}) copy-start(bf16[3,3,1024]{2,1,0:T(4,128)(2,1)} %refs_5_.9) | copy-start | bytes 55300
  16.1 9.4 %collective-permute-start.4 = (bf16[2,2,128,256]{3,2,1,0:T(8,128)(2,1)S(1)}, bf16[2,2,128,256]{3,2,1,0:T(8,128)(2,1)S(1)}, u32[]{:S(2)}, u32[]{:S(2)}) collective-permute-start(bf16[2,2,128,256]{3,2,1,0:T(8,128)(2,1)S(1)} %temporal.2.refs_5_.refs_1_), channel_id=1, source_target_pairs={{0,1},{1,3},{2,0},{3,5},{4,2},{5,7},{6,4},{7,6},{8,9},{9,11},{10,8... | collective-permute-start | bytes 786440 | tf_op jit(solution)/shard_map/ppermute | solution.py:355
  20.4 9.4 %collective-permute-start.7 = (bf16[2,2,128,256]{3,2,1,0:T(8,128)(2,1)S(1)}, bf16[2,2,128,256]{3,2,1,0:T(8,128)(2,1)S(1)}, u32[]{:S(2)}, u32[]{:S(2)}) collective-permute-start(bf16[2,2,128,256]{3,2,1,0:T(8,128)(2,1)S(1)} %temporal.3.refs_2_), channel_id=1, source_target_pairs={{0,2},{1,0},{2,4},{3,1},{4,6},{5,3},{6,7},{7,5},{8,10},{9,8},{10,1... | collective-permute-start | bytes 786440 | tf_op jit(solution)/shard_map/ppermute | solution.py:355
  27.2 6.1 %collective-permute-start.6 = (bf16[2,120,256]{2,1,0:T(8,128)(2,1)S(1)}, bf16[2,120,256]{2,1,0:T(8,128)(2,1)S(1)}, u32[]{:S(2)}, u32[]{:S(2)}) collective-permute-start(bf16[2,120,256]{2,1,0:T(8,128)(2,1)S(1)} %get-tuple-element.36), channel_id=1, source_target_pairs={{1,0},{0,1},{3,2},{2,3},{5,4},{4,5},{7,6},{6,7},{9,8},{8,9},{11,10... | collective-permute-start | bytes 368648 | tf_op jit(solution)/shard_map/ppermute | solution.py:388
  28.0 6.9 %collective-permute-start.5 = (bf16[2,120,256]{2,1,0:T(8,128)(2,1)S(1)}, bf16[2,120,256]{2,1,0:T(8,128)(2,1)S(1)}, u32[]{:S(2)}, u32[]{:S(2)}) collective-permute-start(bf16[2,120,256]{2,1,0:T(8,128)(2,1)S(1)} %get-tuple-element.35), channel_id=1, source_target_pairs={{17,0},{16,1},{19,2},{18,3},{21,4},{20,5},{23,6},{22,7},{25,8},{24... | collective-permute-start | bytes 368648 | tf_op jit(solution)/shard_map/ppermute | solution.py:388
  30.8 5.4 %collective-permute-start.8 = (bf16[2,120,256]{2,1,0:T(8,128)(2,1)S(1)}, bf16[2,120,256]{2,1,0:T(8,128)(2,1)S(1)}, u32[]{:S(2)}, u32[]{:S(2)}) collective-permute-start(bf16[2,120,256]{2,1,0:T(8,128)(2,1)S(1)} %slice_bitcast_fusion), channel_id=1, source_target_pairs={{16,0},{17,1},{18,2},{19,3},{20,4},{21,5},{22,6},{23,7},{24,8},{25... | collective-permute-start | bytes 368648 | tf_op jit(solution)/shard_map/ppermute | solution.py:388
  33.3 3.0 %collective-permute-start.10 = (bf16[2,120,256]{2,1,0:T(8,128)(2,1)S(1)}, bf16[2,120,256]{2,1,0:T(8,128)(2,1)S(1)}, u32[]{:S(2)}, u32[]{:S(2)}) collective-permute-start(bf16[2,120,256]{2,1,0:T(8,128)(2,1)S(1)} %pad_maximum_fusion.5), channel_id=1, source_target_pairs={{0,8},{8,0},{16,24},{24,16},{1,9},{9,1},{17,25},{25,17},{2,10},{10... | collective-permute-start | bytes 368648 | tf_op jit(solution)/shard_map/ppermute | solution.py:392
  36.3 1.4 %collective-permute-start.9 = (bf16[2,120,256]{2,1,0:T(8,128)(2,1)S(1)}, bf16[2,120,256]{2,1,0:T(8,128)(2,1)S(1)}, u32[]{:S(2)}, u32[]{:S(2)}) collective-permute-start(bf16[2,120,256]{2,1,0:T(8,128)(2,1)S(1)} %pad_maximum_fusion.4), channel_id=1, source_target_pairs={{0,8},{8,0},{16,24},{24,16},{1,9},{9,1},{17,25},{25,17},{2,10},{10... | collective-permute-start | bytes 368648 | tf_op jit(solution)/shard_map/ppermute | solution.py:392

commit v8 on v7

--- a/solution.py
+++ b/solution.py
@@ -41,19 +41,27 @@
     ones = jnp.ones((width, 128), jnp.bfloat16)
     owners, window, _ = windows_ref.shape
     tail = round_up((owners - 1) * cols + window, 8) - width
-    groups = []
-    for start in range(0, channels, 128):
-        lanes = slice(start, start + 128)
-        total = jnp.zeros((width, 128), jnp.float32)
-        for head in range(128 // HEAD_DIM):
-            mask = lane_head == head
-            scores = dot_dims(queries[:, lanes], jnp.where(mask, keys[:, lanes], zero), 1, 1)
-            top = jnp.max(scores, axis=1, keepdims=True)
-            weights = jnp.exp2((scores - top) * SCALE_LOG2).astype(jnp.bfloat16)
-            values_head = jnp.where(mask, values[:, lanes], zero)
-            mixed = dot_dims(weights, jnp.concatenate([values_head, ones], axis=1), 1, 0)
-            total = total + mixed[:, :128] * (1.0 / mixed[:, 128:])
-        groups.append(total.astype(jnp.bfloat16))
+    per_group = 128 // HEAD_DIM
+
+    def head_scores(head):
+        lanes = slice(head // per_group * 128, head // per_group * 128 + 128)
+        mask = lane_head == head % per_group
+        return dot_dims(queries[:, lanes], jnp.where(mask, keys[:, lanes], zero), 1, 1)
+
+    totals = [jnp.zeros((width, 128), jnp.float32) for _ in range(channels // 128)]
+    ahead = [head_scores(head) for head in range(3)]
+    for head in range(HEADS):
+        if head + 3 < HEADS:
+            ahead.append(head_scores(head + 3))
+        scores = ahead.pop(0)
+        group = head // per_group
+        top = jnp.max(scores, axis=1, keepdims=True)
+        weights = jnp.exp2((scores - top) * SCALE_LOG2).astype(jnp.bfloat16)
+        mask = lane_head == head % per_group
+        values_head = jnp.where(mask, values[:, group * 128 : group * 128 + 128], zero)
+        mixed = dot_dims(weights, jnp.concatenate([values_head, ones], axis=1), 1, 0)
+        totals[group] = totals[group] + mixed[:, :128] * (1.0 / mixed[:, 128:])
+    groups = [total.astype(jnp.bfloat16) for total in totals]
     update = dot_dims(jnp.concatenate(groups, axis=1), out_ref[...], 1, 0)
     padded = jnp.concatenate([rows + update, jnp.zeros((tail, channels), jnp.float32)], axis=0)
     padded = pltpu.roll(padded, left, 0)

time: 38.9 us -> 38.7 us (level)
  no operation moved by 1% of the time
where the time goes in v8:
time: 38.7 us; the launch traced here: 38.5 us
  Pallas kernels  16.6 us (43%)
  starting transfers between devices  12.2 us (32%)
  waiting for transfers between devices  8.15 us (21%)
  other arithmetic  1.14 us (3%)
    pallas_call x7, Pallas kernels, kernel_call(): pl.pallas_call(ordered_body, in_specs=[pl.BlockSpec(memory_space=pltpu.SM...  12.3 us
    pallas_call x1, Pallas kernels, first_stereo(): pl.pallas_call(functools.partial(first_kernel, left, width // owners), in...  4.29 us
    ppermute x3, starting transfers between devices, shards(): piece = lax.ppermute(piece, both, chip_moves(s, p))  4.21 us
    ppermute x2, starting transfers between devices, shards(): halos.append(lax.ppermute(section, 'rows', band_moves[s]))  3.81 us
    ppermute x3, starting transfers between devices, shards(): piece = lax.ppermute(piece, both, back)  3.62 us
    ppermute x3, waiting for transfers between devices, shards(): piece = lax.ppermute(piece, both, chip_moves(s, p))  3.5 us
    ppermute x3, waiting for transfers between devices, shards(): piece = lax.ppermute(piece, both, back)  3.36 us
    ppermute x2, waiting for transfers between devices, shards(): received = lax.ppermute(sent, 'frame', siblings)  1.28 us
  transfers between devices with their start and end apart: 11, of which 6 were waited for; matrix products, arithmetic and copies ran while one was open for 0% of the time, Pallas kernels for 35%

profile of v8, /device:TPU:0, one launch (start us, length us, event | category | flops | bytes accessed | tf_op | source)
XLA Modules:
  0.0 38.5 jit_solution(9548360193407582578)
XLA Ops:
  0.0 0.5 %collective-permute-start = (bf16[2,1,1,480,256]{4,3,2,1,0:T(8,128)(2,1)}, bf16[2,1,1,480,256]{4,3,2,1,0:T(8,128)(2,1)S(1)}, u32[]{:S(2)}, u32[]{:S(2)}) collective-permute-start(bf16[2,1,1,480,256]{4,3,2,1,0:T(8,128)(2,1)} %refs_0_.1), channel_id=1, source_target_pairs={{0,8},{8,0},{16,24},{24,16},{1,9},{9,1},{17,25},{25,17},{2,10},{10... | collective-permute-start | bytes 1474568 | tf_op jit(solution)/shard_map/ppermute | solution.py:314
  0.5 4.3 %stereo.2 = (bf16[4,128,256]{2,1,0:T(8,128)(2,1)S(1)}, bf16[256,512]{1,0:T(8,128)(2,1)S(1)}, bf16[256,256]{1,0:T(8,128)(2,1)S(1)}, bf16[256,256]{1,0:T(8,128)(2,...) custom-call(s32[1]{0:T(128)} %bitcast.2.core_ref.refs_0_, ...), custom_call_target="tpu_custom_call" | custom-call | flops 2400000000 | bytes 2000000 | tf_op jit(solution)/shard_map/stereo/pallas_call | solution.py:101
  4.8 0.0 collective-permute-done.refs_1_
  4.8 3.0 %stereo.3 = bf16[4,128,256]{2,1,0:T(8,128)(2,1)S(1)} custom-call(s32[1]{0:T(128)} %bitcast.2.core_ref.refs_0_, bf16[2,1,1,480,256]{4,3,2,1,0:T(8,128)(2,1)S(1)} %collective-permute-done.refs_1_, bf16[256,512]{1,0:T(8,128)(2,1)S(1)} %get-tuple-element.15.refs_2_, bf16[256,256]{1,0:T(8,128)(2,1)S(1)} %get-tuple-element.16.refs_3_, ...), custom_call_target="tpu_custom_call" | custom-call | flops 2400000000 | bytes 3000000 | tf_op jit(solution)/shard_map/stereo/pallas_call | solution.py:161
  7.9 2.6 %collective-permute-start.1 = (bf16[2,128,256]{2,1,0:T(8,128)(2,1)S(1)}, bf16[2,128,256]{2,1,0:T(8,128)(2,1)S(1)}, u32[]{:S(2)}, u32[]{:S(2)}) collective-permute-start(bf16[2,128,256]{2,1,0:T(8,128)(2,1)S(1)} %pad_maximum_fusion.1), channel_id=1, source_target_pairs={{0,16},{1,17},{2,18},{3,19},{4,20},{5,21},{6,22},{7,23},{8,24},{9,... | collective-permute-start | bytes 393224 | tf_op jit(solution)/shard_map/ppermute | solution.py:347
  10.5 1.6 %collective-permute-start.2 = (bf16[2,128,256]{2,1,0:T(8,128)(2,1)S(1)}, bf16[2,128,256]{2,1,0:T(8,128)(2,1)S(1)}, u32[]{:S(2)}, u32[]{:S(2)}) collective-permute-start(bf16[2,128,256]{2,1,0:T(8,128)(2,1)S(1)} %pad_maximum_fusion.2), channel_id=1, source_target_pairs={{0,1},{1,0},{2,3},{3,2},{4,5},{5,4},{6,7},{7,6},{8,9},{9,8},{10,11... | collective-permute-start | bytes 393224 | tf_op jit(solution)/shard_map/ppermute | solution.py:347
  12.1 0.1 collective-permute-start.3
  12.2 2.4 %collective-permute-done.1.refs_1_ = bf16[2,128,256]{2,1,0:T(8,128)(2,1)S(1)} collective-permute-done((bf16[2,128,256]{2,1,0:T(8,128)(2,1)S(1)}, bf16[2,128,256]{2,1,0:T(8,128)(2,1)S(1)}, u32[]{:S(2)}, u32[]{:S(2)}) %collective-permute-start.1) | collective-permute-done | bytes 131104 | tf_op jit(solution)/shard_map/ppermute | solution.py:347
  14.6 1.3 %temporal.2.refs_5_.refs_1_ = bf16[2,2,128,256]{3,2,1,0:T(8,128)(2,1)S(1)} custom-call(bf16[2,128,256]{2,1,0:T(8,128)(2,1)S(1)} %pad_maximum_fusion.refs_0_, bf16[2,128,256]{2,1,0:T(8,128)(2,1)S(1)} %collective-permute-done.1.refs_1_, bf16[256,512]{1,0:T(8,128)(2,1)S(1)} %get-tuple-element.18.refs_2_, bf16[256,256]{1,0:T(8,128)(2,1)S(1)} %get-tuple-element.19.refs_3_, ...), custom_call_target="tpu_custom_call" | custom-call | flops 1000000000 | bytes 3000000 | tf_op jit(solution)/shard_map/temporal/pallas_call | solution.py:161
  15.9 0.0 copy-start
  15.9 0.0 copy-start.1
  15.9 0.0 copy-start.2
  15.9 2.0 %collective-permute-start.4 = (bf16[2,2,128,256]{3,2,1,0:T(8,128)(2,1)S(1)}, bf16[2,2,128,256]{3,2,1,0:T(8,128)(2,1)S(1)}, u32[]{:S(2)}, u32[]{:S(2)}) collective-permute-start(bf16[2,2,128,256]{3,2,1,0:T(8,128)(2,1)S(1)} %temporal.2.refs_5_.refs_1_), channel_id=1, source_target_pairs={{0,1},{1,3},{2,0},{3,5},{4,2},{5,7},{6,4},{7,6},{8,9},{9,11},{10,8... | collective-permute-start | bytes 786440 | tf_op jit(solution)/shard_map/ppermute | solution.py:363
  17.9 1.0 %collective-permute-done.2.refs_0_ = bf16[2,128,256]{2,1,0:T(8,128)(2,1)S(1)} collective-permute-done((bf16[2,128,256]{2,1,0:T(8,128)(2,1)S(1)}, bf16[2,128,256]{2,1,0:T(8,128)(2,1)S(1)}, u32[]{:S(2)}, u32[]{:S(2)}) %collective-permute-start.2) | collective-permute-done | bytes 131104 | tf_op jit(solution)/shard_map/ppermute | solution.py:347
  19.0 0.0 collective-permute-done.3.refs_1_
  19.0 1.3 %temporal.3.refs_2_ = bf16[2,2,128,256]{3,2,1,0:T(8,128)(2,1)S(1)} custom-call(bf16[2,128,256]{2,1,0:T(8,128)(2,1)S(1)} %collective-permute-done.2.refs_0_, bf16[2,128,256]{2,1,0:T(8,128)(2,1)S(1)} %collective-permute-done.3.refs_1_, bf16[256,512]{1,0:T(8,128)(2,1)S(1)} %get-tuple-element.18.refs_2_, bf16[256,256]{1,0:T(8,128)(2,1)S(1)} %get-tuple-element.19.refs_3_, ...), custom_call_target="tpu_custom_call" | custom-call | flops 1000000000 | bytes 3000000 | tf_op jit(solution)/shard_map/temporal/pallas_call | solution.py:161
  20.2 1.8 %collective-permute-start.7 = (bf16[2,2,128,256]{3,2,1,0:T(8,128)(2,1)S(1)}, bf16[2,2,128,256]{3,2,1,0:T(8,128)(2,1)S(1)}, u32[]{:S(2)}, u32[]{:S(2)}) collective-permute-start(bf16[2,2,128,256]{3,2,1,0:T(8,128)(2,1)S(1)} %temporal.3.refs_2_), channel_id=1, source_target_pairs={{0,2},{1,0},{2,4},{3,1},{4,6},{5,3},{6,7},{7,5},{8,10},{9,8},{10,1... | collective-permute-start | bytes 786440 | tf_op jit(solution)/shard_map/ppermute | solution.py:363
  22.1 3.3 %inner.1 = (f32[2,2,128,256]{3,2,1,0:T(8,128)S(1)}, f32[2,2,128,256]{3,2,1,0:T(8,128)S(1)}) custom-call(s32[1]{0:T(128)} %bitcast.refs_0_, bf16[2,2,128,256]{3,2,1,0:T(8,128)(2,1)S(1)} %temporal.2.refs_5_.refs_1_, bf16[2,2,128,256]{3,2,1,0:T(8,128)(2,1)S(1)} %temporal.3.refs_2_, bf16[256,1024]{1,0:T(8,128)(2,1)S(1)} %copy-done, ...), custom_call_target="tpu_custom_call" | custom-call | flops 4000000000 | bytes 3000000 | tf_op jit(solution)/shard_map/inner/pallas_call | solution.py:161
  25.4 0.0 collective-permute-done.4.refs_3_
  25.4 1.6 %outer.3.refs_7_ = bf16[2,2,128,256]{3,2,1,0:T(8,128)(2,1)S(1)} custom-call(s32[1]{0:T(128)} %bitcast.refs_0_, s32[1]{0:T(128)} %bitcast.1.refs_1_, f32[2,2,128,256]{3,2,1,0:T(8,128)S(1)} %get-tuple-element.21.refs_2_, bf16[2,2,128,256]{3,2,1,0:T(8,128)(2,1)S(1)} %collective-permute-done.4.refs_3_, bf16[256,1024]{1,0:T(8,128)(2,1)S(1)} %copy-done, ...), custom_call_target="tpu_custom_call" | custom-call | flops 1000000000 | bytes 3000000 | tf_op jit(solution)/shard_map/outer/pallas_call | solution.py:161
  27.0 0.8 %collective-permute-start.6 = (bf16[2,120,256]{2,1,0:T(8,128)(2,1)S(1)}, bf16[2,120,256]{2,1,0:T(8,128)(2,1)S(1)}, u32[]{:S(2)}, u32[]{:S(2)}) collective-permute-start(bf16[2,120,256]{2,1,0:T(8,128)(2,1)S(1)} %get-tuple-element.36), channel_id=1, source_target_pairs={{1,0},{0,1},{3,2},{2,3},{5,4},{4,5},{7,6},{6,7},{9,8},{8,9},{11,10... | collective-permute-start | bytes 368648 | tf_op jit(solution)/shard_map/ppermute | solution.py:396
  27.8 1.9 %collective-permute-start.5 = (bf16[2,120,256]{2,1,0:T(8,128)(2,1)S(1)}, bf16[2,120,256]{2,1,0:T(8,128)(2,1)S(1)}, u32[]{:S(2)}, u32[]{:S(2)}) collective-permute-start(bf16[2,120,256]{2,1,0:T(8,128)(2,1)S(1)} %get-tuple-element.35), channel_id=1, source_target_pairs={{17,0},{16,1},{19,2},{18,3},{21,4},{20,5},{23,6},{22,7},{25,8},{24... | collective-permute-start | bytes 368648 | tf_op jit(solution)/shard_map/ppermute | solution.py:396
  29.7 0.9 %outer.4.refs_7_ = bf16[1,2,128,256]{3,2,1,0:T(8,128)(2,1)S(1)} custom-call(s32[1]{0:T(128)} %bitcast.refs_0_, s32[1]{0:T(128)} %bitcast.7.refs_1_, f32[2,2,128,256]{3,2,1,0:T(8,128)S(1)} %get-tuple-element.22.refs_2_, bf16[2,2,128,256]{3,2,1,0:T(8,128)(2,1)S(1)} %collective-permute-done.7.refs_3_, bf16[256,1024]{1,0:T(8,128)(2,1)S(1)} %copy-done, ...), custom_call_target="tpu_custom_call" | custom-call | flops 500000000 | bytes 3000000 | tf_op jit(solution)/shard_map/outer/pallas_call | solution.py:161
  30.6 0.9 %collective-permute-start.8 = (bf16[2,120,256]{2,1,0:T(8,128)(2,1)S(1)}, bf16[2,120,256]{2,1,0:T(8,128)(2,1)S(1)}, u32[]{:S(2)}, u32[]{:S(2)}) collective-permute-start(bf16[2,120,256]{2,1,0:T(8,128)(2,1)S(1)} %slice_bitcast_fusion), channel_id=1, source_target_pairs={{16,0},{17,1},{18,2},{19,3},{20,4},{21,5},{22,6},{23,7},{24,8},{25... | collective-permute-start | bytes 368648 | tf_op jit(solution)/shard_map/ppermute | solution.py:396
  31.6 0.9 %outer.5 = bf16[1,2,128,256]{3,2,1,0:T(8,128)(2,1)S(1)} custom-call(s32[1]{0:T(128)} %bitcast.refs_0_, s32[1]{0:T(128)} %bitcast.7.refs_1_, f32[2,2,128,256]{3,2,1,0:T(8,128)S(1)} %get-tuple-element.22.refs_2_, bf16[2,2,128,256]{3,2,1,0:T(8,128)(2,1)S(1)} %collective-permute-done.7.refs_3_, bf16[256,1024]{1,0:T(8,128)(2,1)S(1)} %copy-done, ...), custom_call_target="tpu_custom_call" | custom-call | flops 500000000 | bytes 3000000 | tf_op jit(solution)/shard_map/outer/pallas_call | solution.py:161
  32.6 0.6 %collective-permute-done.6 = bf16[2,120,256]{2,1,0:T(8,128)(2,1)S(1)} collective-permute-done((bf16[2,120,256]{2,1,0:T(8,128)(2,1)S(1)}, bf16[2,120,256]{2,1,0:T(8,128)(2,1)S(1)}, u32[]{:S(2)}, u32[]{:S(2)}) %collective-permute-start.6) | collective-permute-done | bytes 122912 | tf_op jit(solution)/shard_map/ppermute | solution.py:396
  33.2 0.1 collective-permute-start.10
  33.2 1.5 %collective-permute-done.5 = bf16[2,120,256]{2,1,0:T(8,128)(2,1)S(1)} collective-permute-done((bf16[2,120,256]{2,1,0:T(8,128)(2,1)S(1)}, bf16[2,120,256]{2,1,0:T(8,128)(2,1)S(1)}, u32[]{:S(2)}, u32[]{:S(2)}) %collective-permute-start.5) | collective-permute-done | bytes 122912 | tf_op jit(solution)/shard_map/ppermute | solution.py:396
  34.7 1.3 %collective-permute-done.8 = bf16[2,120,256]{2,1,0:T(8,128)(2,1)S(1)} collective-permute-done((bf16[2,120,256]{2,1,0:T(8,128)(2,1)S(1)}, bf16[2,120,256]{2,1,0:T(8,128)(2,1)S(1)}, u32[]{:S(2)}, u32[]{:S(2)}) %collective-permute-start.8) | collective-permute-done | bytes 122912 | tf_op jit(solution)/shard_map/ppermute | solution.py:396
  36.1 0.1 collective-permute-start.9
  36.2 1.3 %collective-permute-done.9 = bf16[2,120,256]{2,1,0:T(8,128)(2,1)S(1)} collective-permute-done((bf16[2,120,256]{2,1,0:T(8,128)(2,1)S(1)}, bf16[2,120,256]{2,1,0:T(8,128)(2,1)S(1)}, u32[]{:S(2)}, u32[]{:S(2)}) %collective-permute-start.9) | collective-permute-done | bytes 122912 | tf_op jit(solution)/shard_map/ppermute | solution.py:400
  37.7 0.8 %maximum_bitcast_fusion = bf16[2,1,1,480,256]{4,3,2,1,0:T(8,128)(2,1)} fusion(bf16[1,480,256]{2,1,0:T(8,128)(2,1)S(1)} %maximum_bitcast_fusion.2, bf16[1,480,256]{2,1,0:T(8,128)(2,1)S(1)} %maximum_bitcast_fusion.1), kind=kLoop, calls=%fused_computation | loop fusion | flops 245760 | bytes 983040 | tf_op jit(solution)/shard_map/reshape | solution.py:412
  (27 shorter events, 0.4 us)
Async XLA Ops:
  0.0 4.8 %collective-permute-start = (bf16[2,1,1,480,256]{4,3,2,1,0:T(8,128)(2,1)}, bf16[2,1,1,480,256]{4,3,2,1,0:T(8,128)(2,1)S(1)}, u32[]{:S(2)}, u32[]{:S(2)}) collective-permute-start(bf16[2,1,1,480,256]{4,3,2,1,0:T(8,128)(2,1)} %refs_0_.1), channel_id=1, source_target_pairs={{0,8},{8,0},{16,24},{24,16},{1,9},{9,1},{17,25},{25,17},{2,10},{10... | collective-permute-start | bytes 1474568 | tf_op jit(solution)/shard_map/ppermute | solution.py:314
  7.9 6.7 %collective-permute-start.1 = (bf16[2,128,256]{2,1,0:T(8,128)(2,1)S(1)}, bf16[2,128,256]{2,1,0:T(8,128)(2,1)S(1)}, u32[]{:S(2)}, u32[]{:S(2)}) collective-permute-start(bf16[2,128,256]{2,1,0:T(8,128)(2,1)S(1)} %pad_maximum_fusion.1), channel_id=1, source_target_pairs={{0,16},{1,17},{2,18},{3,19},{4,20},{5,21},{6,22},{7,23},{8,24},{9,... | collective-permute-start | bytes 393224 | tf_op jit(solution)/shard_map/ppermute | solution.py:347
  10.5 8.5 %collective-permute-start.2 = (bf16[2,128,256]{2,1,0:T(8,128)(2,1)S(1)}, bf16[2,128,256]{2,1,0:T(8,128)(2,1)S(1)}, u32[]{:S(2)}, u32[]{:S(2)}) collective-permute-start(bf16[2,128,256]{2,1,0:T(8,128)(2,1)S(1)} %pad_maximum_fusion.2), channel_id=1, source_target_pairs={{0,1},{1,0},{2,3},{3,2},{4,5},{5,4},{6,7},{7,6},{8,9},{9,8},{10,11... | collective-permute-start | bytes 393224 | tf_op jit(solution)/shard_map/ppermute | solution.py:347
  12.1 6.9 %collective-permute-start.3 = (bf16[2,128,256]{2,1,0:T(8,128)(2,1)S(1)}, bf16[2,128,256]{2,1,0:T(8,128)(2,1)S(1)}, u32[]{:S(2)}, u32[]{:S(2)}) collective-permute-start(bf16[2,128,256]{2,1,0:T(8,128)(2,1)S(1)} %pad_maximum_fusion.3), channel_id=1, source_target_pairs={{0,17},{1,16},{2,19},{3,18},{4,21},{5,20},{6,23},{7,22},{8,25},{9,... | collective-permute-start | bytes 393224 | tf_op jit(solution)/shard_map/ppermute | solution.py:347
  15.9 6.2 %copy-start = (bf16[256,1024]{1,0:T(8,128)(2,1)S(1)}, bf16[256,1024]{1,0:T(8,128)(2,1)}, u32[]{:S(2)}) copy-start(bf16[256,1024]{1,0:T(8,128)(2,1)} %refs_4_.9) | copy-start | bytes 1572868
  15.9 6.2 %copy-start.1 = (bf16[1024,256]{1,0:T(8,128)(2,1)S(1)}, bf16[1024,256]{1,0:T(8,128)(2,1)}, u32[]{:S(2)}) copy-start(bf16[1024,256]{1,0:T(8,128)(2,1)} %refs_6_.7) | copy-start | bytes 1572868
  15.9 6.1 %copy-start.2 = (bf16[3,3,1024]{2,1,0:T(4,128)(2,1)S(1)}, bf16[3,3,1024]{2,1,0:T(4,128)(2,1)}, u32[]{:S(2)}) copy-start(bf16[3,3,1024]{2,1,0:T(4,128)(2,1)} %refs_5_.9) | copy-start | bytes 55300
  15.9 9.4 %collective-permute-start.4 = (bf16[2,2,128,256]{3,2,1,0:T(8,128)(2,1)S(1)}, bf16[2,2,128,256]{3,2,1,0:T(8,128)(2,1)S(1)}, u32[]{:S(2)}, u32[]{:S(2)}) collective-permute-start(bf16[2,2,128,256]{3,2,1,0:T(8,128)(2,1)S(1)} %temporal.2.refs_5_.refs_1_), channel_id=1, source_target_pairs={{0,1},{1,3},{2,0},{3,5},{4,2},{5,7},{6,4},{7,6},{8,9},{9,11},{10,8... | collective-permute-start | bytes 786440 | tf_op jit(solution)/shard_map/ppermute | solution.py:363
  20.2 9.4 %collective-permute-start.7 = (bf16[2,2,128,256]{3,2,1,0:T(8,128)(2,1)S(1)}, bf16[2,2,128,256]{3,2,1,0:T(8,128)(2,1)S(1)}, u32[]{:S(2)}, u32[]{:S(2)}) collective-permute-start(bf16[2,2,128,256]{3,2,1,0:T(8,128)(2,1)S(1)} %temporal.3.refs_2_), channel_id=1, source_target_pairs={{0,2},{1,0},{2,4},{3,1},{4,6},{5,3},{6,7},{7,5},{8,10},{9,8},{10,1... | collective-permute-start | bytes 786440 | tf_op jit(solution)/shard_map/ppermute | solution.py:363
  27.0 6.1 %collective-permute-start.6 = (bf16[2,120,256]{2,1,0:T(8,128)(2,1)S(1)}, bf16[2,120,256]{2,1,0:T(8,128)(2,1)S(1)}, u32[]{:S(2)}, u32[]{:S(2)}) collective-permute-start(bf16[2,120,256]{2,1,0:T(8,128)(2,1)S(1)} %get-tuple-element.36), channel_id=1, source_target_pairs={{1,0},{0,1},{3,2},{2,3},{5,4},{4,5},{7,6},{6,7},{9,8},{8,9},{11,10... | collective-permute-start | bytes 368648 | tf_op jit(solution)/shard_map/ppermute | solution.py:396
  27.8 6.9 %collective-permute-start.5 = (bf16[2,120,256]{2,1,0:T(8,128)(2,1)S(1)}, bf16[2,120,256]{2,1,0:T(8,128)(2,1)S(1)}, u32[]{:S(2)}, u32[]{:S(2)}) collective-permute-start(bf16[2,120,256]{2,1,0:T(8,128)(2,1)S(1)} %get-tuple-element.35), channel_id=1, source_target_pairs={{17,0},{16,1},{19,2},{18,3},{21,4},{20,5},{23,6},{22,7},{25,8},{24... | collective-permute-start | bytes 368648 | tf_op jit(solution)/shard_map/ppermute | solution.py:396
  30.6 5.4 %collective-permute-start.8 = (bf16[2,120,256]{2,1,0:T(8,128)(2,1)S(1)}, bf16[2,120,256]{2,1,0:T(8,128)(2,1)S(1)}, u32[]{:S(2)}, u32[]{:S(2)}) collective-permute-start(bf16[2,120,256]{2,1,0:T(8,128)(2,1)S(1)} %slice_bitcast_fusion), channel_id=1, source_target_pairs={{16,0},{17,1},{18,2},{19,3},{20,4},{21,5},{22,6},{23,7},{24,8},{25... | collective-permute-start | bytes 368648 | tf_op jit(solution)/shard_map/ppermute | solution.py:396
  33.2 3.0 %collective-permute-start.10 = (bf16[2,120,256]{2,1,0:T(8,128)(2,1)S(1)}, bf16[2,120,256]{2,1,0:T(8,128)(2,1)S(1)}, u32[]{:S(2)}, u32[]{:S(2)}) collective-permute-start(bf16[2,120,256]{2,1,0:T(8,128)(2,1)S(1)} %pad_maximum_fusion.5), channel_id=1, source_target_pairs={{0,8},{8,0},{16,24},{24,16},{1,9},{9,1},{17,25},{25,17},{2,10},{10... | collective-permute-start | bytes 368648 | tf_op jit(solution)/shard_map/ppermute | solution.py:400
  36.1 1.4 %collective-permute-start.9 = (bf16[2,120,256]{2,1,0:T(8,128)(2,1)S(1)}, bf16[2,120,256]{2,1,0:T(8,128)(2,1)S(1)}, u32[]{:S(2)}, u32[]{:S(2)}) collective-permute-start(bf16[2,120,256]{2,1,0:T(8,128)(2,1)S(1)} %pad_maximum_fusion.4), channel_id=1, source_target_pairs={{0,8},{8,0},{16,24},{24,16},{1,9},{9,1},{17,25},{25,17},{2,10},{10... | collective-permute-start | bytes 368648 | tf_op jit(solution)/shard_map/ppermute | solution.py:400
